TPU v7x, 512 devices: a whole 4x8x8 slice. The times are simulated.
512 devices in a mesh: tm: 128 (over y_hi, x, z), space: 4 (over y_lo, core).
Axes of the slice: x: 4, y: 8 (y_hi: 4, y_lo: 2; y = y_hi * 2 + y_lo), z: 8, core: 2. Of those that a mesh axis runs over, the one named last changes fastest.
Arguments:
- inputs: bfloat16 [128, 1, 144, 1280], P('tm', None, 'space'), may hold values from -120 to 120
- cotangent: bfloat16 [128, 1, 144, 1280], P('tm', None, 'space'), may hold values from -6 to 6
- norm_gain: bfloat16 [1280], replicated, may hold values from 0.5 to 1.5
- query_weight: bfloat16 [1280, 1280], P(None, 'space'), may hold values from -1.5 to 1.5
- key_weight: bfloat16 [1280, 1280], P(None, 'space'), may hold values from -1.5 to 1.5
- value_weight: bfloat16 [1280, 1280], P(None, 'space'), may hold values from -0.15625 to 0.15625
- output_weight: bfloat16 [1280, 1280], P('space'), may hold values from -0.15625 to 0.15625
Outputs:
- block_output: bfloat16 [128, 1, 144, 1280], P('tm', None, 'space')
- input_grads: bfloat16 [128, 1, 144, 1280], P('tm', None, 'space')
All inputs are finite; a program needn't handle non-finite values.
Results may differ from a plain program's by a relative error of at most 0.018.
The roundings to bfloat16 on the way count: a program that leaves them out, or rounds other values in their place, can miss the bound.
Values may be sent and summed in bfloat16 or wider, within the bound.
No kernel may reach another device: no remote copies, remote signals or barrier semaphores. Data moves between devices by JAX's collectives and lax.ppermute only.
A program may use at most 64 MiB of HBM per device.

v0:
```python
import jax
import jax.numpy as jnp
from jax import lax
from jax.sharding import PartitionSpec as P

HEAD_DIM = 64


EPSILON = 1e-05
NEG_FILL = -1e30
OFFSETS = (-2, -1, 1, 2)
ORDERED = (-2, -1, 0, 1, 2)


def passed_along(block, axis, distance):
    devices = range(lax.axis_size(axis))
    route = [(i - distance, i) for i in devices if i - distance in devices]
    return lax.ppermute(block, axis, route)


def frame_stats(inputs):
    values = inputs.astype(jnp.float32)
    center = jnp.mean(values, axis=-1, keepdims=True)
    spread = jnp.mean(jnp.square(values - center), axis=-1, keepdims=True)
    inverse = lax.rsqrt(spread + EPSILON)
    return (values, (values - center) * inverse, inverse)


def split_heads(matrix):
    return matrix.reshape(matrix.shape[:-1] + (matrix.shape[-1] // HEAD_DIM, HEAD_DIM))


def merge_heads(tensor):
    return tensor.reshape(tensor.shape[:-2] + (tensor.shape[-2] * tensor.shape[-1],))


def weigh_rows(weights, tensor):
    return jnp.einsum("fbph,fbphe->fbphe", weights, tensor, preferred_element_type=jnp.float32)


def back_heads(grads, weight):
    return jnp.einsum(
        "fbpc,dc->fbpd", merge_heads(grads), weight, preferred_element_type=jnp.float32
    )


def per_device(inputs, cotangent, norm_gain, query_weight, key_weight, value_weight, output_weight):
    score_scale = HEAD_DIM ** (-0.5)
    frame_index = lax.axis_index("tm")
    frame_count = lax.axis_size("tm")
    local_width = query_weight.shape[1]
    values, normed, inverse = frame_stats(inputs)
    gain_values = norm_gain.astype(jnp.float32)
    hidden = (normed * gain_values).astype(jnp.bfloat16)
    rows_piece = lax.all_gather(hidden, "space", axis=2, tiled=True)
    projections = [
        jnp.dot(rows_piece, weight, preferred_element_type=jnp.float32).astype(jnp.bfloat16)
        for weight in (query_weight, key_weight, value_weight)
    ]
    projected = jnp.concatenate(projections, axis=-1)
    queries = split_heads(projected[..., :local_width])
    key_values = projected[..., local_width:]
    nearby = {0: key_values}
    for offset in OFFSETS:
        nearby[offset] = passed_along(key_values, "tm", -offset)
    key_stack = jnp.stack([split_heads(nearby[offset][..., :local_width]) for offset in ORDERED])
    value_stack = jnp.stack([split_heads(nearby[offset][..., local_width:]) for offset in ORDERED])
    in_range = jnp.stack(
        [(frame_index + offset >= 0) & (frame_index + offset < frame_count) for offset in ORDERED]
    )
    scores = (
        jnp.einsum("fbphe,jfbphe->jfbph", queries, key_stack, preferred_element_type=jnp.float32)
        * score_scale
    )
    masked = jnp.where(in_range[:, None, None, None, None], scores, NEG_FILL)
    row_max = jnp.max(masked, axis=0)
    exponent = jnp.exp(masked - row_max)
    denominator = jnp.sum(exponent, axis=0)
    attention = exponent / denominator
    probs_low = attention.astype(jnp.bfloat16)
    attended = jnp.einsum(
        "jfbph,jfbphe->fbphe", probs_low, value_stack, preferred_element_type=jnp.float32
    ).astype(jnp.bfloat16)
    partial_out = jnp.dot(merge_heads(attended), output_weight, preferred_element_type=jnp.float32)
    summed_out = lax.psum_scatter(
        partial_out.astype(jnp.bfloat16), "space", scatter_dimension=2, tiled=True
    ).astype(jnp.float32)
    block_output = (values + summed_out).astype(jnp.bfloat16)
    out_grads = split_heads(
        jnp.einsum(
            "fbpc,hc->fbph",
            lax.all_gather(cotangent, "space", axis=2, tiled=True),
            output_weight,
            preferred_element_type=jnp.float32,
        ).astype(jnp.bfloat16)
    )
    prob_grads = jnp.einsum(
        "fbphe,jfbphe->jfbph", out_grads, value_stack, preferred_element_type=jnp.float32
    )
    row_delta = jnp.sum(attention * prob_grads, axis=0)
    score_grads = (attention * (prob_grads - row_delta)).astype(jnp.bfloat16)
    query_grads = (
        jnp.einsum(
            "jfbph,jfbphe->fbphe", score_grads, key_stack, preferred_element_type=jnp.float32
        )
        * score_scale
    ).astype(jnp.bfloat16)
    key_total = weigh_rows(score_grads[2], queries) * score_scale
    value_total = weigh_rows(probs_low[2], out_grads)
    for offset in OFFSETS:
        position = offset + 2
        sending = jnp.concatenate(
            [
                merge_heads(weigh_rows(score_grads[position], queries) * score_scale),
                merge_heads(weigh_rows(probs_low[position], out_grads)),
            ],
            axis=-1,
        )
        arrived = passed_along(sending.astype(jnp.bfloat16), "tm", offset).astype(sending.dtype)
        key_total = key_total + split_heads(arrived[..., :local_width])
        value_total = value_total + split_heads(arrived[..., local_width:])
    key_low = key_total.astype(jnp.bfloat16)
    value_low = value_total.astype(jnp.bfloat16)
    hidden_part = (
        back_heads(query_grads, query_weight)
        + back_heads(key_low, key_weight)
        + back_heads(value_low, value_weight)
    )
    hidden_grads = lax.psum_scatter(
        hidden_part.astype(jnp.bfloat16), "space", scatter_dimension=2, tiled=True
    ).astype(jnp.float32)
    scaled = hidden_grads * gain_values
    layer_grads = inverse * (
        scaled
        - jnp.mean(scaled, axis=-1, keepdims=True)
        - normed * jnp.mean(scaled * normed, axis=-1, keepdims=True)
    )
    input_grads = (cotangent.astype(jnp.float32) + layer_grads).astype(jnp.bfloat16)
    return (block_output, input_grads)


def solution(mesh):
    placed = (
        P("tm", None, "space", None),
        P("tm", None, "space", None),
        P(),
        P(None, "space"),
        P(None, "space"),
        P(None, "space"),
        P("space", None),
    )
    return jax.shard_map(
        per_device,
        mesh=mesh,
        in_specs=placed,
        out_specs=(P("tm", None, "space", None), P("tm", None, "space", None)),
        check_vma=False,
    )
```

profile of v0, /device:TPU:40, one launch (start us, length us, event | category | flops | bytes accessed | tf_op | source)
XLA Modules:
  0.0 147.2 jit_solution(5452947903148710020)
XLA Ops:
  1.5 1.3 fusion.36
  2.7 1.5 multiply_reduce_fusion.5
  5.4 8.2 %all_gather.6 = bf16[1,1,144,1280]{3,1,0,2:T(2,128)(2,1)S(1)} all-gather(bf16[1,1,36,1280]{3,1,0,2:T(2,128)(2,1)S(1)} %get-tuple-element.16), channel_id=1, replica_groups=mesh['tm'=128,'space'=4] {'space'}, dimensions={2}, use_global_device_ids=true | all-gather | bytes 460800 | tf_op jit(solution)/shard_map/all_gather | solution.py:55
  16.3 6.1 %collective-permute-start = (bf16[1,1,144,640]{3,2,1,0:T(8,128)(2,1)}, bf16[1,1,144,640]{3,2,1,0:T(8,128)(2,1)}, u32[]{:S(2)}, u32[]{:S(2)}) collective-permute-start(bf16[1,1,144,640]{3,2,1,0:T(8,128)(2,1)} %pad_maximum_fusion.4), channel_id=1, source_target_pairs={{0,8},{4,12},{8,16},{12,20},{16,24},{20,28},{24,32},{28,36},{32,40... | collective-permute-start | bytes 552968 | tf_op jit(solution)/shard_map/ppermute | solution.py:18
  22.4 4.3 %collective-permute-start.1 = (bf16[1,1,144,640]{3,2,1,0:T(8,128)(2,1)}, bf16[1,1,144,640]{3,2,1,0:T(8,128)(2,1)}, u32[]{:S(2)}, u32[]{:S(2)}) collective-permute-start(bf16[1,1,144,640]{3,2,1,0:T(8,128)(2,1)} %pad_maximum_fusion.4), channel_id=1, source_target_pairs={{0,4},{4,8},{8,12},{12,16},{16,20},{20,24},{24,28},{28,32},{32,36}... | collective-permute-start | bytes 552968 | tf_op jit(solution)/shard_map/ppermute | solution.py:18
  26.7 7.9 %collective-permute-start.2 = (bf16[1,1,144,640]{3,2,1,0:T(8,128)(2,1)}, bf16[1,1,144,640]{3,2,1,0:T(8,128)(2,1)S(1)}, u32[]{:S(2)}, u32[]{:S(2)}) collective-permute-start(bf16[1,1,144,640]{3,2,1,0:T(8,128)(2,1)} %pad_maximum_fusion.4), channel_id=1, source_target_pairs={{4,0},{8,4},{12,8},{16,12},{20,16},{24,20},{28,24},{32,28},{36,32}... | collective-permute-start | bytes 552968 | tf_op jit(solution)/shard_map/ppermute | solution.py:18
  34.6 4.0 %collective-permute-start.3 = (bf16[1,1,144,640]{3,2,1,0:T(8,128)(2,1)}, bf16[1,1,144,640]{3,2,1,0:T(8,128)(2,1)S(1)}, u32[]{:S(2)}, u32[]{:S(2)}) collective-permute-start(bf16[1,1,144,640]{3,2,1,0:T(8,128)(2,1)} %pad_maximum_fusion.4), channel_id=1, source_target_pairs={{8,0},{12,4},{16,8},{20,12},{24,16},{28,20},{32,24},{36,28},{40,32... | collective-permute-start | bytes 552968 | tf_op jit(solution)/shard_map/ppermute | solution.py:18
  39.6 14.8 %all_gather.7 = bf16[1,1,144,1280]{3,1,0,2:T(2,128)(2,1)S(1)} all-gather(bf16[1,1,36,1280]{3,1,0,2:T(2,128)(2,1)S(1)} %copy.53), channel_id=1, replica_groups=mesh['tm'=128,'space'=4] {'space'}, dimensions={2}, use_global_device_ids=true | all-gather | bytes 460800 | tf_op jit(solution)/shard_map/all_gather | solution.py:92
  58.1 1.6 %fusion.67 = (bf16[1,1,144,320]{3,2,1,0:T(8,128)(2,1)S(1)}, bf16[1,1,144,320]{3,2,1,0:T(8,128)(2,1)}) fusion(bf16[1,1,144,640]{3,2,1,0:T(8,128)(2,1)} %collective-permute-done.1), kind=kLoop, calls=%fused_computation.130 | loop fusion | bytes 368640 | tf_op jit(solution)/shard_map/slice | solution.py:67
  65.3 1.7 %copy.42 = bf16[1,1,144,320]{2,3,1,0:T(8,128)(2,1)} copy(bf16[1,1,144,320]{3,2,1,0:T(8,128)(2,1)} %get-tuple-element.31) | data formatting | bytes 184320 | tf_op jit(solution)/shard_map/slice | solution.py:66
  67.0 1.7 %copy.44 = bf16[1,1,144,320]{2,3,1,0:T(8,128)(2,1)} copy(bf16[1,1,144,320]{3,2,1,0:T(8,128)(2,1)} %get-tuple-element.29) | data formatting | bytes 184320 | tf_op jit(solution)/shard_map/slice | solution.py:66
  68.7 1.7 %copy.45 = bf16[1,1,144,320]{2,3,1,0:T(8,128)(2,1)} copy(bf16[1,1,144,320]{3,2,1,0:T(8,128)(2,1)} %get-tuple-element.27) | data formatting | bytes 184320 | tf_op jit(solution)/shard_map/slice | solution.py:66
  76.4 1.9 %collective-permute-start.7 = (bf16[1,1,144,640]{2,3,1,0:T(8,128)(2,1)S(1)}, bf16[1,1,144,640]{2,3,1,0:T(8,128)(2,1)S(1)}, u32[]{:S(2)}, u32[]{:S(2)}) collective-permute-start(bf16[1,1,144,640]{2,3,1,0:T(8,128)(2,1)S(1)} %pad_maximum_fusion.3), channel_id=1, source_target_pairs={{0,8},{4,12},{8,16},{12,20},{16,24},{20,28},{24,32},{28,36},{32,40... | collective-permute-start | bytes 552968 | tf_op jit(solution)/shard_map/ppermute | solution.py:18
  78.4 2.1 %collective-permute-start.6 = (bf16[1,1,144,640]{2,3,1,0:T(8,128)(2,1)S(1)}, bf16[1,1,144,640]{2,3,1,0:T(8,128)(2,1)S(1)}, u32[]{:S(2)}, u32[]{:S(2)}) collective-permute-start(bf16[1,1,144,640]{2,3,1,0:T(8,128)(2,1)S(1)} %pad_maximum_fusion.2), channel_id=1, source_target_pairs={{0,4},{4,8},{8,12},{12,16},{16,20},{20,24},{24,28},{28,32},{32,36}... | collective-permute-start | bytes 552968 | tf_op jit(solution)/shard_map/ppermute | solution.py:18
  80.5 10.3 %collective-permute-start.5 = (bf16[1,1,144,640]{2,3,1,0:T(8,128)(2,1)S(1)}, bf16[1,1,144,640]{2,3,1,0:T(8,128)(2,1)S(1)}, u32[]{:S(2)}, u32[]{:S(2)}) collective-permute-start(bf16[1,1,144,640]{2,3,1,0:T(8,128)(2,1)S(1)} %pad_maximum_fusion.1), channel_id=1, source_target_pairs={{4,0},{8,4},{12,8},{16,12},{20,16},{24,20},{28,24},{32,28},{36,32}... | collective-permute-start | bytes 552968 | tf_op jit(solution)/shard_map/ppermute | solution.py:18
  90.8 4.8 %collective-permute-start.4 = (bf16[1,1,144,640]{2,3,1,0:T(8,128)(2,1)S(1)}, bf16[1,1,144,640]{2,3,1,0:T(8,128)(2,1)S(1)}, u32[]{:S(2)}, u32[]{:S(2)}) collective-permute-start(bf16[1,1,144,640]{2,3,1,0:T(8,128)(2,1)S(1)} %pad_maximum_fusion), channel_id=1, source_target_pairs={{8,0},{12,4},{16,8},{20,12},{24,16},{28,20},{32,24},{36,28},{40,32... | collective-permute-start | bytes 552968 | tf_op jit(solution)/shard_map/ppermute | solution.py:18
  96.0 6.0 %collective-permute-done.7 = bf16[1,1,144,640]{2,3,1,0:T(8,128)(2,1)S(1)} collective-permute-done((bf16[1,1,144,640]{2,3,1,0:T(8,128)(2,1)S(1)}, bf16[1,1,144,640]{2,3,1,0:T(8,128)(2,1)S(1)}, u32[]{:S(2)}, u32[]{:S(2)}) %collective-permute-start.7) | collective-permute-done | bytes 184352 | tf_op jit(solution)/shard_map/ppermute | solution.py:18
  102.1 8.4 %collective-permute-done.6 = bf16[1,1,144,640]{2,3,1,0:T(8,128)(2,1)S(1)} collective-permute-done((bf16[1,1,144,640]{2,3,1,0:T(8,128)(2,1)S(1)}, bf16[1,1,144,640]{2,3,1,0:T(8,128)(2,1)S(1)}, u32[]{:S(2)}, u32[]{:S(2)}) %collective-permute-start.6) | collective-permute-done | bytes 184352 | tf_op jit(solution)/shard_map/ppermute | solution.py:18
  110.6 7.3 %collective-permute-done.4 = bf16[1,1,144,640]{2,3,1,0:T(8,128)(2,1)S(1)} collective-permute-done((bf16[1,1,144,640]{2,3,1,0:T(8,128)(2,1)S(1)}, bf16[1,1,144,640]{2,3,1,0:T(8,128)(2,1)S(1)}, u32[]{:S(2)}, u32[]{:S(2)}) %collective-permute-start.4) | collective-permute-done | bytes 184352 | tf_op jit(solution)/shard_map/ppermute | solution.py:18
  121.0 15.1 %fusion.58 = (bf16[40,1280]{1,0:T(8,128)(2,1)S(1)}, bf16[40,1280]{1,0:T(8,128)(2,1)S(1)}) fusion(bf16[1,1,144,1280]{3,2,1,0:T(8,128)(2,1)S(1)} %fusion.4, bf16[1,1,144,1280]{3,2,1,0:T(8,128)(2,1)S(1)} %fusion.3), kind=kCustom, calls=%all-reduce-scatter.2 | all-reduce-scatter fusion | flops 409601 | bytes 944128
  136.1 1.9 %collective-permute-start.8 = (bf16[12,1280]{1,0:T(8,128)(2,1)S(1)}, bf16[12,1280]{1,0:T(8,128)(2,1)S(1)}, u32[]{:S(2)}, u32[]{:S(2)}) collective-permute-start(bf16[12,1280]{1,0:T(8,128)(2,1)S(1)} %slice.130), channel_id=1, source_target_pairs={{0,1},{1,2},{2,3},{4,5},{5,6},{6,7},{8,9},{9,10},{10,11},{12,13},{... | collective-permute-start | bytes 92168
  138.0 1.3 dynamic-slice.6
  140.0 1.9 %collective-permute-start.9 = (bf16[12,1280]{1,0:T(8,128)(2,1)S(1)}, bf16[12,1280]{1,0:T(8,128)(2,1)S(1)}, u32[]{:S(2)}, u32[]{:S(2)}) collective-permute-start(bf16[12,1280]{1,0:T(8,128)(2,1)S(1)} %slice.131), channel_id=1, source_target_pairs={{0,1},{1,2},{2,3},{4,5},{5,6},{6,7},{8,9},{9,10},{10,11},{12,13},{... | collective-permute-start | bytes 92168
  143.1 2.3 %collective-permute-done.9 = bf16[12,1280]{1,0:T(8,128)(2,1)S(1)} collective-permute-done((bf16[12,1280]{1,0:T(8,128)(2,1)S(1)}, bf16[12,1280]{1,0:T(8,128)(2,1)S(1)}, u32[]{:S(2)}, u32[]{:S(2)}) %collective-permute-start.9) | collective-permute-done | bytes 30752
  (114 shorter events, 27.5 us)
Async XLA Ops:
  0.6 54.4 %copy-start = (bf16[1280,320]{0,1:T(8,128)(2,1)S(1)}, bf16[1280,320]{0,1:T(8,128)(2,1)}, u32[]{:S(2)}) copy-start(bf16[1280,320]{0,1:T(8,128)(2,1)} %param.10) | copy-start | bytes 2457604
  0.6 13.0 %copy-start.7 = (bf16[1280,320]{0,1:T(8,128)(2,1)S(1)}, bf16[1280,320]{0,1:T(8,128)(2,1)}, u32[]{:S(2)}) copy-start(bf16[1280,320]{0,1:T(8,128)(2,1)} %param.12) | copy-start | bytes 2457604
  13.6 1.9 %copy-start.9 = (bf16[1,1,144,1280]{3,1,0,2:T(2,128)(2,1)}, bf16[1,1,144,1280]{3,1,0,2:T(2,128)(2,1)S(1)}, u32[]{:S(2)}) copy-start(bf16[1,1,144,1280]{3,1,0,2:T(2,128)(2,1)S(1)} %all_gather.6) | copy-start | bytes 1105924
  13.6 1.4 copy-start.3
  15.5 24.0 %copy-start.15 = (bf16[1,1,36,1280]{3,2,1,0:T(8,128)(2,1)S(1)}, bf16[1,1,36,1280]{3,2,1,0:T(8,128)(2,1)}, u32[]{:S(2)}) copy-start(bf16[1,1,36,1280]{3,2,1,0:T(8,128)(2,1)} %param.8) | copy-start | bytes 276484
  16.3 40.7 %collective-permute-start = (bf16[1,1,144,640]{3,2,1,0:T(8,128)(2,1)}, bf16[1,1,144,640]{3,2,1,0:T(8,128)(2,1)}, u32[]{:S(2)}, u32[]{:S(2)}) collective-permute-start(bf16[1,1,144,640]{3,2,1,0:T(8,128)(2,1)} %pad_maximum_fusion.4), channel_id=1, source_target_pairs={{0,8},{4,12},{8,16},{12,20},{16,24},{20,28},{24,32},{28,36},{32,40... | collective-permute-start | bytes 552968 | tf_op jit(solution)/shard_map/ppermute | solution.py:18
  22.4 35.7 %collective-permute-start.1 = (bf16[1,1,144,640]{3,2,1,0:T(8,128)(2,1)}, bf16[1,1,144,640]{3,2,1,0:T(8,128)(2,1)}, u32[]{:S(2)}, u32[]{:S(2)}) collective-permute-start(bf16[1,1,144,640]{3,2,1,0:T(8,128)(2,1)} %pad_maximum_fusion.4), channel_id=1, source_target_pairs={{0,4},{4,8},{8,12},{12,16},{16,20},{20,24},{24,28},{28,32},{32,36}... | collective-permute-start | bytes 552968 | tf_op jit(solution)/shard_map/ppermute | solution.py:18
  26.7 33.0 %collective-permute-start.2 = (bf16[1,1,144,640]{3,2,1,0:T(8,128)(2,1)}, bf16[1,1,144,640]{3,2,1,0:T(8,128)(2,1)S(1)}, u32[]{:S(2)}, u32[]{:S(2)}) collective-permute-start(bf16[1,1,144,640]{3,2,1,0:T(8,128)(2,1)} %pad_maximum_fusion.4), channel_id=1, source_target_pairs={{4,0},{8,4},{12,8},{16,12},{20,16},{24,20},{28,24},{32,28},{36,32}... | collective-permute-start | bytes 552968 | tf_op jit(solution)/shard_map/ppermute | solution.py:18
  34.6 27.5 %collective-permute-start.3 = (bf16[1,1,144,640]{3,2,1,0:T(8,128)(2,1)}, bf16[1,1,144,640]{3,2,1,0:T(8,128)(2,1)S(1)}, u32[]{:S(2)}, u32[]{:S(2)}) collective-permute-start(bf16[1,1,144,640]{3,2,1,0:T(8,128)(2,1)} %pad_maximum_fusion.4), channel_id=1, source_target_pairs={{8,0},{12,4},{16,8},{20,12},{24,16},{28,20},{32,24},{36,28},{40,32... | collective-permute-start | bytes 552968 | tf_op jit(solution)/shard_map/ppermute | solution.py:18
  39.3 15.1 %copy-start.5 = (bf16[320,1280]{1,0:T(8,128)(2,1)S(1)}, bf16[320,1280]{1,0:T(8,128)(2,1)}, u32[]{:S(2)}) copy-start(bf16[320,1280]{1,0:T(8,128)(2,1)} %param.13) | copy-start | bytes 2457604
  70.4 2.9 %copy-start.11 = (bf16[1,1,144,320]{2,3,1,0:T(8,128)(2,1)S(1)}, bf16[1,1,144,320]{2,3,1,0:T(8,128)(2,1)}, u32[]{:S(2)}) copy-start(bf16[1,1,144,320]{2,3,1,0:T(8,128)(2,1)} %copy.51) | copy-start | bytes 276484
  70.4 3.0 %copy-start.14 = (bf16[1,1,144,320]{2,3,1,0:T(8,128)(2,1)S(1)}, bf16[1,1,144,320]{2,3,1,0:T(8,128)(2,1)}, u32[]{:S(2)}) copy-start(bf16[1,1,144,320]{2,3,1,0:T(8,128)(2,1)} %copy.42) | copy-start | bytes 276484
  71.3 2.1 %copy-start.12 = (bf16[1,1,144,320]{2,3,1,0:T(8,128)(2,1)S(1)}, bf16[1,1,144,320]{2,3,1,0:T(8,128)(2,1)}, u32[]{:S(2)}) copy-start(bf16[1,1,144,320]{2,3,1,0:T(8,128)(2,1)} %copy.44) | copy-start | bytes 276484
  76.4 25.7 %collective-permute-start.7 = (bf16[1,1,144,640]{2,3,1,0:T(8,128)(2,1)S(1)}, bf16[1,1,144,640]{2,3,1,0:T(8,128)(2,1)S(1)}, u32[]{:S(2)}, u32[]{:S(2)}) collective-permute-start(bf16[1,1,144,640]{2,3,1,0:T(8,128)(2,1)S(1)} %pad_maximum_fusion.3), channel_id=1, source_target_pairs={{0,8},{4,12},{8,16},{12,20},{16,24},{20,28},{24,32},{28,36},{32,40... | collective-permute-start | bytes 552968 | tf_op jit(solution)/shard_map/ppermute | solution.py:18
  78.4 17.3 %copy-start.6 = (bf16[320,1280]{1,0:T(8,128)(2,1)S(1)}, bf16[320,1280]{1,0:T(8,128)(2,1)}, u32[]{:S(2)}) copy-start(bf16[320,1280]{1,0:T(8,128)(2,1)} %param.13) | copy-start | bytes 2457604
  78.4 32.1 %collective-permute-start.6 = (bf16[1,1,144,640]{2,3,1,0:T(8,128)(2,1)S(1)}, bf16[1,1,144,640]{2,3,1,0:T(8,128)(2,1)S(1)}, u32[]{:S(2)}, u32[]{:S(2)}) collective-permute-start(bf16[1,1,144,640]{2,3,1,0:T(8,128)(2,1)S(1)} %pad_maximum_fusion.2), channel_id=1, source_target_pairs={{0,4},{4,8},{8,12},{12,16},{16,20},{20,24},{24,28},{28,32},{32,36}... | collective-permute-start | bytes 552968 | tf_op jit(solution)/shard_map/ppermute | solution.py:18
  80.5 30.0 %collective-permute-start.5 = (bf16[1,1,144,640]{2,3,1,0:T(8,128)(2,1)S(1)}, bf16[1,1,144,640]{2,3,1,0:T(8,128)(2,1)S(1)}, u32[]{:S(2)}, u32[]{:S(2)}) collective-permute-start(bf16[1,1,144,640]{2,3,1,0:T(8,128)(2,1)S(1)} %pad_maximum_fusion.1), channel_id=1, source_target_pairs={{4,0},{8,4},{12,8},{16,12},{20,16},{24,20},{28,24},{32,28},{36,32}... | collective-permute-start | bytes 552968 | tf_op jit(solution)/shard_map/ppermute | solution.py:18
  90.8 27.1 %collective-permute-start.4 = (bf16[1,1,144,640]{2,3,1,0:T(8,128)(2,1)S(1)}, bf16[1,1,144,640]{2,3,1,0:T(8,128)(2,1)S(1)}, u32[]{:S(2)}, u32[]{:S(2)}) collective-permute-start(bf16[1,1,144,640]{2,3,1,0:T(8,128)(2,1)S(1)} %pad_maximum_fusion), channel_id=1, source_target_pairs={{8,0},{12,4},{16,8},{20,12},{24,16},{28,20},{32,24},{36,28},{40,32... | collective-permute-start | bytes 552968 | tf_op jit(solution)/shard_map/ppermute | solution.py:18
  117.9 1.1 copy-start.4
  119.5 1.1 copy-start.8
  121.0 21.2 %copy-start.1 = (bf16[1,1,36,1280]{3,2,1,0:T(8,128)(2,1)S(1)}, bf16[1,1,36,1280]{3,2,1,0:T(8,128)(2,1)}, u32[]{:S(2)}) copy-start(bf16[1,1,36,1280]{3,2,1,0:T(8,128)(2,1)} %param.7) | copy-start | bytes 276484
  136.1 5.8 %collective-permute-start.8 = (bf16[12,1280]{1,0:T(8,128)(2,1)S(1)}, bf16[12,1280]{1,0:T(8,128)(2,1)S(1)}, u32[]{:S(2)}, u32[]{:S(2)}) collective-permute-start(bf16[12,1280]{1,0:T(8,128)(2,1)S(1)} %slice.130), channel_id=1, source_target_pairs={{0,1},{1,2},{2,3},{4,5},{5,6},{6,7},{8,9},{9,10},{10,11},{12,13},{... | collective-permute-start | bytes 92168
  140.0 5.3 %collective-permute-start.9 = (bf16[12,1280]{1,0:T(8,128)(2,1)S(1)}, bf16[12,1280]{1,0:T(8,128)(2,1)S(1)}, u32[]{:S(2)}, u32[]{:S(2)}) collective-permute-start(bf16[12,1280]{1,0:T(8,128)(2,1)S(1)} %slice.131), channel_id=1, source_target_pairs={{0,1},{1,2},{2,3},{4,5},{5,6},{6,7},{8,9},{9,10},{10,11},{12,13},{... | collective-permute-start | bytes 92168
  142.1 4.0 %copy-start.16 = (bf16[1,1,36,1280]{3,2,1,0:T(8,128)(2,1)S(1)}, bf16[1,1,36,1280]{3,2,1,0:T(8,128)(2,1)}, u32[]{:S(2)}) copy-start(bf16[1,1,36,1280]{3,2,1,0:T(8,128)(2,1)} %param.8) | copy-start | bytes 276484
  (3 other events, 3.2 us)
where the time goes:
time: 148 us; the launch traced here: 147 us
  starting transfers between devices  45.1 us (30%)
  blocking collectives  38 us (26%)
  local copies, waits for them, and re-layouts  25.4 us (17%)
  waiting for transfers between devices  23.9 us (16%)
  other arithmetic  9.5 us (6%)
  matrix products  3.31 us (2%)
  between operations  1.95 us (1%)
    ppermute x8, starting transfers between devices, passed_along(): return lax.ppermute(block, axis, route)  41.3 us
    ppermute x8, waiting for transfers between devices, passed_along(): return lax.ppermute(block, axis, route)  21.7 us
    unnamed x1, blocking collectives  15.1 us
    all_gather x1, blocking collectives, per_device(): lax.all_gather(cotangent, 'space', axis=2, tiled=True)  14.8 us
    unnamed x52, local copies, waits for them, and re-layouts  11.5 us
    all_gather x1, blocking collectives, per_device(): rows_piece = lax.all_gather(hidden, 'space', axis=2, tiled=True)  8.19 us
    slice x8, local copies, waits for them, and re-layouts, per_device(): nearby[offset][..., local_width:]  6.57 us
    slice x4, local copies, waits for them, and re-layouts, per_device(): nearby[offset][..., :local_width]  5.84 us
  transfers between devices with their start and end apart: 10, of which 4 were waited for; matrix products, arithmetic and copies ran while one was open for 8% of the time, Pallas kernels for 0%

commit v1 on v0

v1 whole, which is shorter than its diff:
```python
import functools

import jax
import jax.numpy as jnp
from jax import lax
from jax.experimental import pallas as pl
from jax.experimental.pallas import tpu as pltpu
from jax.sharding import PartitionSpec as P

HEAD_DIM = 64
EPSILON = 1e-05
NEG_FILL = -1e30
ORDERED = (-2, -1, 0, 1, 2)
OFFSETS = (-2, -1, 1, 2)
SHARDS = 4
BF16 = jnp.bfloat16
F32 = jnp.float32

VMEM = pl.BlockSpec(memory_space=pltpu.VMEM)
SMEM = pl.BlockSpec(memory_space=pltpu.SMEM)
PARAMS = pltpu.CompilerParams(vmem_limit_bytes=48 * 1024 * 1024)


def dot(a, b):
    return lax.dot_general(a, b, (((1,), (0,)), ((), ())), preferred_element_type=F32)


def dot_t(a, b):
    return lax.dot_general(a, b, (((1,), (1,)), ((), ())), preferred_element_type=F32)


def normalized(x):
    center = jnp.mean(x, axis=-1, keepdims=True)
    shifted = x - center
    spread = jnp.mean(jnp.square(shifted), axis=-1, keepdims=True)
    inverse = lax.rsqrt(spread + EPSILON)
    return shifted * inverse, inverse


def norm_kernel(x_ref, cot_ref, gain_ref, out_ref):
    normed, _ = normalized(x_ref[...].astype(F32))
    out_ref[0] = (normed * gain_ref[...].astype(F32)).astype(BF16)
    out_ref[1] = cot_ref[...]


def project_kernel(g_ref, wq_ref, wk_ref, wv_ref, wo_ref, a_ref, b_ref, rows_ref):
    piece = g_ref.shape[2]

    def gathered(which):
        for s in range(SHARDS):
            rows_ref[piece * s : piece * (s + 1), :] = g_ref[s, which].astype(F32)
        return rows_ref[...].astype(BF16)

    hidden = gathered(0)
    keys = dot_t(hidden, wk_ref[...])
    vals = dot_t(hidden, wv_ref[...])
    b_ref[...] = jnp.concatenate([keys, vals], axis=1).astype(BF16)
    queries = dot_t(hidden, wq_ref[...])
    out_grads = dot_t(gathered(1), wo_ref[...])
    a_ref[...] = jnp.concatenate([queries, out_grads], axis=1).astype(BF16)


def head_lanes(width):
    lane = lax.broadcasted_iota(jnp.int32, (width, 256), 0) // HEAD_DIM
    col = lax.broadcasted_iota(jnp.int32, (width, 256), 1)
    heads = width // HEAD_DIM // 2
    want = jnp.where(lane < heads, lane, lane - heads + 128)
    return (col == want).astype(BF16)


def attend_kernel(frames, frame_ref, a_ref, *refs):
    b_refs = refs[:5]
    send_refs, own_ref, mixed_ref = refs[5:9], refs[9], refs[10]
    frame = frame_ref[0]
    a = a_ref[...].astype(F32)
    width = a.shape[1]
    reduce_mat = head_lanes(width)
    scores, prob_grads = [], []
    for offset, b_ref in zip(ORDERED, b_refs):
        product = a * b_ref[...].astype(F32)
        high = product.astype(BF16)
        low = (product - high.astype(F32)).astype(BF16)
        sums = dot(high, reduce_mat) + dot(low, reduce_mat)
        present = (frame + offset >= 0) & (frame + offset < frames)
        scores.append(jnp.where(present, sums[:, :128] * (HEAD_DIM**-0.5), NEG_FILL))
        prob_grads.append(sums[:, 128:])
    row_max = functools.reduce(jnp.maximum, scores)
    exponent = [jnp.exp(s - row_max) for s in scores]
    denominator = sum(exponent)
    attention = [e / denominator for e in exponent]
    row_delta = sum(p * g for p, g in zip(attention, prob_grads))
    mixed = jnp.zeros_like(a)
    scale = jnp.where(
        lax.broadcasted_iota(jnp.int32, a.shape, 1) < width // 2, HEAD_DIM**-0.5, 1.0
    )
    scaled_a = a * scale
    sends = iter(send_refs)
    for offset, b_ref, p, g in zip(ORDERED, b_refs, attention, prob_grads):
        score_grads = (p * (g - row_delta)).astype(BF16)
        small = jnp.concatenate([score_grads, p.astype(BF16)], axis=1)
        weights = dot_t(small, reduce_mat)
        mixed = mixed + weights * b_ref[...].astype(F32)
        if offset == 0:
            own_ref[...] = weights * scaled_a
        else:
            next(sends)[...] = (weights * scaled_a).astype(BF16)
    mixed_ref[...] = (mixed * scale).astype(BF16)


def output_kernel(mixed_ref, wo_ref, out_ref, rows_ref):
    half = mixed_ref.shape[1] // 2
    piece = out_ref.shape[1]
    rows_ref[...] = dot(mixed_ref[:, half:], wo_ref[...])
    for s in range(SHARDS):
        out_ref[s] = rows_ref[piece * s : piece * (s + 1), :].astype(BF16)


def hidden_kernel(mixed_ref, own_ref, r0, r1, r2, r3, wq_ref, wk_ref, wv_ref, out_ref, rows_ref):
    half = mixed_ref.shape[1] // 2
    piece = out_ref.shape[1]
    total = own_ref[...]
    for r in (r0, r1, r2, r3):
        total = total + r[...].astype(F32)
    total = total.astype(BF16)
    rows_ref[...] = (
        dot(mixed_ref[:, :half], wq_ref[...])
        + dot(total[:, :half], wk_ref[...])
        + dot(total[:, half:], wv_ref[...])
    )
    for s in range(SHARDS):
        out_ref[s] = rows_ref[piece * s : piece * (s + 1), :].astype(BF16)


def finish_kernel(x_ref, cot_ref, gain_ref, out_parts, grad_parts, block_ref, grads_ref):
    x = x_ref[...].astype(F32)
    block_ref[...] = (x + sum(out_parts[s].astype(F32) for s in range(SHARDS))).astype(BF16)
    normed, inverse = normalized(x)
    scaled = sum(grad_parts[s].astype(F32) for s in range(SHARDS)) * gain_ref[...].astype(F32)
    layer_grads = inverse * (
        scaled
        - jnp.mean(scaled, axis=-1, keepdims=True)
        - normed * jnp.mean(scaled * normed, axis=-1, keepdims=True)
    )
    grads_ref[...] = (cot_ref[...].astype(F32) + layer_grads).astype(BF16)


def call(kernel, out_shape, in_specs, scratch=(), flops=0, bytes_accessed=0):
    return pl.pallas_call(
        kernel,
        out_shape=out_shape,
        in_specs=in_specs,
        out_specs=jax.tree.map(lambda _: VMEM, out_shape),
        scratch_shapes=list(scratch),
        compiler_params=PARAMS,
        cost_estimate=pl.CostEstimate(flops=flops, bytes_accessed=bytes_accessed, transcendentals=0),
    )


def passed_along(block, distance):
    count = lax.axis_size("tm")
    route = [(i, i + distance) for i in range(count) if 0 <= i + distance < count]
    return lax.ppermute(block, "tm", route)


def swapped(parts):
    return lax.all_to_all(parts, "space", 0, 0)


def per_device(inputs, cotangent, norm_gain, query_weight, key_weight, value_weight, output_weight):
    frame = lax.axis_index("tm").astype(jnp.int32).reshape(1)
    frames = lax.axis_size("tm")
    piece, channels = inputs.shape[2:]
    rows, local = piece * SHARDS, query_weight.shape[1]
    x = inputs.reshape(piece, channels)
    cot = cotangent.reshape(piece, channels)
    gain = norm_gain.reshape(1, channels)
    wq, wk, wv = query_weight.T, key_weight.T, value_weight.T
    wo = output_weight
    shape = jax.ShapeDtypeStruct

    both = call(norm_kernel, shape((2, piece, channels), BF16), [VMEM] * 3)(x, cot, gain)
    gathered = lax.all_gather(both, "space", axis=0)
    a, b = call(
        project_kernel,
        (shape((rows, 2 * local), BF16), shape((rows, 2 * local), BF16)),
        [VMEM] * 5,
        [pltpu.VMEM((rows, channels), F32)],
    )(gathered, wq, wk, wv, wo)
    near = {offset: passed_along(b, -offset) for offset in OFFSETS}
    near[0] = b
    wide = shape((rows, 2 * local), BF16)
    *sends, own, mixed = call(
        functools.partial(attend_kernel, frames),
        (wide, wide, wide, wide, shape((rows, 2 * local), F32), wide),
        [SMEM] + [VMEM] * 6,
    )(frame, a, *[near[offset] for offset in ORDERED])
    arrived = [passed_along(send, offset) for offset, send in zip(OFFSETS, sends)]
    parts = shape((SHARDS, piece, channels), BF16)
    out_parts = call(output_kernel, parts, [VMEM] * 2, [pltpu.VMEM((rows, channels), F32)])(mixed, wo)
    out_parts = swapped(out_parts)
    grad_parts = call(hidden_kernel, parts, [VMEM] * 9, [pltpu.VMEM((rows, channels), F32)])(
        mixed, own, *arrived, wq, wk, wv
    )
    grad_parts = swapped(grad_parts)
    block, grads = call(
        finish_kernel, (shape((piece, channels), BF16), shape((piece, channels), BF16)), [VMEM] * 5
    )(x, cot, gain, out_parts, grad_parts)
    return block.reshape(inputs.shape), grads.reshape(inputs.shape)


def solution(mesh):
    placed = (
        P("tm", None, "space", None),
        P("tm", None, "space", None),
        P(),
        P(None, "space"),
        P(None, "space"),
        P(None, "space"),
        P("space", None),
    )
    return jax.shard_map(
        per_device,
        mesh=mesh,
        in_specs=placed,
        out_specs=(P("tm", None, "space", None), P("tm", None, "space", None)),
        check_vma=False,
    )
```

time: 148 us -> 112 us (0.76)
  the two profiles are of different devices: /device:TPU:40 before, /device:TPU:81 now
where the time goes in v1:
time: 112 us; the launch traced here: 111 us
  starting transfers between devices  43 us (38%)
  blocking collectives  26.6 us (24%)
  waiting for transfers between devices  23.9 us (21%)
  local copies, waits for them, and re-layouts  11.2 us (10%)
  Pallas kernels  5.47 us (5%)
    ppermute x8, starting transfers between devices, passed_along(): return lax.ppermute(block, 'tm', route)  31.6 us
    ppermute x8, waiting for transfers between devices, passed_along(): return lax.ppermute(block, 'tm', route)  23.9 us
    all_to_all x1, blocking collectives, swapped(): return lax.all_to_all(parts, 'space', 0, 0)  17.3 us
    all_to_all x1, starting transfers between devices, swapped(): return lax.all_to_all(parts, 'space', 0, 0)  11.4 us
    unnamed x40, local copies, waits for them, and re-layouts  10.4 us
    all_gather x1, blocking collectives, per_device(): gathered = lax.all_gather(both, 'space', axis=0)  9.38 us
  transfers between devices with their start and end apart: 9, of which 6 were waited for; matrix products, arithmetic and copies ran while one was open for 0% of the time, Pallas kernels for 1%

profile of v1, /device:TPU:81, one launch (start us, length us, event | category | flops | bytes accessed | tf_op | source)
XLA Modules:
  0.0 111.1 jit_solution(3572680061182836698)
XLA Ops:
  1.4 0.9 copy-done.8
  2.3 0.9 copy-done.10
  3.4 9.4 %all-gather = bf16[8,36,1280]{2,1,0:T(8,128)(2,1)S(1)} all-gather(bf16[2,36,1280]{2,1,0:T(8,128)(2,1)S(1)} %shard_map.86), channel_id=2, replica_groups=mesh['tm'=128,'space'=4] {'space'}, dimensions={0}, use_global_device_ids=true | all-gather | bytes 921600 | tf_op jit(solution)/shard_map/all_gather | solution.py:182
  12.8 1.1 %copy-done.1 = bf16[1280,320]{0,1:T(8,128)(2,1)S(1)} copy-done((bf16[1280,320]{0,1:T(8,128)(2,1)S(1)}, bf16[1280,320]{0,1:T(8,128)(2,1)}, u32[]{:S(2)}) %copy-start.1) | copy-done | bytes 819224
  13.9 1.1 %copy-done.3 = bf16[1280,320]{0,1:T(8,128)(2,1)S(1)} copy-done((bf16[1280,320]{0,1:T(8,128)(2,1)S(1)}, bf16[1280,320]{0,1:T(8,128)(2,1)}, u32[]{:S(2)}) %copy-start.3) | copy-done | bytes 819224
  15.1 1.1 %copy-done.5 = bf16[1280,320]{0,1:T(8,128)(2,1)S(1)} copy-done((bf16[1280,320]{0,1:T(8,128)(2,1)S(1)}, bf16[1280,320]{0,1:T(8,128)(2,1)}, u32[]{:S(2)}) %copy-start.5) | copy-done | bytes 819224
  16.2 1.4 %shard_map.87 = (bf16[144,640]{1,0:T(8,128)(2,1)S(1)}, bf16[144,640]{1,0:T(8,128)(2,1)S(1)}) custom-call(bf16[4,2,36,1280]{3,2,1,0:T(8,128)(2,1)S(1)} %bitcast.9, bf16[320,1280]{1,0:T(8,128)(2,1)S(1)} %bitcast.10, bf16[320,1280]{1,0:T(8,128)(2,1)S(1)} %bitcast.12, bf16[320,1280]{1,0:T(8,128)(2,1)S(1)} %bitcast.14, bf16[320,1280]{1,0:T(8,128)(2,1)S(1)} %copy-done), custom_call_target="tpu_custom_call" | custom-call | tf_op jit(solution)/shard_map/pallas_call | solution.py:183
  17.6 11.7 %collective-permute-start.3 = (bf16[144,640]{1,0:T(8,128)(2,1)S(1)}, bf16[144,640]{1,0:T(8,128)(2,1)S(1)}, u32[]{:S(2)}, u32[]{:S(2)}) collective-permute-start(bf16[144,640]{1,0:T(8,128)(2,1)S(1)} %get-tuple-element.13.refs_2_), channel_id=1, source_target_pairs={{8,0},{12,4},{16,8},{20,12},{24,16},{28,20},{32,24},{36,28},{40,32... | collective-permute-start | bytes 552968 | tf_op jit(solution)/shard_map/ppermute | solution.py:162
  29.3 2.2 %collective-permute-start.2 = (bf16[144,640]{1,0:T(8,128)(2,1)S(1)}, bf16[144,640]{1,0:T(8,128)(2,1)S(1)}, u32[]{:S(2)}, u32[]{:S(2)}) collective-permute-start(bf16[144,640]{1,0:T(8,128)(2,1)S(1)} %get-tuple-element.13.refs_2_), channel_id=1, source_target_pairs={{4,0},{8,4},{12,8},{16,12},{20,16},{24,20},{28,24},{32,28},{36,32}... | collective-permute-start | bytes 552968 | tf_op jit(solution)/shard_map/ppermute | solution.py:162
  31.5 3.1 %collective-permute-start.1 = (bf16[144,640]{1,0:T(8,128)(2,1)S(1)}, bf16[144,640]{1,0:T(8,128)(2,1)S(1)}, u32[]{:S(2)}, u32[]{:S(2)}) collective-permute-start(bf16[144,640]{1,0:T(8,128)(2,1)S(1)} %get-tuple-element.13.refs_2_), channel_id=1, source_target_pairs={{0,4},{4,8},{8,12},{12,16},{16,20},{20,24},{24,28},{28,32},{32,36}... | collective-permute-start | bytes 552968 | tf_op jit(solution)/shard_map/ppermute | solution.py:162
  34.6 1.9 %collective-permute-start = (bf16[144,640]{1,0:T(8,128)(2,1)S(1)}, bf16[144,640]{1,0:T(8,128)(2,1)S(1)}, u32[]{:S(2)}, u32[]{:S(2)}) collective-permute-start(bf16[144,640]{1,0:T(8,128)(2,1)S(1)} %get-tuple-element.13.refs_2_), channel_id=1, source_target_pairs={{0,8},{4,12},{8,16},{12,20},{16,24},{20,28},{24,32},{28,36},{32,40... | collective-permute-start | bytes 552968 | tf_op jit(solution)/shard_map/ppermute | solution.py:162
  37.2 1.7 %collective-permute-done.1.refs_1_ = bf16[144,640]{1,0:T(8,128)(2,1)S(1)} collective-permute-done((bf16[144,640]{1,0:T(8,128)(2,1)S(1)}, bf16[144,640]{1,0:T(8,128)(2,1)S(1)}, u32[]{:S(2)}, u32[]{:S(2)}) %collective-permute-start.1) | collective-permute-done | bytes 184352 | tf_op jit(solution)/shard_map/ppermute | solution.py:162
  38.9 11.1 %collective-permute-done.refs_0_ = bf16[144,640]{1,0:T(8,128)(2,1)S(1)} collective-permute-done((bf16[144,640]{1,0:T(8,128)(2,1)S(1)}, bf16[144,640]{1,0:T(8,128)(2,1)S(1)}, u32[]{:S(2)}, u32[]{:S(2)}) %collective-permute-start) | collective-permute-done | bytes 184352 | tf_op jit(solution)/shard_map/ppermute | solution.py:162
  50.0 1.7 %shard_map.88 = (bf16[144,640]{1,0:T(8,128)(2,1)S(1)}, bf16[144,640]{1,0:T(8,128)(2,1)S(1)}, bf16[144,640]{1,0:T(8,128)(2,1)S(1)}, bf16[144,640]{1,0:T(8,128)(2,...) custom-call(s32[1]{0:T(128)} %bitcast.2.frame_ref, bf16[144,640]{1,0:T(8,128)(2,1)S(1)} %get-tuple-element.12.a_ref, ...), custom_call_target="tpu_custom_call" | custom-call | tf_op jit(solution)/shard_map/pallas_call | solution.py:192
  56.3 11.4 %all-to-all-start = ((bf16[4,36,1280]{2,1,0:T(8,128)(2,1)}), bf16[4,36,1280]{2,1,0:T(8,128)(2,1)S(1)}, u32[]{:S(2)}, u32[]{:S(2)}) async-start(bf16[4,36,1280]{2,1,0:T(8,128)(2,1)} %copy-done.7), calls=%async_computation | async-start | bytes 819200 | tf_op jit(solution)/shard_map/all_to_all | solution.py:166
  67.7 1.9 %collective-permute-start.4 = (bf16[144,640]{1,0:T(8,128)(2,1)}, bf16[144,640]{1,0:T(8,128)(2,1)S(1)}, u32[]{:S(2)}, u32[]{:S(2)}) collective-permute-start(bf16[144,640]{1,0:T(8,128)(2,1)} %copy-done.19), channel_id=1, source_target_pairs={{8,0},{12,4},{16,8},{20,12},{24,16},{28,20},{32,24},{36,28},{40,32... | collective-permute-start | bytes 552968 | tf_op jit(solution)/shard_map/ppermute | solution.py:162
  69.6 1.9 %collective-permute-start.5 = (bf16[144,640]{1,0:T(8,128)(2,1)}, bf16[144,640]{1,0:T(8,128)(2,1)S(1)}, u32[]{:S(2)}, u32[]{:S(2)}) collective-permute-start(bf16[144,640]{1,0:T(8,128)(2,1)} %copy-done.18), channel_id=1, source_target_pairs={{4,0},{8,4},{12,8},{16,12},{20,16},{24,20},{28,24},{32,28},{36,32}... | collective-permute-start | bytes 552968 | tf_op jit(solution)/shard_map/ppermute | solution.py:162
  71.6 3.4 %collective-permute-start.6 = (bf16[144,640]{1,0:T(8,128)(2,1)S(1)}, bf16[144,640]{1,0:T(8,128)(2,1)S(1)}, u32[]{:S(2)}, u32[]{:S(2)}) collective-permute-start(bf16[144,640]{1,0:T(8,128)(2,1)S(1)} %copy-done.17), channel_id=1, source_target_pairs={{0,4},{4,8},{8,12},{12,16},{16,20},{20,24},{24,28},{28,32},{32,36}... | collective-permute-start | bytes 552968 | tf_op jit(solution)/shard_map/ppermute | solution.py:162
  75.0 5.5 %collective-permute-start.7 = (bf16[144,640]{1,0:T(8,128)(2,1)S(1)}, bf16[144,640]{1,0:T(8,128)(2,1)S(1)}, u32[]{:S(2)}, u32[]{:S(2)}) collective-permute-start(bf16[144,640]{1,0:T(8,128)(2,1)S(1)} %copy-done.15), channel_id=1, source_target_pairs={{0,8},{4,12},{8,16},{12,20},{16,24},{20,28},{24,32},{28,36},{32,40... | collective-permute-start | bytes 552968 | tf_op jit(solution)/shard_map/ppermute | solution.py:162
  80.5 0.9 collective-permute-done.5.r1
  82.0 8.9 %collective-permute-done.7.r3 = bf16[144,640]{1,0:T(8,128)(2,1)S(1)} collective-permute-done((bf16[144,640]{1,0:T(8,128)(2,1)S(1)}, bf16[144,640]{1,0:T(8,128)(2,1)S(1)}, u32[]{:S(2)}, u32[]{:S(2)}) %collective-permute-start.7) | collective-permute-done | bytes 184352 | tf_op jit(solution)/shard_map/ppermute | solution.py:162
  91.0 1.0 copy-done.13
  92.8 17.3 %all_to_all.10.grad_parts = bf16[4,36,1280]{2,1,0:T(8,128)(2,1)S(1)} all-to-all(bf16[4,36,1280]{2,1,0:T(8,128)(2,1)S(1)} %shard_map.90), channel_id=1, replica_groups=mesh['tm'=128,'space'=4] {'space'}, dimensions={0} | all-to-all | bytes 737280 | tf_op jit(solution)/shard_map/all_to_all | solution.py:166
  110.1 1.0 shard_map.91
  (43 shorter events, 7.6 us)
Async XLA Ops:
  0.6 12.2 %copy-start = (bf16[320,1280]{1,0:T(8,128)(2,1)S(1)}, bf16[320,1280]{1,0:T(8,128)(2,1)}, u32[]{:S(2)}) copy-start(bf16[320,1280]{1,0:T(8,128)(2,1)} %wo_ref.3) | copy-start | bytes 2457604
  1.4 0.9 copy-start.8
  2.3 0.9 copy-start.10
  12.8 1.1 %copy-start.1 = (bf16[1280,320]{0,1:T(8,128)(2,1)S(1)}, bf16[1280,320]{0,1:T(8,128)(2,1)}, u32[]{:S(2)}) copy-start(bf16[1280,320]{0,1:T(8,128)(2,1)} %param.10) | copy-start | bytes 2457604
  13.9 1.1 %copy-start.3 = (bf16[1280,320]{0,1:T(8,128)(2,1)S(1)}, bf16[1280,320]{0,1:T(8,128)(2,1)}, u32[]{:S(2)}) copy-start(bf16[1280,320]{0,1:T(8,128)(2,1)} %param.11) | copy-start | bytes 2457604
  15.1 1.1 %copy-start.5 = (bf16[1280,320]{0,1:T(8,128)(2,1)S(1)}, bf16[1280,320]{0,1:T(8,128)(2,1)}, u32[]{:S(2)}) copy-start(bf16[1280,320]{0,1:T(8,128)(2,1)} %param.12) | copy-start | bytes 2457604
  17.6 19.6 %collective-permute-start.3 = (bf16[144,640]{1,0:T(8,128)(2,1)S(1)}, bf16[144,640]{1,0:T(8,128)(2,1)S(1)}, u32[]{:S(2)}, u32[]{:S(2)}) collective-permute-start(bf16[144,640]{1,0:T(8,128)(2,1)S(1)} %get-tuple-element.13.refs_2_), channel_id=1, source_target_pairs={{8,0},{12,4},{16,8},{20,12},{24,16},{28,20},{32,24},{36,28},{40,32... | collective-permute-start | bytes 552968 | tf_op jit(solution)/shard_map/ppermute | solution.py:162
  29.3 7.8 %collective-permute-start.2 = (bf16[144,640]{1,0:T(8,128)(2,1)S(1)}, bf16[144,640]{1,0:T(8,128)(2,1)S(1)}, u32[]{:S(2)}, u32[]{:S(2)}) collective-permute-start(bf16[144,640]{1,0:T(8,128)(2,1)S(1)} %get-tuple-element.13.refs_2_), channel_id=1, source_target_pairs={{4,0},{8,4},{12,8},{16,12},{20,16},{24,20},{28,24},{32,28},{36,32}... | collective-permute-start | bytes 552968 | tf_op jit(solution)/shard_map/ppermute | solution.py:162
  31.5 7.3 %collective-permute-start.1 = (bf16[144,640]{1,0:T(8,128)(2,1)S(1)}, bf16[144,640]{1,0:T(8,128)(2,1)S(1)}, u32[]{:S(2)}, u32[]{:S(2)}) collective-permute-start(bf16[144,640]{1,0:T(8,128)(2,1)S(1)} %get-tuple-element.13.refs_2_), channel_id=1, source_target_pairs={{0,4},{4,8},{8,12},{12,16},{16,20},{20,24},{24,28},{28,32},{32,36}... | collective-permute-start | bytes 552968 | tf_op jit(solution)/shard_map/ppermute | solution.py:162
  34.6 15.3 %collective-permute-start = (bf16[144,640]{1,0:T(8,128)(2,1)S(1)}, bf16[144,640]{1,0:T(8,128)(2,1)S(1)}, u32[]{:S(2)}, u32[]{:S(2)}) collective-permute-start(bf16[144,640]{1,0:T(8,128)(2,1)S(1)} %get-tuple-element.13.refs_2_), channel_id=1, source_target_pairs={{0,8},{4,12},{8,16},{12,20},{16,24},{20,28},{24,32},{28,36},{32,40... | collective-permute-start | bytes 552968 | tf_op jit(solution)/shard_map/ppermute | solution.py:162
  49.9 41.0 %copy-start.6 = (bf16[1280,320]{0,1:T(8,128)(2,1)S(1)}, bf16[1280,320]{0,1:T(8,128)(2,1)}, u32[]{:S(2)}) copy-start(bf16[1280,320]{0,1:T(8,128)(2,1)} %param.12) | copy-start | bytes 2457604
  55.1 35.9 %copy-start.2 = (bf16[1280,320]{0,1:T(8,128)(2,1)S(1)}, bf16[1280,320]{0,1:T(8,128)(2,1)}, u32[]{:S(2)}) copy-start(bf16[1280,320]{0,1:T(8,128)(2,1)} %param.10) | copy-start | bytes 2457604
  55.1 35.9 %copy-start.4 = (bf16[1280,320]{0,1:T(8,128)(2,1)S(1)}, bf16[1280,320]{0,1:T(8,128)(2,1)}, u32[]{:S(2)}) copy-start(bf16[1280,320]{0,1:T(8,128)(2,1)} %param.11) | copy-start | bytes 2457604
  55.5 0.8 copy-start.7
  56.3 15.3 %copy-start.17 = (bf16[144,640]{1,0:T(8,128)(2,1)S(1)}, bf16[144,640]{1,0:T(8,128)(2,1)}, u32[]{:S(2)}) copy-start(bf16[144,640]{1,0:T(8,128)(2,1)} %copy-done.16) | copy-start | bytes 552964
  56.3 18.7 %copy-start.15 = (bf16[144,640]{1,0:T(8,128)(2,1)S(1)}, bf16[144,640]{1,0:T(8,128)(2,1)}, u32[]{:S(2)}) copy-start(bf16[144,640]{1,0:T(8,128)(2,1)} %copy-done.14) | copy-start | bytes 552964
  56.3 36.5 %all-to-all-start = ((bf16[4,36,1280]{2,1,0:T(8,128)(2,1)}), bf16[4,36,1280]{2,1,0:T(8,128)(2,1)S(1)}, u32[]{:S(2)}, u32[]{:S(2)}) async-start(bf16[4,36,1280]{2,1,0:T(8,128)(2,1)} %copy-done.7), calls=%async_computation | async-start | bytes 819200 | tf_op jit(solution)/shard_map/all_to_all | solution.py:166
  67.7 12.7 %collective-permute-start.4 = (bf16[144,640]{1,0:T(8,128)(2,1)}, bf16[144,640]{1,0:T(8,128)(2,1)S(1)}, u32[]{:S(2)}, u32[]{:S(2)}) collective-permute-start(bf16[144,640]{1,0:T(8,128)(2,1)} %copy-done.19), channel_id=1, source_target_pairs={{8,0},{12,4},{16,8},{20,12},{24,16},{28,20},{32,24},{36,28},{40,32... | collective-permute-start | bytes 552968 | tf_op jit(solution)/shard_map/ppermute | solution.py:162
  69.6 11.8 %collective-permute-start.5 = (bf16[144,640]{1,0:T(8,128)(2,1)}, bf16[144,640]{1,0:T(8,128)(2,1)S(1)}, u32[]{:S(2)}, u32[]{:S(2)}) collective-permute-start(bf16[144,640]{1,0:T(8,128)(2,1)} %copy-done.18), channel_id=1, source_target_pairs={{4,0},{8,4},{12,8},{16,12},{20,16},{24,20},{28,24},{32,28},{36,32}... | collective-permute-start | bytes 552968 | tf_op jit(solution)/shard_map/ppermute | solution.py:162
  71.6 10.5 %collective-permute-start.6 = (bf16[144,640]{1,0:T(8,128)(2,1)S(1)}, bf16[144,640]{1,0:T(8,128)(2,1)S(1)}, u32[]{:S(2)}, u32[]{:S(2)}) collective-permute-start(bf16[144,640]{1,0:T(8,128)(2,1)S(1)} %copy-done.17), channel_id=1, source_target_pairs={{0,4},{4,8},{8,12},{12,16},{16,20},{20,24},{24,28},{28,32},{32,36}... | collective-permute-start | bytes 552968 | tf_op jit(solution)/shard_map/ppermute | solution.py:162
  75.0 16.0 %collective-permute-start.7 = (bf16[144,640]{1,0:T(8,128)(2,1)S(1)}, bf16[144,640]{1,0:T(8,128)(2,1)S(1)}, u32[]{:S(2)}, u32[]{:S(2)}) collective-permute-start(bf16[144,640]{1,0:T(8,128)(2,1)S(1)} %copy-done.15), channel_id=1, source_target_pairs={{0,8},{4,12},{8,16},{12,20},{16,24},{20,28},{24,32},{28,36},{32,40... | collective-permute-start | bytes 552968 | tf_op jit(solution)/shard_map/ppermute | solution.py:162
  91.0 1.0 copy-start.13
  92.8 17.3 %copy-start.9 = (bf16[1,1,36,1280]{3,2,1,0:T(8,128)(2,1)S(1)}, bf16[1,1,36,1280]{3,2,1,0:T(8,128)(2,1)}, u32[]{:S(2)}) copy-start(bf16[1,1,36,1280]{3,2,1,0:T(8,128)(2,1)} %param.7) | copy-start | bytes 276484
  92.8 17.3 %copy-start.11 = (bf16[1,1,36,1280]{3,2,1,0:T(8,128)(2,1)S(1)}, bf16[1,1,36,1280]{3,2,1,0:T(8,128)(2,1)}, u32[]{:S(2)}) copy-start(bf16[1,1,36,1280]{3,2,1,0:T(8,128)(2,1)} %param.8) | copy-start | bytes 276484
  (5 other events, 3.5 us)

commit v2 on v1

v2 whole, which is shorter than its diff:
```python
import functools

import jax
import jax.numpy as jnp
from jax import lax
from jax.experimental import pallas as pl
from jax.experimental.pallas import tpu as pltpu
from jax.sharding import Mesh
from jax.sharding import PartitionSpec as P

HEAD_DIM = 64
EPSILON = 1e-05
NEG_FILL = -1e30
ORDERED = (-2, -1, 0, 1, 2)
PAIR = 2
SHARDS = 4
BF16 = jnp.bfloat16
F32 = jnp.float32

VMEM = pl.BlockSpec(memory_space=pltpu.VMEM)
SMEM = pl.BlockSpec(memory_space=pltpu.SMEM)
PARAMS = pltpu.CompilerParams(vmem_limit_bytes=12 * 1024 * 1024)


def dot(a, b):
    return lax.dot_general(a, b, (((1,), (0,)), ((), ())), preferred_element_type=F32)


def dot_t(a, b):
    return lax.dot_general(a, b, (((1,), (1,)), ((), ())), preferred_element_type=F32)


def normalized(x):
    center = jnp.mean(x, axis=-1, keepdims=True)
    shifted = x - center
    spread = jnp.mean(jnp.square(shifted), axis=-1, keepdims=True)
    inverse = lax.rsqrt(spread + EPSILON)
    return shifted * inverse, inverse


def norm_kernel(x_ref, cot_ref, gain_ref, out_ref):
    half = x_ref.shape[0] // PAIR
    normed, _ = normalized(x_ref[...].astype(F32))
    hidden = normed * gain_ref[...].astype(F32)
    cot = cot_ref[...].astype(F32)
    for h in range(PAIR):
        rows = slice(h * half, (h + 1) * half)
        out_ref[h] = jnp.concatenate([hidden[rows], cot[rows]], axis=0).astype(BF16)


def gathered(g_ref, rows_ref, which):
    half = g_ref.shape[2] // 2
    for frame in range(PAIR):
        for s in range(SHARDS):
            start = (frame * SHARDS + s) * half
            rows_ref[start : start + half, :] = g_ref[
                s, frame, which * half : (which + 1) * half
            ].astype(F32)
    return rows_ref[...].astype(BF16)


def key_value_kernel(g_ref, wk_ref, wv_ref, b_ref, rows_ref):
    hidden = gathered(g_ref, rows_ref, 0)
    keys = dot_t(hidden, wk_ref[...])
    vals = dot_t(hidden, wv_ref[...])
    b_ref[...] = jnp.concatenate([keys, vals], axis=1).astype(BF16)


def query_kernel(g_ref, wq_ref, wo_ref, a_ref, rows_ref):
    queries = dot_t(gathered(g_ref, rows_ref, 0), wq_ref[...])
    out_grads = dot_t(gathered(g_ref, rows_ref, 1), wo_ref[...])
    a_ref[...] = jnp.concatenate([queries, out_grads], axis=1).astype(BF16)


def head_lanes(width):
    lane = lax.broadcasted_iota(jnp.int32, (width, 256), 0) // HEAD_DIM
    col = lax.broadcasted_iota(jnp.int32, (width, 256), 1)
    heads = width // HEAD_DIM // 2
    want = jnp.where(lane < heads, lane, lane - heads + 128)
    return (col == want).astype(BF16)


def attend_kernel(
    frames, pair_ref, a_ref, b_ref, even_ref, odd_ref, even_out, odd_out, own_ref, mixed_ref, near_ref, grads_ref
):
    pair = pair_ref[0]
    is_even = pair % 2 == 0
    rows, width = a_ref.shape
    one = rows // PAIR
    from_even = even_ref[...].astype(F32)
    from_odd = odd_ref[...].astype(F32)
    near_ref[0:rows] = jnp.where(is_even, from_odd, from_even)
    near_ref[rows : 2 * rows] = b_ref[...].astype(F32)
    near_ref[2 * rows : 3 * rows] = jnp.where(is_even, from_even, from_odd)
    a = a_ref[...].astype(F32)
    reduce_mat = head_lanes(width)
    frame = pair * PAIR + lax.broadcasted_iota(jnp.int32, (rows, 128), 0) // one
    scores, prob_grads = [], []
    for offset in ORDERED:
        start = (offset + 2) * one
        product = a * near_ref[start : start + rows]
        high = product.astype(BF16)
        low = (product - high.astype(F32)).astype(BF16)
        sums = dot(high, reduce_mat) + dot(low, reduce_mat)
        present = (frame + offset >= 0) & (frame + offset < frames)
        scores.append(jnp.where(present, sums[:, :128] * (HEAD_DIM**-0.5), NEG_FILL))
        prob_grads.append(sums[:, 128:])
    row_max = functools.reduce(jnp.maximum, scores)
    exponent = [jnp.exp(s - row_max) for s in scores]
    denominator = sum(exponent)
    attention = [e / denominator for e in exponent]
    row_delta = sum(p * g for p, g in zip(attention, prob_grads))
    mixed = jnp.zeros_like(a)
    scale = jnp.where(lax.broadcasted_iota(jnp.int32, a.shape, 1) < width // 2, HEAD_DIM**-0.5, 1.0)
    scaled_a = a * scale
    grads_ref[...] = jnp.zeros_like(grads_ref)
    for offset, p, g in zip(ORDERED, attention, prob_grads):
        start = (offset + 2) * one
        score_grads = (p * (g - row_delta)).astype(BF16)
        small = jnp.concatenate([score_grads, p.astype(BF16)], axis=1)
        weights = dot_t(small, reduce_mat)
        mixed = mixed + weights * near_ref[start : start + rows]
        grads_ref[start : start + rows] += weights * scaled_a
    mixed_ref[...] = (mixed * scale).astype(BF16)
    before = grads_ref[0:rows]
    after = grads_ref[2 * rows : 3 * rows]
    even_out[...] = jnp.where(is_even, after, before).astype(BF16)
    odd_out[...] = jnp.where(is_even, before, after).astype(BF16)
    own_ref[...] = grads_ref[rows : 2 * rows]


def back_kernel(mixed_ref, own_ref, even_ref, odd_ref, wq_ref, wk_ref, wv_ref, wo_ref, parts_ref, rows_ref):
    width = mixed_ref.shape[1] // 2
    half = parts_ref.shape[1] // 2
    total = own_ref[...] + even_ref[...].astype(F32) + odd_ref[...].astype(F32)
    total = total.astype(BF16)
    rows_ref[0] = dot(mixed_ref[:, width:], wo_ref[...])
    rows_ref[1] = (
        dot(mixed_ref[:, :width], wq_ref[...])
        + dot(total[:, :width], wk_ref[...])
        + dot(total[:, width:], wv_ref[...])
    )
    for part in range(PAIR * SHARDS):
        rows = slice(part * half, (part + 1) * half)
        parts_ref[part] = jnp.concatenate([rows_ref[0, rows], rows_ref[1, rows]], axis=0).astype(BF16)


def finish_kernel(x_ref, cot_ref, gain_ref, parts_ref, block_ref, grads_ref):
    half = parts_ref.shape[1] // 2
    summed = [
        sum(parts_ref[h * SHARDS + s].astype(F32) for s in range(SHARDS)) for h in range(PAIR)
    ]
    out = jnp.concatenate([part[:half] for part in summed], axis=0)
    hidden_grads = jnp.concatenate([part[half:] for part in summed], axis=0)
    x = x_ref[...].astype(F32)
    block_ref[...] = (x + out).astype(BF16)
    normed, inverse = normalized(x)
    scaled = hidden_grads * gain_ref[...].astype(F32)
    layer_grads = inverse * (
        scaled
        - jnp.mean(scaled, axis=-1, keepdims=True)
        - normed * jnp.mean(scaled * normed, axis=-1, keepdims=True)
    )
    grads_ref[...] = (cot_ref[...].astype(F32) + layer_grads).astype(BF16)


def call(kernel, out_shape, in_specs, scratch=(), flops=0, bytes_accessed=0):
    return pl.pallas_call(
        kernel,
        out_shape=out_shape,
        in_specs=in_specs,
        out_specs=jax.tree.map(lambda _: VMEM, out_shape),
        scratch_shapes=list(scratch),
        compiler_params=PARAMS,
        cost_estimate=pl.CostEstimate(flops=flops, bytes_accessed=bytes_accessed, transcendentals=0),
    )


def exchanged(block, first):
    count = lax.axis_size("pair")
    route = []
    for i in range(first, count - 1, 2):
        route += [(i, i + 1), (i + 1, i)]
    return lax.ppermute(block, "pair", route)


def per_device(inputs, cotangent, norm_gain, query_weight, key_weight, value_weight, output_weight):
    pair = lax.axis_index("pair").astype(jnp.int32).reshape(1)
    frames = lax.axis_size("pair") * PAIR
    piece, channels = inputs.shape[2:]
    rows, local = piece * SHARDS, query_weight.shape[1]
    x = inputs.reshape(piece, channels)
    cot = cotangent.reshape(piece, channels)
    gain = norm_gain.reshape(1, channels)
    wq, wk, wv, wo = query_weight.T, key_weight.T, value_weight.T, output_weight
    shape = jax.ShapeDtypeStruct
    wide = shape((rows, 2 * local), BF16)
    row_scratch = pltpu.VMEM((rows, channels), F32)
    near_scratch = pltpu.VMEM((3 * rows, 2 * local), F32)

    halves = call(norm_kernel, shape((PAIR, piece, channels), BF16), [VMEM] * 3)(x, cot, gain)
    halves = lax.all_to_all(halves, "half", 0, 0)
    every = lax.all_gather(halves, "space", axis=0)
    b = call(key_value_kernel, wide, [VMEM] * 3, [row_scratch])(every, wk, wv)
    near = [exchanged(b, first) for first in (0, 1)]
    a = call(query_kernel, wide, [VMEM] * 3, [row_scratch])(every, wq, wo)
    *sends, own, mixed = call(
        functools.partial(attend_kernel, frames),
        (wide, wide, shape((rows, 2 * local), F32), wide),
        [SMEM] + [VMEM] * 4,
        [near_scratch, near_scratch],
    )(pair, a, b, *near)
    arrived = [exchanged(send, first) for first, send in zip((0, 1), sends)]
    parts = call(
        back_kernel,
        shape((PAIR * SHARDS, piece, channels), BF16),
        [VMEM] * 8,
        [pltpu.VMEM((2, rows, channels), F32)],
    )(mixed, own, *arrived, wq, wk, wv, wo)
    parts = lax.all_to_all(parts, ("half", "space"), 0, 0)
    block, grads = call(
        finish_kernel, (shape((piece, channels), BF16), shape((piece, channels), BF16)), [VMEM] * 4
    )(x, cot, gain, parts)
    return block.reshape(inputs.shape), grads.reshape(inputs.shape)


def solution(mesh):
    devices = mesh.devices.reshape(-1, PAIR, SHARDS)
    mesh = Mesh(devices, ("pair", "half", "space"))
    frames = ("pair", "half")
    placed = (
        P(frames, None, "space", None),
        P(frames, None, "space", None),
        P(),
        P(None, "space"),
        P(None, "space"),
        P(None, "space"),
        P("space", None),
    )
    return jax.shard_map(
        per_device,
        mesh=mesh,
        in_specs=placed,
        out_specs=(P(frames, None, "space", None), P(frames, None, "space", None)),
        check_vma=False,
    )
```

time: 112 us -> 88.8 us (0.79)
  the two profiles are of different devices: /device:TPU:81 before, /device:TPU:57 now
where the time goes in v2:
time: 88.8 us; the launch traced here: 88.4 us
  blocking collectives  32.7 us (37%)
  waiting for transfers between devices  24 us (27%)
  starting transfers between devices  21.8 us (25%)
  Pallas kernels  6.6 us (7%)
  local copies, waits for them, and re-layouts  2.52 us (3%)
    ppermute x4, waiting for transfers between devices, exchanged(): return lax.ppermute(block, 'pair', route)  24 us
    ppermute x4, starting transfers between devices, exchanged(): return lax.ppermute(block, 'pair', route)  21.8 us
    all_to_all x1, blocking collectives, per_device(): parts = lax.all_to_all(parts, ('half', 'space'), 0, 0)  15.2 us
    all_gather x1, blocking collectives, per_device(): every = lax.all_gather(halves, 'space', axis=0)  10.6 us
    all_to_all x1, blocking collectives, per_device(): halves = lax.all_to_all(halves, 'half', 0, 0)  7.01 us
    pallas_call x1, Pallas kernels, per_device(): call(functools.partial(attend_kernel, frames), (wide, wide, shape((rows,...  2.74 us
    unnamed x18, local copies, waits for them, and re-layouts  1.82 us
  transfers between devices with their start and end apart: 4, of which 4 were waited for; matrix products, arithmetic and copies ran while one was open for 0% of the time, Pallas kernels for 1%

profile of v2, /device:TPU:57, one launch (start us, length us, event | category | flops | bytes accessed | tf_op | source)
XLA Modules:
  0.0 88.4 jit_solution(8548648630456210920)
XLA Ops:
  0.6 0.7 reshape.24.gain_ref
  1.3 0.9 %copy-done.5 = bf16[1,1,36,1280]{3,2,1,0:T(8,128)(2,1)S(1)} copy-done((bf16[1,1,36,1280]{3,2,1,0:T(8,128)(2,1)S(1)}, bf16[1,1,36,1280]{3,2,1,0:T(8,128)(2,1)}, u32[]{:S(2)}) %copy-start.5) | copy-done | bytes 92184
  2.2 0.9 %copy-done.7 = bf16[1,1,36,1280]{3,2,1,0:T(8,128)(2,1)S(1)} copy-done((bf16[1,1,36,1280]{3,2,1,0:T(8,128)(2,1)S(1)}, bf16[1,1,36,1280]{3,2,1,0:T(8,128)(2,1)}, u32[]{:S(2)}) %copy-start.7) | copy-done | bytes 92184
  3.1 0.2 shard_map.86
  3.3 0.0 copy-start.2
  3.3 7.0 %all_to_all.10 = bf16[2,36,1280]{2,1,0:T(8,128)(2,1)S(1)} all-to-all(bf16[2,36,1280]{2,1,0:T(8,128)(2,1)S(1)} %shard_map.86), channel_id=1, replica_groups=mesh['pair'=64,'half'=2,'space'=4] {'half'}, dimensions={0} | all-to-all | bytes 368640 | tf_op jit(solution)/shard_map/all_to_all | solution.py:202
  10.4 10.6 %all-gather = bf16[8,36,1280]{2,1,0:T(8,128)(2,1)S(1)} all-gather(bf16[2,36,1280]{2,1,0:T(8,128)(2,1)S(1)} %all_to_all.10), channel_id=2, replica_groups=mesh['pair'=64,'half'=2,'space'=4] {'space'}, dimensions={0}, use_global_device_ids=true | all-gather | bytes 921600 | tf_op jit(solution)/shard_map/all_gather | solution.py:203
  20.9 0.8 shard_map.88.b_ref
  21.7 13.5 %collective-permute-start.1 = (bf16[144,640]{1,0:T(8,128)(2,1)S(1)}, bf16[144,640]{1,0:T(8,128)(2,1)}, u32[]{:S(2)}, u32[]{:S(2)}) collective-permute-start(bf16[144,640]{1,0:T(8,128)(2,1)S(1)} %shard_map.88.b_ref), channel_id=1, source_target_pairs={{8,16},{16,8},{24,32},{32,24},{40,48},{48,40},{56,64},{64,56},{72,... | collective-permute-start | bytes 552968 | tf_op jit(solution)/shard_map/ppermute | solution.py:184
  35.2 1.9 %collective-permute-start = (bf16[144,640]{1,0:T(8,128)(2,1)S(1)}, bf16[144,640]{1,0:T(8,128)(2,1)}, u32[]{:S(2)}, u32[]{:S(2)}) collective-permute-start(bf16[144,640]{1,0:T(8,128)(2,1)S(1)} %shard_map.88.b_ref), channel_id=1, source_target_pairs={{0,8},{8,0},{16,24},{24,16},{32,40},{40,32},{48,56},{56,48},{64,72... | collective-permute-start | bytes 552968 | tf_op jit(solution)/shard_map/ppermute | solution.py:184
  37.2 0.0 copy-start.4
  37.2 0.8 shard_map.87.a_ref
  38.0 6.2 %collective-permute-done.1.odd_ref = bf16[144,640]{1,0:T(8,128)(2,1)} collective-permute-done((bf16[144,640]{1,0:T(8,128)(2,1)S(1)}, bf16[144,640]{1,0:T(8,128)(2,1)}, u32[]{:S(2)}, u32[]{:S(2)}) %collective-permute-start.1) | collective-permute-done | bytes 184352 | tf_op jit(solution)/shard_map/ppermute | solution.py:184
  44.3 3.9 %collective-permute-done.even_ref = bf16[144,640]{1,0:T(8,128)(2,1)} collective-permute-done((bf16[144,640]{1,0:T(8,128)(2,1)S(1)}, bf16[144,640]{1,0:T(8,128)(2,1)}, u32[]{:S(2)}, u32[]{:S(2)}) %collective-permute-start) | collective-permute-done | bytes 184352 | tf_op jit(solution)/shard_map/ppermute | solution.py:184
  48.2 2.7 %shard_map.89 = (bf16[144,640]{1,0:T(8,128)(2,1)S(1)}, bf16[144,640]{1,0:T(8,128)(2,1)S(1)}, f32[144,640]{1,0:T(8,128)S(1)}, bf16[144,640]{1,0:T(8,128)(2,1)S(1)}) custom-call(s32[1]{0:T(128)} %bitcast.2.pair_ref, bf16[144,640]{1,0:T(8,128)(2,1)S(1)} %shard_map.87.a_ref, bf16[144,640]{1,0:T(8,128)(2,1)S(1)} %shard_map.88.b_ref, ...), custom_call_target="tpu_custom_call" | custom-call | tf_op jit(solution)/shard_map/pallas_call | solution.py:207
  50.9 1.9 %collective-permute-start.2 = (bf16[144,640]{1,0:T(8,128)(2,1)S(1)}, bf16[144,640]{1,0:T(8,128)(2,1)S(1)}, u32[]{:S(2)}, u32[]{:S(2)}) collective-permute-start(bf16[144,640]{1,0:T(8,128)(2,1)S(1)} %get-tuple-element.10), channel_id=1, source_target_pairs={{0,8},{8,0},{16,24},{24,16},{32,40},{40,32},{48,56},{56,48},{64,72... | collective-permute-start | bytes 552968 | tf_op jit(solution)/shard_map/ppermute | solution.py:184
  52.8 4.4 %collective-permute-start.3 = (bf16[144,640]{1,0:T(8,128)(2,1)S(1)}, bf16[144,640]{1,0:T(8,128)(2,1)S(1)}, u32[]{:S(2)}, u32[]{:S(2)}) collective-permute-start(bf16[144,640]{1,0:T(8,128)(2,1)S(1)} %get-tuple-element.11), channel_id=1, source_target_pairs={{8,16},{16,8},{24,32},{32,24},{40,48},{48,40},{56,64},{64,56},{72,... | collective-permute-start | bytes 552968 | tf_op jit(solution)/shard_map/ppermute | solution.py:184
  57.3 4.1 %collective-permute-done.2.even_ref = bf16[144,640]{1,0:T(8,128)(2,1)S(1)} collective-permute-done((bf16[144,640]{1,0:T(8,128)(2,1)S(1)}, bf16[144,640]{1,0:T(8,128)(2,1)S(1)}, u32[]{:S(2)}, u32[]{:S(2)}) %collective-permute-start.2) | collective-permute-done | bytes 184352 | tf_op jit(solution)/shard_map/ppermute | solution.py:184
  61.4 9.7 %collective-permute-done.3.odd_ref = bf16[144,640]{1,0:T(8,128)(2,1)S(1)} collective-permute-done((bf16[144,640]{1,0:T(8,128)(2,1)S(1)}, bf16[144,640]{1,0:T(8,128)(2,1)S(1)}, u32[]{:S(2)}, u32[]{:S(2)}) %collective-permute-start.3) | collective-permute-done | bytes 184352 | tf_op jit(solution)/shard_map/ppermute | solution.py:184
  71.1 1.1 %shard_map.90 = bf16[8,36,1280]{2,1,0:T(8,128)(2,1)S(1)} custom-call(bf16[144,640]{1,0:T(8,128)(2,1)S(1)} %get-tuple-element.8.mixed_ref, f32[144,640]{1,0:T(8,128)S(1)} %get-tuple-element.9.own_ref, bf16[144,640]{1,0:T(8,128)(2,1)S(1)} %collective-permute-done.2.even_ref, bf16[144,640]{1,0:T(8,128)(2,1)S(1)} %collective-permute-done.3.odd_ref, ...), custom_call_target="tpu_custom_call" | custom-call | tf_op jit(solution)/shard_map/pallas_call | solution.py:214
  72.2 0.0 copy-start.6
  72.2 0.0 copy-start.8
  72.2 15.2 %all_to_all.11.parts_ref = bf16[8,36,1280]{2,1,0:T(8,128)(2,1)S(1)} all-to-all(bf16[8,36,1280]{2,1,0:T(8,128)(2,1)S(1)} %shard_map.90), channel_id=1, replica_groups=mesh['pair'=64,'half'=2,'space'=4] {'half','space'}, dimensions={0} | all-to-all | bytes 1474560 | tf_op jit(solution)/shard_map/all_to_all | solution.py:220
  87.4 1.0 %shard_map.91 = (bf16[36,1280]{1,0:T(8,128)(2,1)}, bf16[36,1280]{1,0:T(8,128)(2,1)}) custom-call(bf16[36,1280]{1,0:T(8,128)(2,1)S(1)} %bitcast.18, bf16[36,1280]{1,0:T(8,128)(2,1)S(1)} %bitcast.20, bf16[1,1280]{1,0:T(2,128)(2,1)S(1)} %reshape.24.gain_ref, bf16[8,36,1280]{2,1,0:T(8,128)(2,1)S(1)} %all_to_all.11.parts_ref), custom_call_target="tpu_custom_call" | custom-call | tf_op jit(solution)/shard_map/pallas_call | solution.py:221
  (12 shorter events, 0.0 us)
Async XLA Ops:
  1.3 0.9 %copy-start.5 = (bf16[1,1,36,1280]{3,2,1,0:T(8,128)(2,1)S(1)}, bf16[1,1,36,1280]{3,2,1,0:T(8,128)(2,1)}, u32[]{:S(2)}) copy-start(bf16[1,1,36,1280]{3,2,1,0:T(8,128)(2,1)} %param.7) | copy-start | bytes 276484
  2.2 0.9 %copy-start.7 = (bf16[1,1,36,1280]{3,2,1,0:T(8,128)(2,1)S(1)}, bf16[1,1,36,1280]{3,2,1,0:T(8,128)(2,1)}, u32[]{:S(2)}) copy-start(bf16[1,1,36,1280]{3,2,1,0:T(8,128)(2,1)} %param.8) | copy-start | bytes 276484
  3.1 17.8 %copy-start.3 = (bf16[1280,320]{0,1:T(8,128)(2,1)S(1)}, bf16[1280,320]{0,1:T(8,128)(2,1)}, u32[]{:S(2)}) copy-start(bf16[1280,320]{0,1:T(8,128)(2,1)} %param.12) | copy-start | bytes 2457604
  3.3 17.6 %copy-start.2 = (bf16[1280,320]{0,1:T(8,128)(2,1)S(1)}, bf16[1280,320]{0,1:T(8,128)(2,1)}, u32[]{:S(2)}) copy-start(bf16[1280,320]{0,1:T(8,128)(2,1)} %param.11) | copy-start | bytes 2457604
  20.9 16.2 %copy-start = (bf16[1280,320]{0,1:T(8,128)(2,1)S(1)}, bf16[1280,320]{0,1:T(8,128)(2,1)}, u32[]{:S(2)}) copy-start(bf16[1280,320]{0,1:T(8,128)(2,1)} %param.10) | copy-start | bytes 2457604
  20.9 16.3 %copy-start.1 = (bf16[320,1280]{1,0:T(8,128)(2,1)S(1)}, bf16[320,1280]{1,0:T(8,128)(2,1)}, u32[]{:S(2)}) copy-start(bf16[320,1280]{1,0:T(8,128)(2,1)} %wo_ref.3) | copy-start | bytes 2457604
  21.7 22.6 %collective-permute-start.1 = (bf16[144,640]{1,0:T(8,128)(2,1)S(1)}, bf16[144,640]{1,0:T(8,128)(2,1)}, u32[]{:S(2)}, u32[]{:S(2)}) collective-permute-start(bf16[144,640]{1,0:T(8,128)(2,1)S(1)} %shard_map.88.b_ref), channel_id=1, source_target_pairs={{8,16},{16,8},{24,32},{32,24},{40,48},{48,40},{56,64},{64,56},{72,... | collective-permute-start | bytes 552968 | tf_op jit(solution)/shard_map/ppermute | solution.py:184
  35.2 12.9 %collective-permute-start = (bf16[144,640]{1,0:T(8,128)(2,1)S(1)}, bf16[144,640]{1,0:T(8,128)(2,1)}, u32[]{:S(2)}, u32[]{:S(2)}) collective-permute-start(bf16[144,640]{1,0:T(8,128)(2,1)S(1)} %shard_map.88.b_ref), channel_id=1, source_target_pairs={{0,8},{8,0},{16,24},{24,16},{32,40},{40,32},{48,56},{56,48},{64,72... | collective-permute-start | bytes 552968 | tf_op jit(solution)/shard_map/ppermute | solution.py:184
  37.2 34.0 %copy-start.4 = (bf16[1280,320]{0,1:T(8,128)(2,1)S(1)}, bf16[1280,320]{0,1:T(8,128)(2,1)}, u32[]{:S(2)}) copy-start(bf16[1280,320]{0,1:T(8,128)(2,1)} %param.12) | copy-start | bytes 2457604
  50.9 10.5 %collective-permute-start.2 = (bf16[144,640]{1,0:T(8,128)(2,1)S(1)}, bf16[144,640]{1,0:T(8,128)(2,1)S(1)}, u32[]{:S(2)}, u32[]{:S(2)}) collective-permute-start(bf16[144,640]{1,0:T(8,128)(2,1)S(1)} %get-tuple-element.10), channel_id=1, source_target_pairs={{0,8},{8,0},{16,24},{24,16},{32,40},{40,32},{48,56},{56,48},{64,72... | collective-permute-start | bytes 552968 | tf_op jit(solution)/shard_map/ppermute | solution.py:184
  52.8 18.3 %collective-permute-start.3 = (bf16[144,640]{1,0:T(8,128)(2,1)S(1)}, bf16[144,640]{1,0:T(8,128)(2,1)S(1)}, u32[]{:S(2)}, u32[]{:S(2)}) collective-permute-start(bf16[144,640]{1,0:T(8,128)(2,1)S(1)} %get-tuple-element.11), channel_id=1, source_target_pairs={{8,16},{16,8},{24,32},{32,24},{40,48},{48,40},{56,64},{64,56},{72,... | collective-permute-start | bytes 552968 | tf_op jit(solution)/shard_map/ppermute | solution.py:184
  72.2 15.2 %copy-start.6 = (bf16[1,1,36,1280]{3,2,1,0:T(8,128)(2,1)S(1)}, bf16[1,1,36,1280]{3,2,1,0:T(8,128)(2,1)}, u32[]{:S(2)}) copy-start(bf16[1,1,36,1280]{3,2,1,0:T(8,128)(2,1)} %param.7) | copy-start | bytes 276484
  72.2 15.2 %copy-start.8 = (bf16[1,1,36,1280]{3,2,1,0:T(8,128)(2,1)S(1)}, bf16[1,1,36,1280]{3,2,1,0:T(8,128)(2,1)}, u32[]{:S(2)}) copy-start(bf16[1,1,36,1280]{3,2,1,0:T(8,128)(2,1)} %param.8) | copy-start | bytes 276484

commit v3 on v2

--- a/solution.py
+++ b/solution.py
@@ -9,6 +9,7 @@
 from jax.sharding import PartitionSpec as P
 
 HEAD_DIM = 64
+HEAD_SHIFT = 6
 EPSILON = 1e-05
 NEG_FILL = -1e30
 ORDERED = (-2, -1, 0, 1, 2)
@@ -38,63 +39,91 @@
     return shifted * inverse, inverse
 
 
-def norm_kernel(x_ref, cot_ref, gain_ref, out_ref):
+def norm_kernel(x_hbm, cot_hbm, gain_hbm, out_ref, x_ref, cot_ref, gain_ref, sems):
+    copies = [
+        pltpu.make_async_copy(source, target, sems.at[i])
+        for i, (source, target) in enumerate(
+            ((x_hbm, x_ref), (gain_hbm, gain_ref), (cot_hbm, cot_ref))
+        )
+    ]
+    for copy in copies:
+        copy.start()
     half = x_ref.shape[0] // PAIR
+    copies[0].wait()
     normed, _ = normalized(x_ref[...].astype(F32))
-    hidden = normed * gain_ref[...].astype(F32)
+    copies[1].wait()
+    hidden = normed * gain_ref[...].astype(F32).reshape(1, -1)
+    copies[2].wait()
     cot = cot_ref[...].astype(F32)
     for h in range(PAIR):
         rows = slice(h * half, (h + 1) * half)
         out_ref[h] = jnp.concatenate([hidden[rows], cot[rows]], axis=0).astype(BF16)
 
 
-def gathered(g_ref, rows_ref, which):
-    half = g_ref.shape[2] // 2
+def take_kernel(halves_ref, hidden_ref, cot_ref):
+    half = halves_ref.shape[1] // 2
+    both = [halves_ref[f].astype(F32) for f in range(PAIR)]
+    hidden_ref[...] = jnp.concatenate([v[:half] for v in both], axis=0).astype(BF16)
+    cot_ref[...] = jnp.concatenate([v[half:] for v in both], axis=0).astype(BF16)
+
+
+def gathered(g_ref, rows_ref):
+    half = g_ref.shape[1] // PAIR
     for frame in range(PAIR):
         for s in range(SHARDS):
             start = (frame * SHARDS + s) * half
-            rows_ref[start : start + half, :] = g_ref[
-                s, frame, which * half : (which + 1) * half
-            ].astype(F32)
+            rows_ref[start : start + half, :] = g_ref[s, frame * half : (frame + 1) * half].astype(F32)
     return rows_ref[...].astype(BF16)
 
 
 def key_value_kernel(g_ref, wk_ref, wv_ref, b_ref, rows_ref):
-    hidden = gathered(g_ref, rows_ref, 0)
+    hidden = gathered(g_ref, rows_ref)
     keys = dot_t(hidden, wk_ref[...])
     vals = dot_t(hidden, wv_ref[...])
     b_ref[...] = jnp.concatenate([keys, vals], axis=1).astype(BF16)
 
 
-def query_kernel(g_ref, wq_ref, wo_ref, a_ref, rows_ref):
-    queries = dot_t(gathered(g_ref, rows_ref, 0), wq_ref[...])
-    out_grads = dot_t(gathered(g_ref, rows_ref, 1), wo_ref[...])
+def query_kernel(hidden_ref, cot_ref, wq_ref, wo_ref, a_ref, rows_ref):
+    queries = dot_t(gathered(hidden_ref, rows_ref), wq_ref[...])
+    out_grads = dot_t(gathered(cot_ref, rows_ref), wo_ref[...])
     a_ref[...] = jnp.concatenate([queries, out_grads], axis=1).astype(BF16)
 
 
-def head_lanes(width):
-    lane = lax.broadcasted_iota(jnp.int32, (width, 256), 0) // HEAD_DIM
-    col = lax.broadcasted_iota(jnp.int32, (width, 256), 1)
-    heads = width // HEAD_DIM // 2
+def head_lanes(width, transposed=False):
+    shape = (256, width) if transposed else (width, 256)
+    lane = lax.broadcasted_iota(jnp.int32, shape, 1 if transposed else 0) >> HEAD_SHIFT
+    col = lax.broadcasted_iota(jnp.int32, shape, 0 if transposed else 1)
+    heads = (width >> HEAD_SHIFT) // 2
     want = jnp.where(lane < heads, lane, lane - heads + 128)
     return (col == want).astype(BF16)
 
 
-def attend_kernel(
-    frames, pair_ref, a_ref, b_ref, even_ref, odd_ref, even_out, odd_out, own_ref, mixed_ref, near_ref, grads_ref
-):
-    pair = pair_ref[0]
-    is_even = pair % 2 == 0
-    rows, width = a_ref.shape
-    one = rows // PAIR
+def build_near(pair_ref, b_ref, even_ref, odd_ref, near_ref):
+    rows = b_ref.shape[0]
+    is_even = pair_ref[0] % 2 == 0
     from_even = even_ref[...].astype(F32)
     from_odd = odd_ref[...].astype(F32)
     near_ref[0:rows] = jnp.where(is_even, from_odd, from_even)
     near_ref[rows : 2 * rows] = b_ref[...].astype(F32)
     near_ref[2 * rows : 3 * rows] = jnp.where(is_even, from_even, from_odd)
+
+
+def lane_scale(shape):
+    lane = lax.broadcasted_iota(jnp.int32, shape, 1)
+    return jnp.where(lane < shape[1] // 2, HEAD_DIM**-0.5, 1.0)
+
+
+def attend_kernel(
+    frames, pair_ref, a_ref, b_ref, even_ref, odd_ref, even_out, odd_out, own_ref, small_ref, near_ref
+):
+    pair = pair_ref[0]
+    rows, width = a_ref.shape
+    one = rows // PAIR
+    build_near(pair_ref, b_ref, even_ref, odd_ref, near_ref)
     a = a_ref[...].astype(F32)
     reduce_mat = head_lanes(width)
-    frame = pair * PAIR + lax.broadcasted_iota(jnp.int32, (rows, 128), 0) // one
+    later = lax.broadcasted_iota(jnp.int32, (rows, 128), 0) >= one
+    frame = pair * PAIR + later.astype(jnp.int32)
     scores, prob_grads = [], []
     for offset in ORDERED:
         start = (offset + 2) * one
@@ -110,39 +139,59 @@
     denominator = sum(exponent)
     attention = [e / denominator for e in exponent]
     row_delta = sum(p * g for p, g in zip(attention, prob_grads))
-    mixed = jnp.zeros_like(a)
-    scale = jnp.where(lax.broadcasted_iota(jnp.int32, a.shape, 1) < width // 2, HEAD_DIM**-0.5, 1.0)
-    scaled_a = a * scale
-    grads_ref[...] = jnp.zeros_like(grads_ref)
-    for offset, p, g in zip(ORDERED, attention, prob_grads):
-        start = (offset + 2) * one
+    scaled_a = a * lane_scale(a.shape)
+    spread_mat = head_lanes(width, transposed=True)
+    sent = []
+    for i, (p, g) in enumerate(zip(attention, prob_grads)):
         score_grads = (p * (g - row_delta)).astype(BF16)
         small = jnp.concatenate([score_grads, p.astype(BF16)], axis=1)
-        weights = dot_t(small, reduce_mat)
-        mixed = mixed + weights * near_ref[start : start + rows]
-        grads_ref[start : start + rows] += weights * scaled_a
-    mixed_ref[...] = (mixed * scale).astype(BF16)
-    before = grads_ref[0:rows]
-    after = grads_ref[2 * rows : 3 * rows]
+        small_ref[i] = small
+        sent.append(dot(small, spread_mat) * scaled_a)
+    segments = []
+    for i in range(len(ORDERED) + 1):
+        terms = []
+        if i < len(ORDERED):
+            terms.append(sent[i][:one])
+        if i > 0:
+            terms.append(sent[i - 1][one:])
+        segments.append(sum(terms))
+    before = jnp.concatenate(segments[0:2], axis=0)
+    after = jnp.concatenate(segments[4:6], axis=0)
+    is_even = pair % 2 == 0
     even_out[...] = jnp.where(is_even, after, before).astype(BF16)
     odd_out[...] = jnp.where(is_even, before, after).astype(BF16)
-    own_ref[...] = grads_ref[rows : 2 * rows]
-
-
-def back_kernel(mixed_ref, own_ref, even_ref, odd_ref, wq_ref, wk_ref, wv_ref, wo_ref, parts_ref, rows_ref):
-    width = mixed_ref.shape[1] // 2
+    own_ref[0:one] = segments[2]
+    own_ref[one:rows] = segments[3]
+
+
+def mix_kernel(
+    pair_ref, small_ref, b_ref, even_ref, odd_ref, wq_ref, wo_ref, out_ref, query_part_ref, near_ref
+):
+    build_near(pair_ref, b_ref, even_ref, odd_ref, near_ref)
+    rows, width = b_ref.shape
+    one, half = rows // PAIR, width // 2
+    reduce_mat = head_lanes(width)
+    mixed = jnp.zeros((rows, width), F32)
+    for i in range(len(ORDERED)):
+        mixed = mixed + dot_t(small_ref[i], reduce_mat) * near_ref[i * one : i * one + rows]
+    mixed = (mixed * lane_scale(mixed.shape)).astype(BF16)
+    query_part_ref[...] = dot(mixed[:, :half], wq_ref[...])
+    out_ref[...] = dot(mixed[:, half:], wo_ref[...])
+
+
+def back_kernel(out_ref, query_part_ref, own_ref, even_ref, odd_ref, wk_ref, wv_ref, parts_ref, rows_ref):
+    width = own_ref.shape[1] // 2
     half = parts_ref.shape[1] // 2
     total = own_ref[...] + even_ref[...].astype(F32) + odd_ref[...].astype(F32)
     total = total.astype(BF16)
-    rows_ref[0] = dot(mixed_ref[:, width:], wo_ref[...])
-    rows_ref[1] = (
-        dot(mixed_ref[:, :width], wq_ref[...])
+    rows_ref[...] = (
+        query_part_ref[...]
         + dot(total[:, :width], wk_ref[...])
         + dot(total[:, width:], wv_ref[...])
     )
     for part in range(PAIR * SHARDS):
         rows = slice(part * half, (part + 1) * half)
-        parts_ref[part] = jnp.concatenate([rows_ref[0, rows], rows_ref[1, rows]], axis=0).astype(BF16)
+        parts_ref[part] = jnp.concatenate([out_ref[rows], rows_ref[rows]], axis=0).astype(BF16)
 
 
 def finish_kernel(x_ref, cot_ref, gain_ref, parts_ref, block_ref, grads_ref):
@@ -155,7 +204,7 @@
     x = x_ref[...].astype(F32)
     block_ref[...] = (x + out).astype(BF16)
     normed, inverse = normalized(x)
-    scaled = hidden_grads * gain_ref[...].astype(F32)
+    scaled = hidden_grads * gain_ref[...].astype(F32).reshape(1, -1)
     layer_grads = inverse * (
         scaled
         - jnp.mean(scaled, axis=-1, keepdims=True)
@@ -191,32 +240,46 @@
     rows, local = piece * SHARDS, query_weight.shape[1]
     x = inputs.reshape(piece, channels)
     cot = cotangent.reshape(piece, channels)
-    gain = norm_gain.reshape(1, channels)
+    gain = norm_gain
     wq, wk, wv, wo = query_weight.T, key_weight.T, value_weight.T, output_weight
     shape = jax.ShapeDtypeStruct
     wide = shape((rows, 2 * local), BF16)
     row_scratch = pltpu.VMEM((rows, channels), F32)
     near_scratch = pltpu.VMEM((3 * rows, 2 * local), F32)
 
-    halves = call(norm_kernel, shape((PAIR, piece, channels), BF16), [VMEM] * 3)(x, cot, gain)
+    halves = call(
+        norm_kernel,
+        shape((PAIR, piece, channels), BF16),
+        [pl.BlockSpec(memory_space=pl.ANY)] * 3,
+        [
+            pltpu.VMEM((piece, channels), BF16),
+            pltpu.VMEM((piece, channels), BF16),
+            pltpu.VMEM((channels,), BF16),
+            pltpu.SemaphoreType.DMA((3,)),
+        ],
+    )(x, cot, gain)
     halves = lax.all_to_all(halves, "half", 0, 0)
-    every = lax.all_gather(halves, "space", axis=0)
-    b = call(key_value_kernel, wide, [VMEM] * 3, [row_scratch])(every, wk, wv)
+    own_rows = shape((piece, channels), BF16)
+    hidden, cot_rows = call(take_kernel, (own_rows, own_rows), [VMEM])(halves)
+    hidden = lax.all_gather(hidden, "space", axis=0)
+    b = call(key_value_kernel, wide, [VMEM] * 3, [row_scratch])(hidden, wk, wv)
     near = [exchanged(b, first) for first in (0, 1)]
-    a = call(query_kernel, wide, [VMEM] * 3, [row_scratch])(every, wq, wo)
-    *sends, own, mixed = call(
+    cot_rows = lax.all_gather(cot_rows, "space", axis=0)
+    a = call(query_kernel, wide, [VMEM] * 4, [row_scratch])(hidden, cot_rows, wq, wo)
+    *sends, own, small = call(
         functools.partial(attend_kernel, frames),
-        (wide, wide, shape((rows, 2 * local), F32), wide),
+        (wide, wide, shape((rows, 2 * local), F32), shape((len(ORDERED), rows, 256), BF16)),
         [SMEM] + [VMEM] * 4,
-        [near_scratch, near_scratch],
+        [near_scratch],
     )(pair, a, b, *near)
     arrived = [exchanged(send, first) for first, send in zip((0, 1), sends)]
-    parts = call(
-        back_kernel,
-        shape((PAIR * SHARDS, piece, channels), BF16),
-        [VMEM] * 8,
-        [pltpu.VMEM((2, rows, channels), F32)],
-    )(mixed, own, *arrived, wq, wk, wv, wo)
+    full = shape((rows, channels), F32)
+    out, query_part = call(mix_kernel, (full, full), [SMEM] + [VMEM] * 6, [near_scratch])(
+        pair, small, b, *near, wq, wo
+    )
+    parts = call(back_kernel, shape((PAIR * SHARDS, piece, channels), BF16), [VMEM] * 7, [row_scratch])(
+        out, query_part, own, *arrived, wk, wv
+    )
     parts = lax.all_to_all(parts, ("half", "space"), 0, 0)
     block, grads = call(
         finish_kernel, (shape((piece, channels), BF16), shape((piece, channels), BF16)), [VMEM] * 4

time: 88.8 us -> 86.7 us (0.976)
  waiting for transfers between devices: 24 us -> 14.6 us
  blocking collectives: 32.7 us -> 38.7 us
  local copies, waits for them, and re-layouts: 2.52 us -> 3.73 us
    ppermute x4, waiting for transfers between devices: 24 us -> 14.6 us  [exchanged(): return lax.ppermute(block, 'pair', route)]
    all_gather x1 -> x2, blocking collectives: 10.6 us -> 15 us  [the longest x1 8.35 us: per_device(): hidden = lax.all_gather(hidden, 'space', axis=0)]
    unnamed x18 -> x22, local copies, waits for them, and re-layouts: 1.82 us -> 3.73 us
    all_to_all x1, blocking collectives: 15.2 us -> 16.8 us  [per_device(): parts = lax.all_to_all(parts, ('half', 'space'), 0, 0)]
    pallas_call x3 -> x5, Pallas kernels: 1.78 us -> 3.27 us  [the longest x1 1.18 us: per_device(): call(mix_kernel, (full, full), [SMEM] + [VMEM] * 6, [near_scratch])]
    pallas_call x1, Pallas kernels: 2.74 us -> 1.57 us  [per_device(): call(functools.partial(attend_kernel, frames), (wide, wide, shape((rows,...]
  transfers between devices with their start and end apart: 4 -> 4, of which waited for: 4 -> 3; matrix products, arithmetic and copies ran while one was open for 0% -> 0% of each run, Pallas kernels for 1% -> 2%
where the time goes in v3:
time: 86.7 us; the launch traced here: 86 us
  blocking collectives  38.7 us (45%)
  starting transfers between devices  21.8 us (25%)
  waiting for transfers between devices  14.6 us (17%)
  Pallas kernels  6.44 us (7%)
  local copies, waits for them, and re-layouts  3.73 us (4%)
    ppermute x4, starting transfers between devices, exchanged(): return lax.ppermute(block, 'pair', route)  21.8 us
    all_to_all x1, blocking collectives, per_device(): parts = lax.all_to_all(parts, ('half', 'space'), 0, 0)  16.8 us
    ppermute x4, waiting for transfers between devices, exchanged(): return lax.ppermute(block, 'pair', route)  14.6 us
    all_gather x1, blocking collectives, per_device(): hidden = lax.all_gather(hidden, 'space', axis=0)  8.35 us
    all_to_all x1, blocking collectives, per_device(): halves = lax.all_to_all(halves, 'half', 0, 0)  6.88 us
    all_gather x1, blocking collectives, per_device(): cot_rows = lax.all_gather(cot_rows, 'space', axis=0)  6.67 us
    unnamed x22, local copies, waits for them, and re-layouts  3.73 us
  transfers between devices with their start and end apart: 4, of which 3 were waited for; matrix products, arithmetic and copies ran while one was open for 0% of the time, Pallas kernels for 2%

profile of v3, /device:TPU:57, one launch (start us, length us, event | category | flops | bytes accessed | tf_op | source)
XLA Modules:
  0.0 86.0 jit_solution(5809615201112922682)
XLA Ops:
  0.6 0.0 copy-start.5
  0.7 1.0 %copy-done.5 = bf16[1,1,36,1280]{3,2,1,0:T(8,128)(2,1)S(1)} copy-done((bf16[1,1,36,1280]{3,2,1,0:T(8,128)(2,1)S(1)}, bf16[1,1,36,1280]{3,2,1,0:T(8,128)(2,1)}, u32[]{:S(2)}) %copy-start.5) | copy-done | bytes 92184
  1.6 0.9 %copy-done.7 = bf16[1,1,36,1280]{3,2,1,0:T(8,128)(2,1)S(1)} copy-done((bf16[1,1,36,1280]{3,2,1,0:T(8,128)(2,1)S(1)}, bf16[1,1,36,1280]{3,2,1,0:T(8,128)(2,1)}, u32[]{:S(2)}) %copy-start.7) | copy-done | bytes 92184
  2.5 0.7 copy-done.9
  3.2 0.5 shard_map.86
  3.7 6.9 %all_to_all.10.halves_ref = bf16[2,36,1280]{2,1,0:T(8,128)(2,1)S(1)} all-to-all(bf16[2,36,1280]{2,1,0:T(8,128)(2,1)S(1)} %shard_map.86), channel_id=1, replica_groups=mesh['pair'=64,'half'=2,'space'=4] {'half'}, dimensions={0} | all-to-all | bytes 368640 | tf_op jit(solution)/shard_map/all_to_all | solution.py:261
  10.6 8.3 %all-gather.2.hidden_ref.g_ref = bf16[4,36,1280]{2,1,0:T(8,128)(2,1)S(1)} all-gather(bf16[1,36,1280]{2,1,0:T(8,128)(2,1)S(1)} %bitcast.21), channel_id=2, replica_groups=mesh['pair'=64,'half'=2,'space'=4] {'space'}, dimensions={0}, use_global_device_ids=true | all-gather | bytes 460800 | tf_op jit(solution)/shard_map/all_gather | solution.py:264
  19.0 1.1 %copy-done.1 = bf16[1280,320]{0,1:T(8,128)(2,1)S(1)} copy-done((bf16[1280,320]{0,1:T(8,128)(2,1)S(1)}, bf16[1280,320]{0,1:T(8,128)(2,1)}, u32[]{:S(2)}) %copy-start.1) | copy-done | bytes 819224
  20.1 0.8 shard_map.89.b_ref
  20.9 13.5 %collective-permute-start.1 = (bf16[144,640]{1,0:T(8,128)(2,1)S(1)}, bf16[144,640]{1,0:T(8,128)(2,1)S(1)}, u32[]{:S(2)}, u32[]{:S(2)}) collective-permute-start(bf16[144,640]{1,0:T(8,128)(2,1)S(1)} %shard_map.89.b_ref), channel_id=1, source_target_pairs={{8,16},{16,8},{24,32},{32,24},{40,48},{48,40},{56,64},{64,56},{72,... | collective-permute-start | bytes 552968 | tf_op jit(solution)/shard_map/ppermute | solution.py:233
  34.4 1.9 %collective-permute-start = (bf16[144,640]{1,0:T(8,128)(2,1)S(1)}, bf16[144,640]{1,0:T(8,128)(2,1)S(1)}, u32[]{:S(2)}, u32[]{:S(2)}) collective-permute-start(bf16[144,640]{1,0:T(8,128)(2,1)S(1)} %shard_map.89.b_ref), channel_id=1, source_target_pairs={{0,8},{8,0},{16,24},{24,16},{32,40},{40,32},{48,56},{56,48},{64,72... | collective-permute-start | bytes 552968 | tf_op jit(solution)/shard_map/ppermute | solution.py:233
  36.3 6.7 %all-gather.3.cot_ref = bf16[4,36,1280]{2,1,0:T(8,128)(2,1)S(1)} all-gather(bf16[1,36,1280]{2,1,0:T(8,128)(2,1)S(1)} %bitcast.20), channel_id=3, replica_groups=mesh['pair'=64,'half'=2,'space'=4] {'space'}, dimensions={0}, use_global_device_ids=true | all-gather | bytes 460800 | tf_op jit(solution)/shard_map/all_gather | solution.py:267
  43.0 0.8 shard_map.88.a_ref
  43.8 3.4 %collective-permute-done.even_ref = bf16[144,640]{1,0:T(8,128)(2,1)S(1)} collective-permute-done((bf16[144,640]{1,0:T(8,128)(2,1)S(1)}, bf16[144,640]{1,0:T(8,128)(2,1)S(1)}, u32[]{:S(2)}, u32[]{:S(2)}) %collective-permute-start) | collective-permute-done | bytes 184352 | tf_op jit(solution)/shard_map/ppermute | solution.py:233
  47.2 1.6 %shard_map.90 = (bf16[144,640]{1,0:T(8,128)(2,1)S(1)}, bf16[144,640]{1,0:T(8,128)(2,1)S(1)}, f32[144,640]{1,0:T(8,128)S(1)}, bf16[5,144,256]{2,1,0:T(8,128)(2,1)S(1)}) custom-call(s32[1]{0:T(128)} %bitcast.2.pair_ref, bf16[144,640]{1,0:T(8,128)(2,1)S(1)} %shard_map.88.a_ref, bf16[144,640]{1,0:T(8,128)(2,1)S(1)} %shard_map.89.b_ref, ...), custom_call_target="tpu_custom_call" | custom-call | tf_op jit(solution)/shard_map/pallas_call | solution.py:269
  48.8 1.9 %collective-permute-start.2 = (bf16[144,640]{1,0:T(8,128)(2,1)S(1)}, bf16[144,640]{1,0:T(8,128)(2,1)S(1)}, u32[]{:S(2)}, u32[]{:S(2)}) collective-permute-start(bf16[144,640]{1,0:T(8,128)(2,1)S(1)} %get-tuple-element.18), channel_id=1, source_target_pairs={{0,8},{8,0},{16,24},{24,16},{32,40},{40,32},{48,56},{56,48},{64,72... | collective-permute-start | bytes 552968 | tf_op jit(solution)/shard_map/ppermute | solution.py:233
  50.7 4.4 %collective-permute-start.3 = (bf16[144,640]{1,0:T(8,128)(2,1)S(1)}, bf16[144,640]{1,0:T(8,128)(2,1)S(1)}, u32[]{:S(2)}, u32[]{:S(2)}) collective-permute-start(bf16[144,640]{1,0:T(8,128)(2,1)S(1)} %get-tuple-element.19), channel_id=1, source_target_pairs={{8,16},{16,8},{24,32},{32,24},{40,48},{48,40},{56,64},{64,56},{72,... | collective-permute-start | bytes 552968 | tf_op jit(solution)/shard_map/ppermute | solution.py:233
  55.2 1.2 %shard_map.91 = (f32[144,1280]{1,0:T(8,128)S(1)}, f32[144,1280]{1,0:T(8,128)S(1)}) custom-call(s32[1]{0:T(128)} %bitcast.2.pair_ref, bf16[5,144,256]{2,1,0:T(8,128)(2,1)S(1)} %get-tuple-element.14.small_ref, bf16[144,640]{1,0:T(8,128)(2,1)S(1)} %shard_map.89.b_ref, bf16[144,640]{1,0:T(8,128)(2,1)S(1)} %collective-permute-done.even_ref, ...), custom_call_target="tpu_custom_call" | custom-call | tf_op jit(solution)/shard_map/pallas_call | solution.py:277
  56.4 2.9 %collective-permute-done.2.even_ref = bf16[144,640]{1,0:T(8,128)(2,1)S(1)} collective-permute-done((bf16[144,640]{1,0:T(8,128)(2,1)S(1)}, bf16[144,640]{1,0:T(8,128)(2,1)S(1)}, u32[]{:S(2)}, u32[]{:S(2)}) %collective-permute-start.2) | collective-permute-done | bytes 184352 | tf_op jit(solution)/shard_map/ppermute | solution.py:233
  59.3 8.2 %collective-permute-done.3.odd_ref = bf16[144,640]{1,0:T(8,128)(2,1)S(1)} collective-permute-done((bf16[144,640]{1,0:T(8,128)(2,1)S(1)}, bf16[144,640]{1,0:T(8,128)(2,1)S(1)}, u32[]{:S(2)}, u32[]{:S(2)}) %collective-permute-start.3) | collective-permute-done | bytes 184352 | tf_op jit(solution)/shard_map/ppermute | solution.py:233
  67.5 0.6 shard_map.92
  68.2 0.0 copy-start.10
  68.2 16.8 %all_to_all.11.parts_ref = bf16[8,36,1280]{2,1,0:T(8,128)(2,1)S(1)} all-to-all(bf16[8,36,1280]{2,1,0:T(8,128)(2,1)S(1)} %shard_map.92), channel_id=1, replica_groups=mesh['pair'=64,'half'=2,'space'=4] {'half','space'}, dimensions={0} | all-to-all | bytes 1474560 | tf_op jit(solution)/shard_map/all_to_all | solution.py:283
  85.0 1.0 %shard_map.93 = (bf16[36,1280]{1,0:T(8,128)(2,1)}, bf16[36,1280]{1,0:T(8,128)(2,1)}) custom-call(bf16[36,1280]{1,0:T(8,128)(2,1)S(1)} %bitcast.17, bf16[36,1280]{1,0:T(8,128)(2,1)S(1)} %bitcast.19, bf16[1280]{0:T(1024)(128)(2,1)S(1)} %copy-done.10, bf16[8,36,1280]{2,1,0:T(8,128)(2,1)S(1)} %all_to_all.11.parts_ref), custom_call_target="tpu_custom_call" | custom-call | tf_op jit(solution)/shard_map/pallas_call | solution.py:284
  (18 shorter events, 0.1 us)
Async XLA Ops:
  0.6 18.3 %copy-start = (bf16[1280,320]{0,1:T(8,128)(2,1)S(1)}, bf16[1280,320]{0,1:T(8,128)(2,1)}, u32[]{:S(2)}) copy-start(bf16[1280,320]{0,1:T(8,128)(2,1)} %param.11) | copy-start | bytes 2457604
  0.6 1.0 %copy-start.5 = (bf16[1,1,36,1280]{3,2,1,0:T(8,128)(2,1)S(1)}, bf16[1,1,36,1280]{3,2,1,0:T(8,128)(2,1)}, u32[]{:S(2)}) copy-start(bf16[1,1,36,1280]{3,2,1,0:T(8,128)(2,1)} %param.7) | copy-start | bytes 276484
  1.6 0.9 %copy-start.7 = (bf16[1,1,36,1280]{3,2,1,0:T(8,128)(2,1)S(1)}, bf16[1,1,36,1280]{3,2,1,0:T(8,128)(2,1)}, u32[]{:S(2)}) copy-start(bf16[1,1,36,1280]{3,2,1,0:T(8,128)(2,1)} %param.8) | copy-start | bytes 276484
  2.5 0.7 copy-start.9
  19.0 1.1 %copy-start.1 = (bf16[1280,320]{0,1:T(8,128)(2,1)S(1)}, bf16[1280,320]{0,1:T(8,128)(2,1)}, u32[]{:S(2)}) copy-start(bf16[1280,320]{0,1:T(8,128)(2,1)} %param.12) | copy-start | bytes 2457604
  20.1 22.9 %copy-start.3 = (bf16[1280,320]{0,1:T(8,128)(2,1)S(1)}, bf16[1280,320]{0,1:T(8,128)(2,1)}, u32[]{:S(2)}) copy-start(bf16[1280,320]{0,1:T(8,128)(2,1)} %param.10) | copy-start | bytes 2457604
  20.1 22.9 %copy-start.4 = (bf16[320,1280]{1,0:T(8,128)(2,1)S(1)}, bf16[320,1280]{1,0:T(8,128)(2,1)}, u32[]{:S(2)}) copy-start(bf16[320,1280]{1,0:T(8,128)(2,1)} %wo_ref.3) | copy-start | bytes 2457604
  20.9 22.9 %collective-permute-start.1 = (bf16[144,640]{1,0:T(8,128)(2,1)S(1)}, bf16[144,640]{1,0:T(8,128)(2,1)S(1)}, u32[]{:S(2)}, u32[]{:S(2)}) collective-permute-start(bf16[144,640]{1,0:T(8,128)(2,1)S(1)} %shard_map.89.b_ref), channel_id=1, source_target_pairs={{8,16},{16,8},{24,32},{32,24},{40,48},{48,40},{56,64},{64,56},{72,... | collective-permute-start | bytes 552968 | tf_op jit(solution)/shard_map/ppermute | solution.py:233
  34.4 12.8 %collective-permute-start = (bf16[144,640]{1,0:T(8,128)(2,1)S(1)}, bf16[144,640]{1,0:T(8,128)(2,1)S(1)}, u32[]{:S(2)}, u32[]{:S(2)}) collective-permute-start(bf16[144,640]{1,0:T(8,128)(2,1)S(1)} %shard_map.89.b_ref), channel_id=1, source_target_pairs={{0,8},{8,0},{16,24},{24,16},{32,40},{40,32},{48,56},{56,48},{64,72... | collective-permute-start | bytes 552968 | tf_op jit(solution)/shard_map/ppermute | solution.py:233
  48.8 10.5 %collective-permute-start.2 = (bf16[144,640]{1,0:T(8,128)(2,1)S(1)}, bf16[144,640]{1,0:T(8,128)(2,1)S(1)}, u32[]{:S(2)}, u32[]{:S(2)}) collective-permute-start(bf16[144,640]{1,0:T(8,128)(2,1)S(1)} %get-tuple-element.18), channel_id=1, source_target_pairs={{0,8},{8,0},{16,24},{24,16},{32,40},{40,32},{48,56},{56,48},{64,72... | collective-permute-start | bytes 552968 | tf_op jit(solution)/shard_map/ppermute | solution.py:233
  50.7 16.8 %collective-permute-start.3 = (bf16[144,640]{1,0:T(8,128)(2,1)S(1)}, bf16[144,640]{1,0:T(8,128)(2,1)S(1)}, u32[]{:S(2)}, u32[]{:S(2)}) collective-permute-start(bf16[144,640]{1,0:T(8,128)(2,1)S(1)} %get-tuple-element.19), channel_id=1, source_target_pairs={{8,16},{16,8},{24,32},{32,24},{40,48},{48,40},{56,64},{64,56},{72,... | collective-permute-start | bytes 552968 | tf_op jit(solution)/shard_map/ppermute | solution.py:233
  55.2 12.4 %copy-start.2 = (bf16[1280,320]{0,1:T(8,128)(2,1)S(1)}, bf16[1280,320]{0,1:T(8,128)(2,1)}, u32[]{:S(2)}) copy-start(bf16[1280,320]{0,1:T(8,128)(2,1)} %param.12) | copy-start | bytes 2457604
  68.1 16.9 %copy-start.6 = (bf16[1,1,36,1280]{3,2,1,0:T(8,128)(2,1)S(1)}, bf16[1,1,36,1280]{3,2,1,0:T(8,128)(2,1)}, u32[]{:S(2)}) copy-start(bf16[1,1,36,1280]{3,2,1,0:T(8,128)(2,1)} %param.7) | copy-start | bytes 276484
  68.1 16.9 %copy-start.8 = (bf16[1,1,36,1280]{3,2,1,0:T(8,128)(2,1)S(1)}, bf16[1,1,36,1280]{3,2,1,0:T(8,128)(2,1)}, u32[]{:S(2)}) copy-start(bf16[1,1,36,1280]{3,2,1,0:T(8,128)(2,1)} %param.8) | copy-start | bytes 276484
  68.2 16.8 %copy-start.10 = (bf16[1280]{0:T(1024)(128)(2,1)S(1)}, bf16[1280]{0:T(1024)(128)(2,1)}, u32[]{:S(2)}) copy-start(bf16[1280]{0:T(1024)(128)(2,1)} %gain_ref.1) | copy-start | bytes 7684

commit v4 on v3

--- a/solution.py
+++ b/solution.py
@@ -10,6 +10,7 @@
 
 HEAD_DIM = 64
 HEAD_SHIFT = 6
+COST = 10_000_000_000
 EPSILON = 1e-05
 NEG_FILL = -1e30
 ORDERED = (-2, -1, 0, 1, 2)
@@ -39,40 +40,45 @@
     return shifted * inverse, inverse
 
 
-def norm_kernel(x_hbm, cot_hbm, gain_hbm, out_ref, x_ref, cot_ref, gain_ref, sems):
-    copies = [
-        pltpu.make_async_copy(source, target, sems.at[i])
-        for i, (source, target) in enumerate(
-            ((x_hbm, x_ref), (gain_hbm, gain_ref), (cot_hbm, cot_ref))
-        )
-    ]
-    for copy in copies:
-        copy.start()
+def packed(block):
+    width = block.shape[1] // 2
+    return [block[:, :width], block[:, width:]]
+
+
+def unpacked(block):
+    rows = block.shape[0] // 2
+    return jnp.concatenate([block[:rows], block[rows:]], axis=1)
+
+
+def split_kernel(x_ref, cot_ref, out_ref):
     half = x_ref.shape[0] // PAIR
-    copies[0].wait()
-    normed, _ = normalized(x_ref[...].astype(F32))
-    copies[1].wait()
-    hidden = normed * gain_ref[...].astype(F32).reshape(1, -1)
-    copies[2].wait()
-    cot = cot_ref[...].astype(F32)
+    x, cot = x_ref[...].astype(F32), cot_ref[...].astype(F32)
     for h in range(PAIR):
         rows = slice(h * half, (h + 1) * half)
-        out_ref[h] = jnp.concatenate([hidden[rows], cot[rows]], axis=0).astype(BF16)
-
-
-def take_kernel(halves_ref, hidden_ref, cot_ref):
+        out_ref[h] = jnp.concatenate(packed(x[rows]) + packed(cot[rows]), axis=0).astype(BF16)
+
+
+def norm_kernel(halves_ref, gain_ref, hidden_ref, cot_ref):
     half = halves_ref.shape[1] // 2
     both = [halves_ref[f].astype(F32) for f in range(PAIR)]
-    hidden_ref[...] = jnp.concatenate([v[:half] for v in both], axis=0).astype(BF16)
+    x = jnp.concatenate([unpacked(v[:half]) for v in both], axis=0)
+    normed, _ = normalized(x)
+    hidden = normed * gain_ref[...].astype(F32).reshape(1, -1)
+    rows = x.shape[0] // PAIR
+    hidden = packed(hidden[:rows]) + packed(hidden[rows:])
+    hidden_ref[...] = jnp.concatenate(hidden, axis=0).astype(BF16)
     cot_ref[...] = jnp.concatenate([v[half:] for v in both], axis=0).astype(BF16)
 
 
 def gathered(g_ref, rows_ref):
-    half = g_ref.shape[1] // PAIR
+    whole, width = g_ref.shape[1] // PAIR, g_ref.shape[2]
+    half = whole // 2
     for frame in range(PAIR):
         for s in range(SHARDS):
             start = (frame * SHARDS + s) * half
-            rows_ref[start : start + half, :] = g_ref[s, frame * half : (frame + 1) * half].astype(F32)
+            block = g_ref[s, frame * whole : (frame + 1) * whole].astype(F32)
+            rows_ref[start : start + half, :width] = block[:half]
+            rows_ref[start : start + half, width:] = block[half:]
     return rows_ref[...].astype(BF16)
 
 
@@ -181,7 +187,7 @@
 
 def back_kernel(out_ref, query_part_ref, own_ref, even_ref, odd_ref, wk_ref, wv_ref, parts_ref, rows_ref):
     width = own_ref.shape[1] // 2
-    half = parts_ref.shape[1] // 2
+    half = rows_ref.shape[0] // parts_ref.shape[0]
     total = own_ref[...] + even_ref[...].astype(F32) + odd_ref[...].astype(F32)
     total = total.astype(BF16)
     rows_ref[...] = (
@@ -191,7 +197,8 @@
     )
     for part in range(PAIR * SHARDS):
         rows = slice(part * half, (part + 1) * half)
-        parts_ref[part] = jnp.concatenate([out_ref[rows], rows_ref[rows]], axis=0).astype(BF16)
+        both = packed(out_ref[rows]) + packed(rows_ref[rows])
+        parts_ref[part] = jnp.concatenate(both, axis=0).astype(BF16)
 
 
 def finish_kernel(x_ref, cot_ref, gain_ref, parts_ref, block_ref, grads_ref):
@@ -199,8 +206,8 @@
     summed = [
         sum(parts_ref[h * SHARDS + s].astype(F32) for s in range(SHARDS)) for h in range(PAIR)
     ]
-    out = jnp.concatenate([part[:half] for part in summed], axis=0)
-    hidden_grads = jnp.concatenate([part[half:] for part in summed], axis=0)
+    out = jnp.concatenate([unpacked(part[:half]) for part in summed], axis=0)
+    hidden_grads = jnp.concatenate([unpacked(part[half:]) for part in summed], axis=0)
     x = x_ref[...].astype(F32)
     block_ref[...] = (x + out).astype(BF16)
     normed, inverse = normalized(x)
@@ -213,7 +220,7 @@
     grads_ref[...] = (cot_ref[...].astype(F32) + layer_grads).astype(BF16)
 
 
-def call(kernel, out_shape, in_specs, scratch=(), flops=0, bytes_accessed=0):
+def call(kernel, out_shape, in_specs, scratch=(), cost=0):
     return pl.pallas_call(
         kernel,
         out_shape=out_shape,
@@ -221,7 +228,7 @@
         out_specs=jax.tree.map(lambda _: VMEM, out_shape),
         scratch_shapes=list(scratch),
         compiler_params=PARAMS,
-        cost_estimate=pl.CostEstimate(flops=flops, bytes_accessed=bytes_accessed, transcendentals=0),
+        cost_estimate=pl.CostEstimate(flops=cost, bytes_accessed=0, transcendentals=0),
     )
 
 
@@ -247,20 +254,11 @@
     row_scratch = pltpu.VMEM((rows, channels), F32)
     near_scratch = pltpu.VMEM((3 * rows, 2 * local), F32)
 
-    halves = call(
-        norm_kernel,
-        shape((PAIR, piece, channels), BF16),
-        [pl.BlockSpec(memory_space=pl.ANY)] * 3,
-        [
-            pltpu.VMEM((piece, channels), BF16),
-            pltpu.VMEM((piece, channels), BF16),
-            pltpu.VMEM((channels,), BF16),
-            pltpu.SemaphoreType.DMA((3,)),
-        ],
-    )(x, cot, gain)
+    packed_rows, packed_width = 2 * piece, channels // 2
+    halves = call(split_kernel, shape((PAIR, packed_rows, packed_width), BF16), [VMEM] * 2, cost=COST)(x, cot)
     halves = lax.all_to_all(halves, "half", 0, 0)
-    own_rows = shape((piece, channels), BF16)
-    hidden, cot_rows = call(take_kernel, (own_rows, own_rows), [VMEM])(halves)
+    own_rows = shape((packed_rows, packed_width), BF16)
+    hidden, cot_rows = call(norm_kernel, (own_rows, own_rows), [VMEM] * 2, cost=COST)(halves, gain)
     hidden = lax.all_gather(hidden, "space", axis=0)
     b = call(key_value_kernel, wide, [VMEM] * 3, [row_scratch])(hidden, wk, wv)
     near = [exchanged(b, first) for first in (0, 1)]
@@ -277,7 +275,7 @@
     out, query_part = call(mix_kernel, (full, full), [SMEM] + [VMEM] * 6, [near_scratch])(
         pair, small, b, *near, wq, wo
     )
-    parts = call(back_kernel, shape((PAIR * SHARDS, piece, channels), BF16), [VMEM] * 7, [row_scratch])(
+    parts = call(back_kernel, shape((PAIR * SHARDS, packed_rows, packed_width), BF16), [VMEM] * 7, [row_scratch])(
         out, query_part, own, *arrived, wk, wv
     )
     parts = lax.all_to_all(parts, ("half", "space"), 0, 0)

time: 86.7 us -> 84 us (0.969)
  local copies, waits for them, and re-layouts: 3.73 us -> 1.82 us
  blocking collectives: 38.7 us -> 37.6 us
    unnamed x22 -> x20, local copies, waits for them, and re-layouts: 3.73 us -> 1.82 us
where the time goes in v4:
time: 84 us; the launch traced here: 82.8 us
  blocking collectives  37.6 us (45%)
  starting transfers between devices  21.8 us (26%)
  waiting for transfers between devices  14.5 us (17%)
  Pallas kernels  6.3 us (8%)
  local copies, waits for them, and re-layouts  1.82 us (2%)
    ppermute x4, starting transfers between devices, exchanged(): return lax.ppermute(block, 'pair', route)  21.8 us
    all_to_all x1, blocking collectives, per_device(): parts = lax.all_to_all(parts, ('half', 'space'), 0, 0)  16.1 us
    ppermute x4, waiting for transfers between devices, exchanged(): return lax.ppermute(block, 'pair', route)  14.5 us
    all_gather x1, blocking collectives, per_device(): hidden = lax.all_gather(hidden, 'space', axis=0)  8.26 us
    all_to_all x1, blocking collectives, per_device(): halves = lax.all_to_all(halves, 'half', 0, 0)  6.77 us
    all_gather x1, blocking collectives, per_device(): cot_rows = lax.all_gather(cot_rows, 'space', axis=0)  6.44 us
    unnamed x20, local copies, waits for them, and re-layouts  1.82 us
  transfers between devices with their start and end apart: 4, of which 3 were waited for; matrix products, arithmetic and copies ran while one was open for 0% of the time, Pallas kernels for 2%

profile of v4, /device:TPU:57, one launch (start us, length us, event | category | flops | bytes accessed | tf_op | source)
XLA Modules:
  0.0 82.8 jit_solution(16773655885671276011)
XLA Ops:
  0.6 0.0 copy-start.5
  0.6 0.9 %copy-done.5 = bf16[1,1,36,1280]{3,2,1,0:T(8,128)(2,1)S(1)} copy-done((bf16[1,1,36,1280]{3,2,1,0:T(8,128)(2,1)S(1)}, bf16[1,1,36,1280]{3,2,1,0:T(8,128)(2,1)}, u32[]{:S(2)}) %copy-start.5) | copy-done | bytes 92184
  1.5 0.9 %copy-done.7 = bf16[1,1,36,1280]{3,2,1,0:T(8,128)(2,1)S(1)} copy-done((bf16[1,1,36,1280]{3,2,1,0:T(8,128)(2,1)S(1)}, bf16[1,1,36,1280]{3,2,1,0:T(8,128)(2,1)}, u32[]{:S(2)}) %copy-start.7) | copy-done | bytes 92184
  2.5 0.0 copy-start.9
  2.5 6.8 %all_to_all.10.halves_ref = bf16[2,72,640]{2,1,0:T(8,128)(2,1)S(1)} all-to-all(bf16[2,72,640]{2,1,0:T(8,128)(2,1)S(1)} %shard_map.86), channel_id=1, replica_groups=mesh['pair'=64,'half'=2,'space'=4] {'half'}, dimensions={0} | all-to-all | bytes 368640 | tf_op jit(solution)/shard_map/all_to_all | solution.py:259
  9.3 0.2 shard_map.87
  9.5 8.3 %all-gather = bf16[288,640]{1,0:T(8,128)(2,1)S(1)} all-gather(bf16[72,640]{1,0:T(8,128)(2,1)S(1)} %get-tuple-element.12), channel_id=2, replica_groups=mesh['pair'=64,'half'=2,'space'=4] {'space'}, dimensions={0}, use_global_device_ids=true | all-gather | bytes 460800 | tf_op jit(solution)/shard_map/all_gather | solution.py:262
  17.8 0.8 shard_map.89.b_ref
  18.6 13.5 %collective-permute-start.1 = (bf16[144,640]{1,0:T(8,128)(2,1)S(1)}, bf16[144,640]{1,0:T(8,128)(2,1)S(1)}, u32[]{:S(2)}, u32[]{:S(2)}) collective-permute-start(bf16[144,640]{1,0:T(8,128)(2,1)S(1)} %shard_map.89.b_ref), channel_id=1, source_target_pairs={{8,16},{16,8},{24,32},{32,24},{40,48},{48,40},{56,64},{64,56},{72,... | collective-permute-start | bytes 552968 | tf_op jit(solution)/shard_map/ppermute | solution.py:240
  32.1 1.9 %collective-permute-start = (bf16[144,640]{1,0:T(8,128)(2,1)S(1)}, bf16[144,640]{1,0:T(8,128)(2,1)S(1)}, u32[]{:S(2)}, u32[]{:S(2)}) collective-permute-start(bf16[144,640]{1,0:T(8,128)(2,1)S(1)} %shard_map.89.b_ref), channel_id=1, source_target_pairs={{0,8},{8,0},{16,24},{24,16},{32,40},{40,32},{48,56},{56,48},{64,72... | collective-permute-start | bytes 552968 | tf_op jit(solution)/shard_map/ppermute | solution.py:240
  34.0 6.4 %all-gather.1 = bf16[288,640]{1,0:T(8,128)(2,1)S(1)} all-gather(bf16[72,640]{1,0:T(8,128)(2,1)S(1)} %get-tuple-element.13), channel_id=3, replica_groups=mesh['pair'=64,'half'=2,'space'=4] {'space'}, dimensions={0}, use_global_device_ids=true | all-gather | bytes 460800 | tf_op jit(solution)/shard_map/all_gather | solution.py:265
  40.5 0.8 %shard_map.88.a_ref = bf16[144,640]{1,0:T(8,128)(2,1)S(1)} custom-call(bf16[4,72,640]{2,1,0:T(8,128)(2,1)S(1)} %bitcast.11, bf16[4,72,640]{2,1,0:T(8,128)(2,1)S(1)} %bitcast.18, bf16[320,1280]{1,0:T(8,128)(2,1)S(1)} %bitcast.12, bf16[320,1280]{1,0:T(8,128)(2,1)S(1)} %copy-done.1), custom_call_target="tpu_custom_call" | custom-call | tf_op jit(solution)/shard_map/pallas_call | solution.py:266
  41.3 3.5 %collective-permute-done.even_ref = bf16[144,640]{1,0:T(8,128)(2,1)S(1)} collective-permute-done((bf16[144,640]{1,0:T(8,128)(2,1)S(1)}, bf16[144,640]{1,0:T(8,128)(2,1)S(1)}, u32[]{:S(2)}, u32[]{:S(2)}) %collective-permute-start) | collective-permute-done | bytes 184352 | tf_op jit(solution)/shard_map/ppermute | solution.py:240
  44.8 1.6 %shard_map.90 = (bf16[144,640]{1,0:T(8,128)(2,1)S(1)}, bf16[144,640]{1,0:T(8,128)(2,1)S(1)}, f32[144,640]{1,0:T(8,128)S(1)}, bf16[5,144,256]{2,1,0:T(8,128)(2,1)S(1)}) custom-call(s32[1]{0:T(128)} %bitcast.2.pair_ref, bf16[144,640]{1,0:T(8,128)(2,1)S(1)} %shard_map.88.a_ref, bf16[144,640]{1,0:T(8,128)(2,1)S(1)} %shard_map.89.b_ref, ...), custom_call_target="tpu_custom_call" | custom-call | tf_op jit(solution)/shard_map/pallas_call | solution.py:267
  46.4 1.9 %collective-permute-start.2 = (bf16[144,640]{1,0:T(8,128)(2,1)S(1)}, bf16[144,640]{1,0:T(8,128)(2,1)S(1)}, u32[]{:S(2)}, u32[]{:S(2)}) collective-permute-start(bf16[144,640]{1,0:T(8,128)(2,1)S(1)} %get-tuple-element.18), channel_id=1, source_target_pairs={{0,8},{8,0},{16,24},{24,16},{32,40},{40,32},{48,56},{56,48},{64,72... | collective-permute-start | bytes 552968 | tf_op jit(solution)/shard_map/ppermute | solution.py:240
  48.3 4.4 %collective-permute-start.3 = (bf16[144,640]{1,0:T(8,128)(2,1)S(1)}, bf16[144,640]{1,0:T(8,128)(2,1)S(1)}, u32[]{:S(2)}, u32[]{:S(2)}) collective-permute-start(bf16[144,640]{1,0:T(8,128)(2,1)S(1)} %get-tuple-element.19), channel_id=1, source_target_pairs={{8,16},{16,8},{24,32},{32,24},{40,48},{48,40},{56,64},{64,56},{72,... | collective-permute-start | bytes 552968 | tf_op jit(solution)/shard_map/ppermute | solution.py:240
  52.8 1.2 %shard_map.91 = (f32[144,1280]{1,0:T(8,128)S(1)}, f32[144,1280]{1,0:T(8,128)S(1)}) custom-call(s32[1]{0:T(128)} %bitcast.2.pair_ref, bf16[5,144,256]{2,1,0:T(8,128)(2,1)S(1)} %get-tuple-element.14.small_ref, bf16[144,640]{1,0:T(8,128)(2,1)S(1)} %shard_map.89.b_ref, bf16[144,640]{1,0:T(8,128)(2,1)S(1)} %collective-permute-done.even_ref, ...), custom_call_target="tpu_custom_call" | custom-call | tf_op jit(solution)/shard_map/pallas_call | solution.py:275
  54.0 2.9 %collective-permute-done.2.even_ref = bf16[144,640]{1,0:T(8,128)(2,1)S(1)} collective-permute-done((bf16[144,640]{1,0:T(8,128)(2,1)S(1)}, bf16[144,640]{1,0:T(8,128)(2,1)S(1)}, u32[]{:S(2)}, u32[]{:S(2)}) %collective-permute-start.2) | collective-permute-done | bytes 184352 | tf_op jit(solution)/shard_map/ppermute | solution.py:240
  56.9 8.1 %collective-permute-done.3.odd_ref = bf16[144,640]{1,0:T(8,128)(2,1)S(1)} collective-permute-done((bf16[144,640]{1,0:T(8,128)(2,1)S(1)}, bf16[144,640]{1,0:T(8,128)(2,1)S(1)}, u32[]{:S(2)}, u32[]{:S(2)}) %collective-permute-start.3) | collective-permute-done | bytes 184352 | tf_op jit(solution)/shard_map/ppermute | solution.py:240
  65.0 0.6 shard_map.92
  65.6 0.0 copy-start.6
  65.6 0.0 copy-start.8
  65.6 16.1 %all_to_all.11.parts_ref = bf16[8,72,640]{2,1,0:T(8,128)(2,1)S(1)} all-to-all(bf16[8,72,640]{2,1,0:T(8,128)(2,1)S(1)} %shard_map.92), channel_id=1, replica_groups=mesh['pair'=64,'half'=2,'space'=4] {'half','space'}, dimensions={0} | all-to-all | bytes 1474560 | tf_op jit(solution)/shard_map/all_to_all | solution.py:281
  81.8 1.0 %shard_map.93 = (bf16[36,1280]{1,0:T(8,128)(2,1)}, bf16[36,1280]{1,0:T(8,128)(2,1)}) custom-call(bf16[36,1280]{1,0:T(8,128)(2,1)S(1)} %bitcast.20, bf16[36,1280]{1,0:T(8,128)(2,1)S(1)} %bitcast.22, bf16[1280]{0:T(1024)(128)(2,1)S(1)} %copy-done.9, bf16[8,72,640]{2,1,0:T(8,128)(2,1)S(1)} %all_to_all.11.parts_ref), custom_call_target="tpu_custom_call" | custom-call | tf_op jit(solution)/shard_map/pallas_call | solution.py:282
  (16 shorter events, 0.1 us)
Async XLA Ops:
  0.6 0.9 %copy-start.5 = (bf16[1,1,36,1280]{3,2,1,0:T(8,128)(2,1)S(1)}, bf16[1,1,36,1280]{3,2,1,0:T(8,128)(2,1)}, u32[]{:S(2)}) copy-start(bf16[1,1,36,1280]{3,2,1,0:T(8,128)(2,1)} %param.7) | copy-start | bytes 276484
  1.5 0.9 %copy-start.7 = (bf16[1,1,36,1280]{3,2,1,0:T(8,128)(2,1)S(1)}, bf16[1,1,36,1280]{3,2,1,0:T(8,128)(2,1)}, u32[]{:S(2)}) copy-start(bf16[1,1,36,1280]{3,2,1,0:T(8,128)(2,1)} %param.8) | copy-start | bytes 276484
  2.5 6.8 %copy-start.9 = (bf16[1280]{0:T(1024)(128)(2,1)S(1)}, bf16[1280]{0:T(1024)(128)(2,1)}, u32[]{:S(2)}) copy-start(bf16[1280]{0:T(1024)(128)(2,1)} %gain_ref.3) | copy-start | bytes 7684
  9.3 8.5 %copy-start.2 = (bf16[1280,320]{0,1:T(8,128)(2,1)S(1)}, bf16[1280,320]{0,1:T(8,128)(2,1)}, u32[]{:S(2)}) copy-start(bf16[1280,320]{0,1:T(8,128)(2,1)} %param.11) | copy-start | bytes 2457604
  9.3 8.5 %copy-start.3 = (bf16[1280,320]{0,1:T(8,128)(2,1)S(1)}, bf16[1280,320]{0,1:T(8,128)(2,1)}, u32[]{:S(2)}) copy-start(bf16[1280,320]{0,1:T(8,128)(2,1)} %param.12) | copy-start | bytes 2457604
  17.8 22.7 %copy-start = (bf16[1280,320]{0,1:T(8,128)(2,1)S(1)}, bf16[1280,320]{0,1:T(8,128)(2,1)}, u32[]{:S(2)}) copy-start(bf16[1280,320]{0,1:T(8,128)(2,1)} %param.10) | copy-start | bytes 2457604
  17.8 22.7 %copy-start.1 = (bf16[320,1280]{1,0:T(8,128)(2,1)S(1)}, bf16[320,1280]{1,0:T(8,128)(2,1)}, u32[]{:S(2)}) copy-start(bf16[320,1280]{1,0:T(8,128)(2,1)} %wo_ref.3) | copy-start | bytes 2457604
  18.6 22.8 %collective-permute-start.1 = (bf16[144,640]{1,0:T(8,128)(2,1)S(1)}, bf16[144,640]{1,0:T(8,128)(2,1)S(1)}, u32[]{:S(2)}, u32[]{:S(2)}) collective-permute-start(bf16[144,640]{1,0:T(8,128)(2,1)S(1)} %shard_map.89.b_ref), channel_id=1, source_target_pairs={{8,16},{16,8},{24,32},{32,24},{40,48},{48,40},{56,64},{64,56},{72,... | collective-permute-start | bytes 552968 | tf_op jit(solution)/shard_map/ppermute | solution.py:240
  32.1 12.8 %collective-permute-start = (bf16[144,640]{1,0:T(8,128)(2,1)S(1)}, bf16[144,640]{1,0:T(8,128)(2,1)S(1)}, u32[]{:S(2)}, u32[]{:S(2)}) collective-permute-start(bf16[144,640]{1,0:T(8,128)(2,1)S(1)} %shard_map.89.b_ref), channel_id=1, source_target_pairs={{0,8},{8,0},{16,24},{24,16},{32,40},{40,32},{48,56},{56,48},{64,72... | collective-permute-start | bytes 552968 | tf_op jit(solution)/shard_map/ppermute | solution.py:240
  46.4 10.5 %collective-permute-start.2 = (bf16[144,640]{1,0:T(8,128)(2,1)S(1)}, bf16[144,640]{1,0:T(8,128)(2,1)S(1)}, u32[]{:S(2)}, u32[]{:S(2)}) collective-permute-start(bf16[144,640]{1,0:T(8,128)(2,1)S(1)} %get-tuple-element.18), channel_id=1, source_target_pairs={{0,8},{8,0},{16,24},{24,16},{32,40},{40,32},{48,56},{56,48},{64,72... | collective-permute-start | bytes 552968 | tf_op jit(solution)/shard_map/ppermute | solution.py:240
  48.3 16.7 %collective-permute-start.3 = (bf16[144,640]{1,0:T(8,128)(2,1)S(1)}, bf16[144,640]{1,0:T(8,128)(2,1)S(1)}, u32[]{:S(2)}, u32[]{:S(2)}) collective-permute-start(bf16[144,640]{1,0:T(8,128)(2,1)S(1)} %get-tuple-element.19), channel_id=1, source_target_pairs={{8,16},{16,8},{24,32},{32,24},{40,48},{48,40},{56,64},{64,56},{72,... | collective-permute-start | bytes 552968 | tf_op jit(solution)/shard_map/ppermute | solution.py:240
  52.8 12.2 %copy-start.4 = (bf16[1280,320]{0,1:T(8,128)(2,1)S(1)}, bf16[1280,320]{0,1:T(8,128)(2,1)}, u32[]{:S(2)}) copy-start(bf16[1280,320]{0,1:T(8,128)(2,1)} %param.12) | copy-start | bytes 2457604
  65.6 16.1 %copy-start.6 = (bf16[1,1,36,1280]{3,2,1,0:T(8,128)(2,1)S(1)}, bf16[1,1,36,1280]{3,2,1,0:T(8,128)(2,1)}, u32[]{:S(2)}) copy-start(bf16[1,1,36,1280]{3,2,1,0:T(8,128)(2,1)} %param.7) | copy-start | bytes 276484
  65.6 16.1 %copy-start.8 = (bf16[1,1,36,1280]{3,2,1,0:T(8,128)(2,1)S(1)}, bf16[1,1,36,1280]{3,2,1,0:T(8,128)(2,1)}, u32[]{:S(2)}) copy-start(bf16[1,1,36,1280]{3,2,1,0:T(8,128)(2,1)} %param.8) | copy-start | bytes 276484

commit v5 on v4

--- a/solution.py
+++ b/solution.py
@@ -182,12 +182,24 @@
         mixed = mixed + dot_t(small_ref[i], reduce_mat) * near_ref[i * one : i * one + rows]
     mixed = (mixed * lane_scale(mixed.shape)).astype(BF16)
     query_part_ref[...] = dot(mixed[:, :half], wq_ref[...])
-    out_ref[...] = dot(mixed[:, half:], wo_ref[...])
-
-
-def back_kernel(out_ref, query_part_ref, own_ref, even_ref, odd_ref, wk_ref, wv_ref, parts_ref, rows_ref):
+    out_ref[...] = dot(mixed[:, half:], wo_ref[...]).astype(BF16)
+
+
+def join_kernel(core_ref, both_ref, out_ref, sum_ref):
+    sum_ref[...] = both_ref[0].astype(F32) + both_ref[1].astype(F32)
+    second = core_ref[0] == 1
+    share = out_ref.shape[0] // (PAIR * SHARDS)
+    for part in range(PAIR * SHARDS):
+        start = part * 2 * share
+        out_ref[part * share : (part + 1) * share] = jnp.where(
+            second, sum_ref[start + share : start + 2 * share], sum_ref[start : start + share]
+        )
+
+
+def back_kernel(out_ref, query_part_ref, own_ref, odd_ref, even_ref, wk_ref, wv_ref, parts_ref, rows_ref):
     width = own_ref.shape[1] // 2
     half = rows_ref.shape[0] // parts_ref.shape[0]
+    share = half // 2
     total = own_ref[...] + even_ref[...].astype(F32) + odd_ref[...].astype(F32)
     total = total.astype(BF16)
     rows_ref[...] = (
@@ -196,18 +208,21 @@
         + dot(total[:, width:], wv_ref[...])
     )
     for part in range(PAIR * SHARDS):
-        rows = slice(part * half, (part + 1) * half)
-        both = packed(out_ref[rows]) + packed(rows_ref[rows])
-        parts_ref[part] = jnp.concatenate(both, axis=0).astype(BF16)
+        grads = rows_ref[part * half : (part + 1) * half]
+        out = out_ref[part * share : (part + 1) * share]
+        parts_ref[part] = jnp.concatenate(packed(grads) + packed(out), axis=0).astype(BF16)
 
 
 def finish_kernel(x_ref, cot_ref, gain_ref, parts_ref, block_ref, grads_ref):
-    half = parts_ref.shape[1] // 2
-    summed = [
-        sum(parts_ref[h * SHARDS + s].astype(F32) for s in range(SHARDS)) for h in range(PAIR)
-    ]
-    out = jnp.concatenate([unpacked(part[:half]) for part in summed], axis=0)
-    hidden_grads = jnp.concatenate([unpacked(part[half:]) for part in summed], axis=0)
+    rows = x_ref.shape[0]
+    out, hidden_grads = [], []
+    for h in range(PAIR):
+        parts = [parts_ref[h * SHARDS + s].astype(F32) for s in range(SHARDS)]
+        hidden_grads.append(unpacked(sum(part[:rows] for part in parts)))
+        for core in range(2):
+            out.append(unpacked(sum(part[rows:] for part in parts[core::2])))
+    out = jnp.concatenate(out, axis=0)
+    hidden_grads = jnp.concatenate(hidden_grads, axis=0)
     x = x_ref[...].astype(F32)
     block_ref[...] = (x + out).astype(BF16)
     normed, inverse = normalized(x)
@@ -270,14 +285,23 @@
         [SMEM] + [VMEM] * 4,
         [near_scratch],
     )(pair, a, b, *near)
-    arrived = [exchanged(send, first) for first, send in zip((0, 1), sends)]
-    full = shape((rows, channels), F32)
-    out, query_part = call(mix_kernel, (full, full), [SMEM] + [VMEM] * 6, [near_scratch])(
-        pair, small, b, *near, wq, wo
-    )
-    parts = call(back_kernel, shape((PAIR * SHARDS, packed_rows, packed_width), BF16), [VMEM] * 7, [row_scratch])(
-        out, query_part, own, *arrived, wk, wv
-    )
+    arrived = [exchanged(sends[first], first) for first in (1, 0)]
+    out, query_part = call(
+        mix_kernel,
+        (shape((rows, channels), BF16), shape((rows, channels), F32)),
+        [SMEM] + [VMEM] * 6,
+        [near_scratch],
+    )(pair, small, b, *near, wq, wo)
+    cores = [[s, s + 1] for s in range(0, SHARDS, 2)]
+    out = lax.all_gather(out, "space", axis=0, axis_index_groups=cores)
+    core = (lax.axis_index("space") % 2).astype(jnp.int32).reshape(1)
+    out = call(join_kernel, shape((rows // 2, channels), F32), [SMEM, VMEM], [row_scratch])(core, out)
+    parts = call(
+        back_kernel,
+        shape((PAIR * SHARDS, packed_rows // PAIR + piece // 2, packed_width), BF16),
+        [VMEM] * 7,
+        [row_scratch],
+    )(out, query_part, own, *arrived, wk, wv)
     parts = lax.all_to_all(parts, ("half", "space"), 0, 0)
     block, grads = call(
         finish_kernel, (shape((piece, channels), BF16), shape((piece, channels), BF16)), [VMEM] * 4

time: 84 us -> 80.7 us (0.961)
  waiting for transfers between devices: 14.5 us -> 8.71 us
  blocking collectives: 37.6 us -> 40.7 us
    ppermute x4, waiting for transfers between devices: 14.5 us -> 8.71 us  [exchanged(): return lax.ppermute(block, 'pair', route)]
    all_gather x0 -> x1, blocking collectives: none -> 3.5 us  [per_device(): out = lax.all_gather(out, 'space', axis=0, axis_index_groups=cores)]
    pallas_call x2 -> x3, Pallas kernels: 1.8 us -> 2.03 us  [the longest x1 1.19 us: per_device(): call(mix_kernel, (shape((rows, channels), BF16), shape((rows, channels),...]
  transfers between devices with their start and end apart: 4 -> 4, of which waited for: 3 -> 2; matrix products, arithmetic and copies ran while one was open for 0% -> 0% of each run, Pallas kernels for 2% -> 3%
where the time goes in v5:
time: 80.7 us; the launch traced here: 80.3 us
  blocking collectives  40.7 us (50%)
  starting transfers between devices  21.8 us (27%)
  waiting for transfers between devices  8.71 us (11%)
  Pallas kernels  6.52 us (8%)
  local copies, waits for them, and re-layouts  1.82 us (2%)
    ppermute x4, starting transfers between devices, exchanged(): return lax.ppermute(block, 'pair', route)  21.8 us
    all_to_all x1, blocking collectives, per_device(): parts = lax.all_to_all(parts, ('half', 'space'), 0, 0)  15.7 us
    ppermute x4, waiting for transfers between devices, exchanged(): return lax.ppermute(block, 'pair', route)  8.71 us
    all_gather x1, blocking collectives, per_device(): hidden = lax.all_gather(hidden, 'space', axis=0)  8.26 us
    all_to_all x1, blocking collectives, per_device(): halves = lax.all_to_all(halves, 'half', 0, 0)  6.77 us
    all_gather x1, blocking collectives, per_device(): cot_rows = lax.all_gather(cot_rows, 'space', axis=0)  6.44 us
    all_gather x1, blocking collectives, per_device(): out = lax.all_gather(out, 'space', axis=0, axis_index_groups=cores)  3.5 us
    unnamed x20, local copies, waits for them, and re-layouts  1.82 us
  transfers between devices with their start and end apart: 4, of which 2 were waited for; matrix products, arithmetic and copies ran while one was open for 0% of the time, Pallas kernels for 3%

profile of v5, /device:TPU:57, one launch (start us, length us, event | category | flops | bytes accessed | tf_op | source)
XLA Modules:
  0.0 80.3 jit_solution(4695003498057592310)
XLA Ops:
  0.6 0.0 copy-start.5
  0.6 0.9 %copy-done.5 = bf16[1,1,36,1280]{3,2,1,0:T(8,128)(2,1)S(1)} copy-done((bf16[1,1,36,1280]{3,2,1,0:T(8,128)(2,1)S(1)}, bf16[1,1,36,1280]{3,2,1,0:T(8,128)(2,1)}, u32[]{:S(2)}) %copy-start.5) | copy-done | bytes 92184
  1.5 0.9 %copy-done.7 = bf16[1,1,36,1280]{3,2,1,0:T(8,128)(2,1)S(1)} copy-done((bf16[1,1,36,1280]{3,2,1,0:T(8,128)(2,1)S(1)}, bf16[1,1,36,1280]{3,2,1,0:T(8,128)(2,1)}, u32[]{:S(2)}) %copy-start.7) | copy-done | bytes 92184
  2.5 0.0 copy-start.9
  2.5 6.8 %all_to_all.10.halves_ref = bf16[2,72,640]{2,1,0:T(8,128)(2,1)S(1)} all-to-all(bf16[2,72,640]{2,1,0:T(8,128)(2,1)S(1)} %shard_map.86), channel_id=1, replica_groups=mesh['pair'=64,'half'=2,'space'=4] {'half'}, dimensions={0} | all-to-all | bytes 368640 | tf_op jit(solution)/shard_map/all_to_all | solution.py:274
  9.3 0.2 shard_map.87
  9.5 8.3 %all-gather = bf16[288,640]{1,0:T(8,128)(2,1)S(1)} all-gather(bf16[72,640]{1,0:T(8,128)(2,1)S(1)} %get-tuple-element.12), channel_id=2, replica_groups=mesh['pair'=64,'half'=2,'space'=4] {'space'}, dimensions={0}, use_global_device_ids=true | all-gather | bytes 460800 | tf_op jit(solution)/shard_map/all_gather | solution.py:277
  17.8 0.8 shard_map.89.b_ref
  18.6 13.5 %collective-permute-start.1 = (bf16[144,640]{1,0:T(8,128)(2,1)S(1)}, bf16[144,640]{1,0:T(8,128)(2,1)S(1)}, u32[]{:S(2)}, u32[]{:S(2)}) collective-permute-start(bf16[144,640]{1,0:T(8,128)(2,1)S(1)} %shard_map.89.b_ref), channel_id=1, source_target_pairs={{8,16},{16,8},{24,32},{32,24},{40,48},{48,40},{56,64},{64,56},{72,... | collective-permute-start | bytes 552968 | tf_op jit(solution)/shard_map/ppermute | solution.py:255
  32.1 1.9 %collective-permute-start = (bf16[144,640]{1,0:T(8,128)(2,1)S(1)}, bf16[144,640]{1,0:T(8,128)(2,1)S(1)}, u32[]{:S(2)}, u32[]{:S(2)}) collective-permute-start(bf16[144,640]{1,0:T(8,128)(2,1)S(1)} %shard_map.89.b_ref), channel_id=1, source_target_pairs={{0,8},{8,0},{16,24},{24,16},{32,40},{40,32},{48,56},{56,48},{64,72... | collective-permute-start | bytes 552968 | tf_op jit(solution)/shard_map/ppermute | solution.py:255
  34.0 6.4 %all-gather.1 = bf16[288,640]{1,0:T(8,128)(2,1)S(1)} all-gather(bf16[72,640]{1,0:T(8,128)(2,1)S(1)} %get-tuple-element.13), channel_id=3, replica_groups=mesh['pair'=64,'half'=2,'space'=4] {'space'}, dimensions={0}, use_global_device_ids=true | all-gather | bytes 460800 | tf_op jit(solution)/shard_map/all_gather | solution.py:280
  40.5 0.8 %shard_map.88.a_ref = bf16[144,640]{1,0:T(8,128)(2,1)S(1)} custom-call(bf16[4,72,640]{2,1,0:T(8,128)(2,1)S(1)} %bitcast.13, bf16[4,72,640]{2,1,0:T(8,128)(2,1)S(1)} %bitcast.21, bf16[320,1280]{1,0:T(8,128)(2,1)S(1)} %bitcast.14, bf16[320,1280]{1,0:T(8,128)(2,1)S(1)} %copy-done.1), custom_call_target="tpu_custom_call" | custom-call | tf_op jit(solution)/shard_map/pallas_call | solution.py:281
  41.3 3.5 %collective-permute-done.even_ref = bf16[144,640]{1,0:T(8,128)(2,1)S(1)} collective-permute-done((bf16[144,640]{1,0:T(8,128)(2,1)S(1)}, bf16[144,640]{1,0:T(8,128)(2,1)S(1)}, u32[]{:S(2)}, u32[]{:S(2)}) %collective-permute-start) | collective-permute-done | bytes 184352 | tf_op jit(solution)/shard_map/ppermute | solution.py:255
  44.8 1.6 %shard_map.90 = (bf16[144,640]{1,0:T(8,128)(2,1)S(1)}, bf16[144,640]{1,0:T(8,128)(2,1)S(1)}, f32[144,640]{1,0:T(8,128)S(1)}, bf16[5,144,256]{2,1,0:T(8,128)(2,1)S(1)}) custom-call(s32[1]{0:T(128)} %bitcast.3.pair_ref, bf16[144,640]{1,0:T(8,128)(2,1)S(1)} %shard_map.88.a_ref, bf16[144,640]{1,0:T(8,128)(2,1)S(1)} %shard_map.89.b_ref, ...), custom_call_target="tpu_custom_call" | custom-call | tf_op jit(solution)/shard_map/pallas_call | solution.py:282
  46.4 4.4 %collective-permute-start.2 = (bf16[144,640]{1,0:T(8,128)(2,1)S(1)}, bf16[144,640]{1,0:T(8,128)(2,1)S(1)}, u32[]{:S(2)}, u32[]{:S(2)}) collective-permute-start(bf16[144,640]{1,0:T(8,128)(2,1)S(1)} %get-tuple-element.18), channel_id=1, source_target_pairs={{8,16},{16,8},{24,32},{32,24},{40,48},{48,40},{56,64},{64,56},{72,... | collective-permute-start | bytes 552968 | tf_op jit(solution)/shard_map/ppermute | solution.py:255
  50.9 1.9 %collective-permute-start.3 = (bf16[144,640]{1,0:T(8,128)(2,1)S(1)}, bf16[144,640]{1,0:T(8,128)(2,1)S(1)}, u32[]{:S(2)}, u32[]{:S(2)}) collective-permute-start(bf16[144,640]{1,0:T(8,128)(2,1)S(1)} %get-tuple-element.19), channel_id=1, source_target_pairs={{0,8},{8,0},{16,24},{24,16},{32,40},{40,32},{48,56},{56,48},{64,72... | collective-permute-start | bytes 552968 | tf_op jit(solution)/shard_map/ppermute | solution.py:255
  52.8 1.2 %shard_map.91 = (bf16[144,1280]{1,0:T(8,128)(2,1)S(1)}, f32[144,1280]{1,0:T(8,128)S(1)}) custom-call(s32[1]{0:T(128)} %bitcast.3.pair_ref, bf16[5,144,256]{2,1,0:T(8,128)(2,1)S(1)} %get-tuple-element.14.small_ref, bf16[144,640]{1,0:T(8,128)(2,1)S(1)} %shard_map.89.b_ref, bf16[144,640]{1,0:T(8,128)(2,1)S(1)} %collective-permute-done.even_ref, ...), custom_call_target="tpu_custom_call" | custom-call | tf_op jit(solution)/shard_map/pallas_call | solution.py:289
  54.0 3.5 %all-gather.2 = bf16[288,1280]{1,0:T(8,128)(2,1)S(1)} all-gather(bf16[144,1280]{1,0:T(8,128)(2,1)S(1)} %get-tuple-element.15), channel_id=4, replica_groups={{0,1},{2,3},{4,5},{6,7},{8,9},{10,11},{12,13},{14,15},{16,17},{18,19},{..., dimensions={0}, use_global_device_ids=true | all-gather | bytes 1105920 | tf_op jit(solution)/shard_map/all_gather | solution.py:296
  57.5 0.2 shard_map.92.out_ref
  57.7 5.2 %collective-permute-done.2.odd_ref = bf16[144,640]{1,0:T(8,128)(2,1)S(1)} collective-permute-done((bf16[144,640]{1,0:T(8,128)(2,1)S(1)}, bf16[144,640]{1,0:T(8,128)(2,1)S(1)}, u32[]{:S(2)}, u32[]{:S(2)}) %collective-permute-start.2) | collective-permute-done | bytes 184352 | tf_op jit(solution)/shard_map/ppermute | solution.py:255
  62.9 0.6 shard_map.93
  63.5 0.0 copy-start.6
  63.6 15.7 %all_to_all.11.parts_ref = bf16[8,54,640]{2,1,0:T(8,128)(2,1)S(1)} all-to-all(bf16[8,54,640]{2,1,0:T(8,128)(2,1)S(1)} %shard_map.93), channel_id=1, replica_groups=mesh['pair'=64,'half'=2,'space'=4] {'half','space'}, dimensions={0} | all-to-all | bytes 1105920 | tf_op jit(solution)/shard_map/all_to_all | solution.py:305
  79.3 1.0 %shard_map.94 = (bf16[36,1280]{1,0:T(8,128)(2,1)}, bf16[36,1280]{1,0:T(8,128)(2,1)}) custom-call(bf16[36,1280]{1,0:T(8,128)(2,1)S(1)} %bitcast.23, bf16[36,1280]{1,0:T(8,128)(2,1)S(1)} %bitcast.25, bf16[1280]{0:T(1024)(128)(2,1)S(1)} %copy-done.9, bf16[8,54,640]{2,1,0:T(8,128)(2,1)S(1)} %all_to_all.11.parts_ref), custom_call_target="tpu_custom_call" | custom-call | tf_op jit(solution)/shard_map/pallas_call | solution.py:306
  (18 shorter events, 0.1 us)
Async XLA Ops:
  0.6 0.9 %copy-start.5 = (bf16[1,1,36,1280]{3,2,1,0:T(8,128)(2,1)S(1)}, bf16[1,1,36,1280]{3,2,1,0:T(8,128)(2,1)}, u32[]{:S(2)}) copy-start(bf16[1,1,36,1280]{3,2,1,0:T(8,128)(2,1)} %param.7) | copy-start | bytes 276484
  1.5 0.9 %copy-start.7 = (bf16[1,1,36,1280]{3,2,1,0:T(8,128)(2,1)S(1)}, bf16[1,1,36,1280]{3,2,1,0:T(8,128)(2,1)}, u32[]{:S(2)}) copy-start(bf16[1,1,36,1280]{3,2,1,0:T(8,128)(2,1)} %param.8) | copy-start | bytes 276484
  2.5 6.8 %copy-start.9 = (bf16[1280]{0:T(1024)(128)(2,1)S(1)}, bf16[1280]{0:T(1024)(128)(2,1)}, u32[]{:S(2)}) copy-start(bf16[1280]{0:T(1024)(128)(2,1)} %gain_ref.3) | copy-start | bytes 7684
  9.3 8.5 %copy-start.2 = (bf16[1280,320]{0,1:T(8,128)(2,1)S(1)}, bf16[1280,320]{0,1:T(8,128)(2,1)}, u32[]{:S(2)}) copy-start(bf16[1280,320]{0,1:T(8,128)(2,1)} %param.11) | copy-start | bytes 2457604
  9.3 8.5 %copy-start.3 = (bf16[1280,320]{0,1:T(8,128)(2,1)S(1)}, bf16[1280,320]{0,1:T(8,128)(2,1)}, u32[]{:S(2)}) copy-start(bf16[1280,320]{0,1:T(8,128)(2,1)} %param.12) | copy-start | bytes 2457604
  17.8 22.7 %copy-start = (bf16[1280,320]{0,1:T(8,128)(2,1)S(1)}, bf16[1280,320]{0,1:T(8,128)(2,1)}, u32[]{:S(2)}) copy-start(bf16[1280,320]{0,1:T(8,128)(2,1)} %param.10) | copy-start | bytes 2457604
  17.8 22.7 %copy-start.1 = (bf16[320,1280]{1,0:T(8,128)(2,1)S(1)}, bf16[320,1280]{1,0:T(8,128)(2,1)}, u32[]{:S(2)}) copy-start(bf16[320,1280]{1,0:T(8,128)(2,1)} %wo_ref.3) | copy-start | bytes 2457604
  18.6 22.8 %collective-permute-start.1 = (bf16[144,640]{1,0:T(8,128)(2,1)S(1)}, bf16[144,640]{1,0:T(8,128)(2,1)S(1)}, u32[]{:S(2)}, u32[]{:S(2)}) collective-permute-start(bf16[144,640]{1,0:T(8,128)(2,1)S(1)} %shard_map.89.b_ref), channel_id=1, source_target_pairs={{8,16},{16,8},{24,32},{32,24},{40,48},{48,40},{56,64},{64,56},{72,... | collective-permute-start | bytes 552968 | tf_op jit(solution)/shard_map/ppermute | solution.py:255
  32.1 12.8 %collective-permute-start = (bf16[144,640]{1,0:T(8,128)(2,1)S(1)}, bf16[144,640]{1,0:T(8,128)(2,1)S(1)}, u32[]{:S(2)}, u32[]{:S(2)}) collective-permute-start(bf16[144,640]{1,0:T(8,128)(2,1)S(1)} %shard_map.89.b_ref), channel_id=1, source_target_pairs={{0,8},{8,0},{16,24},{24,16},{32,40},{40,32},{48,56},{56,48},{64,72... | collective-permute-start | bytes 552968 | tf_op jit(solution)/shard_map/ppermute | solution.py:255
  46.4 16.5 %collective-permute-start.2 = (bf16[144,640]{1,0:T(8,128)(2,1)S(1)}, bf16[144,640]{1,0:T(8,128)(2,1)S(1)}, u32[]{:S(2)}, u32[]{:S(2)}) collective-permute-start(bf16[144,640]{1,0:T(8,128)(2,1)S(1)} %get-tuple-element.18), channel_id=1, source_target_pairs={{8,16},{16,8},{24,32},{32,24},{40,48},{48,40},{56,64},{64,56},{72,... | collective-permute-start | bytes 552968 | tf_op jit(solution)/shard_map/ppermute | solution.py:255
  50.9 12.1 %collective-permute-start.3 = (bf16[144,640]{1,0:T(8,128)(2,1)S(1)}, bf16[144,640]{1,0:T(8,128)(2,1)S(1)}, u32[]{:S(2)}, u32[]{:S(2)}) collective-permute-start(bf16[144,640]{1,0:T(8,128)(2,1)S(1)} %get-tuple-element.19), channel_id=1, source_target_pairs={{0,8},{8,0},{16,24},{24,16},{32,40},{40,32},{48,56},{56,48},{64,72... | collective-permute-start | bytes 552968 | tf_op jit(solution)/shard_map/ppermute | solution.py:255
  57.5 5.4 %copy-start.4 = (bf16[1280,320]{0,1:T(8,128)(2,1)S(1)}, bf16[1280,320]{0,1:T(8,128)(2,1)}, u32[]{:S(2)}) copy-start(bf16[1280,320]{0,1:T(8,128)(2,1)} %param.12) | copy-start | bytes 2457604
  63.5 15.7 %copy-start.6 = (bf16[1,1,36,1280]{3,2,1,0:T(8,128)(2,1)S(1)}, bf16[1,1,36,1280]{3,2,1,0:T(8,128)(2,1)}, u32[]{:S(2)}) copy-start(bf16[1,1,36,1280]{3,2,1,0:T(8,128)(2,1)} %param.7) | copy-start | bytes 276484
  63.6 15.7 %copy-start.8 = (bf16[1,1,36,1280]{3,2,1,0:T(8,128)(2,1)S(1)}, bf16[1,1,36,1280]{3,2,1,0:T(8,128)(2,1)}, u32[]{:S(2)}) copy-start(bf16[1,1,36,1280]{3,2,1,0:T(8,128)(2,1)} %param.8) | copy-start | bytes 276484

commit v6 on v5

--- a/solution.py
+++ b/solution.py
@@ -50,24 +50,17 @@
     return jnp.concatenate([block[:rows], block[rows:]], axis=1)
 
 
-def split_kernel(x_ref, cot_ref, out_ref):
-    half = x_ref.shape[0] // PAIR
-    x, cot = x_ref[...].astype(F32), cot_ref[...].astype(F32)
-    for h in range(PAIR):
-        rows = slice(h * half, (h + 1) * half)
-        out_ref[h] = jnp.concatenate(packed(x[rows]) + packed(cot[rows]), axis=0).astype(BF16)
-
-
 def norm_kernel(halves_ref, gain_ref, hidden_ref, cot_ref):
     half = halves_ref.shape[1] // 2
     both = [halves_ref[f].astype(F32) for f in range(PAIR)]
-    x = jnp.concatenate([unpacked(v[:half]) for v in both], axis=0)
+    x = jnp.concatenate([v[:half] for v in both], axis=0)
     normed, _ = normalized(x)
     hidden = normed * gain_ref[...].astype(F32).reshape(1, -1)
     rows = x.shape[0] // PAIR
     hidden = packed(hidden[:rows]) + packed(hidden[rows:])
     hidden_ref[...] = jnp.concatenate(hidden, axis=0).astype(BF16)
-    cot_ref[...] = jnp.concatenate([v[half:] for v in both], axis=0).astype(BF16)
+    cot = packed(both[0][half:]) + packed(both[1][half:])
+    cot_ref[...] = jnp.concatenate(cot, axis=0).astype(BF16)
 
 
 def gathered(g_ref, rows_ref):
@@ -270,7 +263,8 @@
     near_scratch = pltpu.VMEM((3 * rows, 2 * local), F32)
 
     packed_rows, packed_width = 2 * piece, channels // 2
-    halves = call(split_kernel, shape((PAIR, packed_rows, packed_width), BF16), [VMEM] * 2, cost=COST)(x, cot)
+    halves = [block.reshape(PAIR, piece // PAIR, channels) for block in (x, cot)]
+    halves = jnp.concatenate(halves, axis=1)
     halves = lax.all_to_all(halves, "half", 0, 0)
     own_rows = shape((packed_rows, packed_width), BF16)
     hidden, cot_rows = call(norm_kernel, (own_rows, own_rows), [VMEM] * 2, cost=COST)(halves, gain)

time: 80.7 us -> 80 us (level)
    unnamed x20 -> x18, local copies, waits for them, and re-layouts: 1.82 us -> 0.05 us
    another operation x0 -> x2, local copies, waits for them, and re-layouts: none -> 0.98 us  [per_device(): block.reshape(PAIR, piece // PAIR, channels)]
where the time goes in v6:
time: 80 us; the launch traced here: 79.6 us
  blocking collectives  41.1 us (51%)
  starting transfers between devices  21.8 us (27%)
  waiting for transfers between devices  8.39 us (10%)
  Pallas kernels  6.48 us (8%)
  local copies, waits for them, and re-layouts  1.03 us (1%)
  between operations  0.81 us (1%)
    ppermute x4, starting transfers between devices, exchanged(): return lax.ppermute(block, 'pair', route)  21.8 us
    all_to_all x1, blocking collectives, per_device(): parts = lax.all_to_all(parts, ('half', 'space'), 0, 0)  15.8 us
    ppermute x4, waiting for transfers between devices, exchanged(): return lax.ppermute(block, 'pair', route)  8.39 us
    all_gather x1, blocking collectives, per_device(): hidden = lax.all_gather(hidden, 'space', axis=0)  8.26 us
    all_to_all x1, blocking collectives, per_device(): halves = lax.all_to_all(halves, 'half', 0, 0)  6.88 us
    all_gather x1, blocking collectives, per_device(): cot_rows = lax.all_gather(cot_rows, 'space', axis=0)  6.66 us
    all_gather x1, blocking collectives, per_device(): out = lax.all_gather(out, 'space', axis=0, axis_index_groups=cores)  3.49 us
  transfers between devices with their start and end apart: 4, of which 2 were waited for; matrix products, arithmetic and copies ran while one was open for 0% of the time, Pallas kernels for 3%

profile of v6, /device:TPU:57, one launch (start us, length us, event | category | flops | bytes accessed | tf_op | source)
XLA Modules:
  0.0 79.6 jit_solution(15018286201980834683)
XLA Ops:
  0.6 1.0 %reshape_reshape.6 = bf16[2,18,1280]{2,1,0:T(8,128)(2,1)S(1)} reshape(bf16[1,1,36,1280]{3,2,1,0:T(8,128)(2,1)} %param.7) | data formatting | bytes 184320 | tf_op jit(solution)/shard_map/reshape;reshape | solution.py:266
  1.7 0.0 copy-start.8
  1.7 6.9 %all_to_all.10.halves_ref = bf16[2,36,1280]{2,1,0:T(8,128)(2,1)S(1)} all-to-all(bf16[2,36,1280]{2,1,0:T(8,128)(2,1)S(1)} %pad_maximum_fusion), channel_id=1, replica_groups=mesh['pair'=64,'half'=2,'space'=4] {'half'}, dimensions={0} | all-to-all | bytes 368640 | tf_op jit(solution)/shard_map/all_to_all | solution.py:268
  8.6 0.2 shard_map.86
  8.8 0.0 copy-start.7
  8.8 8.3 %all-gather = bf16[288,640]{1,0:T(8,128)(2,1)S(1)} all-gather(bf16[72,640]{1,0:T(8,128)(2,1)S(1)} %get-tuple-element.12), channel_id=2, replica_groups=mesh['pair'=64,'half'=2,'space'=4] {'space'}, dimensions={0}, use_global_device_ids=true | all-gather | bytes 460800 | tf_op jit(solution)/shard_map/all_gather | solution.py:271
  17.1 0.0 copy-start
  17.1 0.8 shard_map.88.b_ref
  17.9 13.5 %collective-permute-start.1 = (bf16[144,640]{1,0:T(8,128)(2,1)S(1)}, bf16[144,640]{1,0:T(8,128)(2,1)S(1)}, u32[]{:S(2)}, u32[]{:S(2)}) collective-permute-start(bf16[144,640]{1,0:T(8,128)(2,1)S(1)} %shard_map.88.b_ref), channel_id=1, source_target_pairs={{8,16},{16,8},{24,32},{32,24},{40,48},{48,40},{56,64},{64,56},{72,... | collective-permute-start | bytes 552968 | tf_op jit(solution)/shard_map/ppermute | solution.py:248
  31.5 1.9 %collective-permute-start = (bf16[144,640]{1,0:T(8,128)(2,1)S(1)}, bf16[144,640]{1,0:T(8,128)(2,1)S(1)}, u32[]{:S(2)}, u32[]{:S(2)}) collective-permute-start(bf16[144,640]{1,0:T(8,128)(2,1)S(1)} %shard_map.88.b_ref), channel_id=1, source_target_pairs={{0,8},{8,0},{16,24},{24,16},{32,40},{40,32},{48,56},{56,48},{64,72... | collective-permute-start | bytes 552968 | tf_op jit(solution)/shard_map/ppermute | solution.py:248
  33.4 6.7 %all-gather.1 = bf16[288,640]{1,0:T(8,128)(2,1)S(1)} all-gather(bf16[72,640]{1,0:T(8,128)(2,1)} %copy-done.7), channel_id=3, replica_groups=mesh['pair'=64,'half'=2,'space'=4] {'space'}, dimensions={0}, use_global_device_ids=true | all-gather | bytes 460800 | tf_op jit(solution)/shard_map/all_gather | solution.py:274
  40.1 0.8 %shard_map.87.a_ref = bf16[144,640]{1,0:T(8,128)(2,1)S(1)} custom-call(bf16[4,72,640]{2,1,0:T(8,128)(2,1)S(1)} %bitcast.13, bf16[4,72,640]{2,1,0:T(8,128)(2,1)S(1)} %bitcast.21, bf16[320,1280]{1,0:T(8,128)(2,1)S(1)} %bitcast.14, bf16[320,1280]{1,0:T(8,128)(2,1)S(1)} %copy-done.1), custom_call_target="tpu_custom_call" | custom-call | tf_op jit(solution)/shard_map/pallas_call | solution.py:275
  40.9 3.4 %collective-permute-done.even_ref = bf16[144,640]{1,0:T(8,128)(2,1)S(1)} collective-permute-done((bf16[144,640]{1,0:T(8,128)(2,1)S(1)}, bf16[144,640]{1,0:T(8,128)(2,1)S(1)}, u32[]{:S(2)}, u32[]{:S(2)}) %collective-permute-start) | collective-permute-done | bytes 184352 | tf_op jit(solution)/shard_map/ppermute | solution.py:248
  44.3 1.6 %shard_map.89 = (bf16[144,640]{1,0:T(8,128)(2,1)S(1)}, bf16[144,640]{1,0:T(8,128)(2,1)S(1)}, f32[144,640]{1,0:T(8,128)S(1)}, bf16[5,144,256]{2,1,0:T(8,128)(2,1)S(1)}) custom-call(s32[1]{0:T(128)} %bitcast.3.pair_ref, bf16[144,640]{1,0:T(8,128)(2,1)S(1)} %shard_map.87.a_ref, bf16[144,640]{1,0:T(8,128)(2,1)S(1)} %shard_map.88.b_ref, ...), custom_call_target="tpu_custom_call" | custom-call | tf_op jit(solution)/shard_map/pallas_call | solution.py:276
  45.9 4.4 %collective-permute-start.2 = (bf16[144,640]{1,0:T(8,128)(2,1)S(1)}, bf16[144,640]{1,0:T(8,128)(2,1)S(1)}, u32[]{:S(2)}, u32[]{:S(2)}) collective-permute-start(bf16[144,640]{1,0:T(8,128)(2,1)S(1)} %get-tuple-element.18), channel_id=1, source_target_pairs={{8,16},{16,8},{24,32},{32,24},{40,48},{48,40},{56,64},{64,56},{72,... | collective-permute-start | bytes 552968 | tf_op jit(solution)/shard_map/ppermute | solution.py:248
  50.3 1.9 %collective-permute-start.3 = (bf16[144,640]{1,0:T(8,128)(2,1)S(1)}, bf16[144,640]{1,0:T(8,128)(2,1)S(1)}, u32[]{:S(2)}, u32[]{:S(2)}) collective-permute-start(bf16[144,640]{1,0:T(8,128)(2,1)S(1)} %get-tuple-element.19), channel_id=1, source_target_pairs={{0,8},{8,0},{16,24},{24,16},{32,40},{40,32},{48,56},{56,48},{64,72... | collective-permute-start | bytes 552968 | tf_op jit(solution)/shard_map/ppermute | solution.py:248
  52.2 1.2 %shard_map.90 = (bf16[144,1280]{1,0:T(8,128)(2,1)S(1)}, f32[144,1280]{1,0:T(8,128)S(1)}) custom-call(s32[1]{0:T(128)} %bitcast.3.pair_ref, bf16[5,144,256]{2,1,0:T(8,128)(2,1)S(1)} %get-tuple-element.14.small_ref, bf16[144,640]{1,0:T(8,128)(2,1)S(1)} %shard_map.88.b_ref, bf16[144,640]{1,0:T(8,128)(2,1)S(1)} %collective-permute-done.even_ref, ...), custom_call_target="tpu_custom_call" | custom-call | tf_op jit(solution)/shard_map/pallas_call | solution.py:283
  53.4 3.5 %all-gather.2 = bf16[288,1280]{1,0:T(8,128)(2,1)S(1)} all-gather(bf16[144,1280]{1,0:T(8,128)(2,1)S(1)} %get-tuple-element.15), channel_id=4, replica_groups={{0,1},{2,3},{4,5},{6,7},{8,9},{10,11},{12,13},{14,15},{16,17},{18,19},{..., dimensions={0}, use_global_device_ids=true | all-gather | bytes 1105920 | tf_op jit(solution)/shard_map/all_gather | solution.py:290
  56.9 0.2 shard_map.91.out_ref
  57.1 5.0 %collective-permute-done.2.odd_ref = bf16[144,640]{1,0:T(8,128)(2,1)S(1)} collective-permute-done((bf16[144,640]{1,0:T(8,128)(2,1)S(1)}, bf16[144,640]{1,0:T(8,128)(2,1)S(1)}, u32[]{:S(2)}, u32[]{:S(2)}) %collective-permute-start.2) | collective-permute-done | bytes 184352 | tf_op jit(solution)/shard_map/ppermute | solution.py:248
  62.2 0.6 shard_map.92
  62.8 0.0 copy-start.5
  62.8 15.8 %all_to_all.11.parts_ref = bf16[8,54,640]{2,1,0:T(8,128)(2,1)S(1)} all-to-all(bf16[8,54,640]{2,1,0:T(8,128)(2,1)S(1)} %shard_map.92), channel_id=1, replica_groups=mesh['pair'=64,'half'=2,'space'=4] {'half','space'}, dimensions={0} | all-to-all | bytes 1105920 | tf_op jit(solution)/shard_map/all_to_all | solution.py:299
  78.6 1.0 %shard_map.93 = (bf16[36,1280]{1,0:T(8,128)(2,1)}, bf16[36,1280]{1,0:T(8,128)(2,1)}) custom-call(bf16[36,1280]{1,0:T(8,128)(2,1)S(1)} %bitcast.22, bf16[36,1280]{1,0:T(8,128)(2,1)S(1)} %bitcast.23, bf16[1280]{0:T(1024)(128)(2,1)S(1)} %copy-done.8, bf16[8,54,640]{2,1,0:T(8,128)(2,1)S(1)} %all_to_all.11.parts_ref), custom_call_target="tpu_custom_call" | custom-call | tf_op jit(solution)/shard_map/pallas_call | solution.py:300
  (18 shorter events, 0.1 us)
Async XLA Ops:
  0.6 1.0 %copy-start.6 = (bf16[1,1,36,1280]{3,2,1,0:T(8,128)(2,1)S(1)}, bf16[1,1,36,1280]{3,2,1,0:T(8,128)(2,1)}, u32[]{:S(2)}) copy-start(bf16[1,1,36,1280]{3,2,1,0:T(8,128)(2,1)} %param.8) | copy-start | bytes 276484
  1.7 6.9 %copy-start.8 = (bf16[1280]{0:T(1024)(128)(2,1)S(1)}, bf16[1280]{0:T(1024)(128)(2,1)}, u32[]{:S(2)}) copy-start(bf16[1280]{0:T(1024)(128)(2,1)} %gain_ref.3) | copy-start | bytes 7684
  8.6 8.5 %copy-start.2 = (bf16[1280,320]{0,1:T(8,128)(2,1)S(1)}, bf16[1280,320]{0,1:T(8,128)(2,1)}, u32[]{:S(2)}) copy-start(bf16[1280,320]{0,1:T(8,128)(2,1)} %param.11) | copy-start | bytes 2457604
  8.6 8.5 %copy-start.3 = (bf16[1280,320]{0,1:T(8,128)(2,1)S(1)}, bf16[1280,320]{0,1:T(8,128)(2,1)}, u32[]{:S(2)}) copy-start(bf16[1280,320]{0,1:T(8,128)(2,1)} %param.12) | copy-start | bytes 2457604
  8.8 8.3 %copy-start.7 = (bf16[72,640]{1,0:T(8,128)(2,1)}, bf16[72,640]{1,0:T(8,128)(2,1)S(1)}, u32[]{:S(2)}) copy-start(bf16[72,640]{1,0:T(8,128)(2,1)S(1)} %get-tuple-element.13) | copy-start | bytes 276484
  17.1 22.9 %copy-start = (bf16[1280,320]{0,1:T(8,128)(2,1)S(1)}, bf16[1280,320]{0,1:T(8,128)(2,1)}, u32[]{:S(2)}) copy-start(bf16[1280,320]{0,1:T(8,128)(2,1)} %param.10) | copy-start | bytes 2457604
  17.1 22.9 %copy-start.1 = (bf16[320,1280]{1,0:T(8,128)(2,1)S(1)}, bf16[320,1280]{1,0:T(8,128)(2,1)}, u32[]{:S(2)}) copy-start(bf16[320,1280]{1,0:T(8,128)(2,1)} %wo_ref.3) | copy-start | bytes 2457604
  17.9 23.0 %collective-permute-start.1 = (bf16[144,640]{1,0:T(8,128)(2,1)S(1)}, bf16[144,640]{1,0:T(8,128)(2,1)S(1)}, u32[]{:S(2)}, u32[]{:S(2)}) collective-permute-start(bf16[144,640]{1,0:T(8,128)(2,1)S(1)} %shard_map.88.b_ref), channel_id=1, source_target_pairs={{8,16},{16,8},{24,32},{32,24},{40,48},{48,40},{56,64},{64,56},{72,... | collective-permute-start | bytes 552968 | tf_op jit(solution)/shard_map/ppermute | solution.py:248
  31.5 12.8 %collective-permute-start = (bf16[144,640]{1,0:T(8,128)(2,1)S(1)}, bf16[144,640]{1,0:T(8,128)(2,1)S(1)}, u32[]{:S(2)}, u32[]{:S(2)}) collective-permute-start(bf16[144,640]{1,0:T(8,128)(2,1)S(1)} %shard_map.88.b_ref), channel_id=1, source_target_pairs={{0,8},{8,0},{16,24},{24,16},{32,40},{40,32},{48,56},{56,48},{64,72... | collective-permute-start | bytes 552968 | tf_op jit(solution)/shard_map/ppermute | solution.py:248
  45.9 16.3 %collective-permute-start.2 = (bf16[144,640]{1,0:T(8,128)(2,1)S(1)}, bf16[144,640]{1,0:T(8,128)(2,1)S(1)}, u32[]{:S(2)}, u32[]{:S(2)}) collective-permute-start(bf16[144,640]{1,0:T(8,128)(2,1)S(1)} %get-tuple-element.18), channel_id=1, source_target_pairs={{8,16},{16,8},{24,32},{32,24},{40,48},{48,40},{56,64},{64,56},{72,... | collective-permute-start | bytes 552968 | tf_op jit(solution)/shard_map/ppermute | solution.py:248
  50.3 11.9 %collective-permute-start.3 = (bf16[144,640]{1,0:T(8,128)(2,1)S(1)}, bf16[144,640]{1,0:T(8,128)(2,1)S(1)}, u32[]{:S(2)}, u32[]{:S(2)}) collective-permute-start(bf16[144,640]{1,0:T(8,128)(2,1)S(1)} %get-tuple-element.19), channel_id=1, source_target_pairs={{0,8},{8,0},{16,24},{24,16},{32,40},{40,32},{48,56},{56,48},{64,72... | collective-permute-start | bytes 552968 | tf_op jit(solution)/shard_map/ppermute | solution.py:248
  56.9 5.2 %copy-start.4 = (bf16[1280,320]{0,1:T(8,128)(2,1)S(1)}, bf16[1280,320]{0,1:T(8,128)(2,1)}, u32[]{:S(2)}) copy-start(bf16[1280,320]{0,1:T(8,128)(2,1)} %param.12) | copy-start | bytes 2457604
  62.8 15.8 %copy-start.5 = (bf16[1,1,36,1280]{3,2,1,0:T(8,128)(2,1)S(1)}, bf16[1,1,36,1280]{3,2,1,0:T(8,128)(2,1)}, u32[]{:S(2)}) copy-start(bf16[1,1,36,1280]{3,2,1,0:T(8,128)(2,1)} %param.7) | copy-start | bytes 276484

commit v7 on v6

--- a/solution.py
+++ b/solution.py
@@ -66,10 +66,11 @@
 def gathered(g_ref, rows_ref):
     whole, width = g_ref.shape[1] // PAIR, g_ref.shape[2]
     half = whole // 2
-    for frame in range(PAIR):
-        for s in range(SHARDS):
+    for s in range(SHARDS):
+        blocks = g_ref[s].astype(F32)
+        for frame in range(PAIR):
             start = (frame * SHARDS + s) * half
-            block = g_ref[s, frame * whole : (frame + 1) * whole].astype(F32)
+            block = blocks[frame * whole : (frame + 1) * whole]
             rows_ref[start : start + half, :width] = block[:half]
             rows_ref[start : start + half, width:] = block[half:]
     return rows_ref[...].astype(BF16)
@@ -211,9 +212,9 @@
     out, hidden_grads = [], []
     for h in range(PAIR):
         parts = [parts_ref[h * SHARDS + s].astype(F32) for s in range(SHARDS)]
-        hidden_grads.append(unpacked(sum(part[:rows] for part in parts)))
-        for core in range(2):
-            out.append(unpacked(sum(part[rows:] for part in parts[core::2])))
+        first, second = parts[0] + parts[2], parts[1] + parts[3]
+        hidden_grads.append(unpacked(first[:rows] + second[:rows]))
+        out += [unpacked(first[rows:]), unpacked(second[rows:])]
     out = jnp.concatenate(out, axis=0)
     hidden_grads = jnp.concatenate(hidden_grads, axis=0)
     x = x_ref[...].astype(F32)

time: 80 us -> 80 us (level)
  no operation moved by 1% of the time
where the time goes in v7:
time: 80 us; the launch traced here: 79.6 us
  blocking collectives  41 us (51%)
  starting transfers between devices  21.8 us (27%)
  waiting for transfers between devices  8.41 us (11%)
  Pallas kernels  6.47 us (8%)
  local copies, waits for them, and re-layouts  1.03 us (1%)
  between operations  0.81 us (1%)
    ppermute x4, starting transfers between devices, exchanged(): return lax.ppermute(block, 'pair', route)  21.8 us
    all_to_all x1, blocking collectives, per_device(): parts = lax.all_to_all(parts, ('half', 'space'), 0, 0)  15.8 us
    ppermute x4, waiting for transfers between devices, exchanged(): return lax.ppermute(block, 'pair', route)  8.41 us
    all_gather x1, blocking collectives, per_device(): hidden = lax.all_gather(hidden, 'space', axis=0)  8.26 us
    all_to_all x1, blocking collectives, per_device(): halves = lax.all_to_all(halves, 'half', 0, 0)  6.88 us
    all_gather x1, blocking collectives, per_device(): cot_rows = lax.all_gather(cot_rows, 'space', axis=0)  6.66 us
    all_gather x1, blocking collectives, per_device(): out = lax.all_gather(out, 'space', axis=0, axis_index_groups=cores)  3.49 us
  transfers between devices with their start and end apart: 4, of which 2 were waited for; matrix products, arithmetic and copies ran while one was open for 0% of the time, Pallas kernels for 3%

profile of v7, /device:TPU:57, one launch (start us, length us, event | category | flops | bytes accessed | tf_op | source)
XLA Modules:
  0.0 79.6 jit_solution(13325070710201196449)
XLA Ops:
  0.6 1.0 %reshape_reshape.6 = bf16[2,18,1280]{2,1,0:T(8,128)(2,1)S(1)} reshape(bf16[1,1,36,1280]{3,2,1,0:T(8,128)(2,1)} %param.7) | data formatting | bytes 184320 | tf_op jit(solution)/shard_map/reshape;reshape | solution.py:267
  1.7 0.0 copy-start.8
  1.7 6.9 %all_to_all.10.halves_ref = bf16[2,36,1280]{2,1,0:T(8,128)(2,1)S(1)} all-to-all(bf16[2,36,1280]{2,1,0:T(8,128)(2,1)S(1)} %pad_maximum_fusion), channel_id=1, replica_groups=mesh['pair'=64,'half'=2,'space'=4] {'half'}, dimensions={0} | all-to-all | bytes 368640 | tf_op jit(solution)/shard_map/all_to_all | solution.py:269
  8.6 0.2 shard_map.86
  8.8 8.3 %all-gather = bf16[288,640]{1,0:T(8,128)(2,1)S(1)} all-gather(bf16[72,640]{1,0:T(8,128)(2,1)S(1)} %get-tuple-element.12), channel_id=2, replica_groups=mesh['pair'=64,'half'=2,'space'=4] {'space'}, dimensions={0}, use_global_device_ids=true | all-gather | bytes 460800 | tf_op jit(solution)/shard_map/all_gather | solution.py:272
  17.1 0.0 copy-start
  17.1 0.0 copy-start.1
  17.1 0.8 shard_map.88.b_ref
  17.9 13.5 %collective-permute-start.1 = (bf16[144,640]{1,0:T(8,128)(2,1)S(1)}, bf16[144,640]{1,0:T(8,128)(2,1)S(1)}, u32[]{:S(2)}, u32[]{:S(2)}) collective-permute-start(bf16[144,640]{1,0:T(8,128)(2,1)S(1)} %shard_map.88.b_ref), channel_id=1, source_target_pairs={{8,16},{16,8},{24,32},{32,24},{40,48},{48,40},{56,64},{64,56},{72,... | collective-permute-start | bytes 552968 | tf_op jit(solution)/shard_map/ppermute | solution.py:249
  31.4 1.9 %collective-permute-start = (bf16[144,640]{1,0:T(8,128)(2,1)S(1)}, bf16[144,640]{1,0:T(8,128)(2,1)S(1)}, u32[]{:S(2)}, u32[]{:S(2)}) collective-permute-start(bf16[144,640]{1,0:T(8,128)(2,1)S(1)} %shard_map.88.b_ref), channel_id=1, source_target_pairs={{0,8},{8,0},{16,24},{24,16},{32,40},{40,32},{48,56},{56,48},{64,72... | collective-permute-start | bytes 552968 | tf_op jit(solution)/shard_map/ppermute | solution.py:249
  33.4 6.7 %all-gather.1 = bf16[288,640]{1,0:T(8,128)(2,1)S(1)} all-gather(bf16[72,640]{1,0:T(8,128)(2,1)} %copy-done.7), channel_id=3, replica_groups=mesh['pair'=64,'half'=2,'space'=4] {'space'}, dimensions={0}, use_global_device_ids=true | all-gather | bytes 460800 | tf_op jit(solution)/shard_map/all_gather | solution.py:275
  40.0 0.8 %shard_map.87.a_ref = bf16[144,640]{1,0:T(8,128)(2,1)S(1)} custom-call(bf16[4,72,640]{2,1,0:T(8,128)(2,1)S(1)} %bitcast.13, bf16[4,72,640]{2,1,0:T(8,128)(2,1)S(1)} %bitcast.21, bf16[320,1280]{1,0:T(8,128)(2,1)S(1)} %bitcast.14, bf16[320,1280]{1,0:T(8,128)(2,1)S(1)} %copy-done.1), custom_call_target="tpu_custom_call" | custom-call | tf_op jit(solution)/shard_map/pallas_call | solution.py:276
  40.9 3.4 %collective-permute-done.even_ref = bf16[144,640]{1,0:T(8,128)(2,1)S(1)} collective-permute-done((bf16[144,640]{1,0:T(8,128)(2,1)S(1)}, bf16[144,640]{1,0:T(8,128)(2,1)S(1)}, u32[]{:S(2)}, u32[]{:S(2)}) %collective-permute-start) | collective-permute-done | bytes 184352 | tf_op jit(solution)/shard_map/ppermute | solution.py:249
  44.3 1.6 %shard_map.89 = (bf16[144,640]{1,0:T(8,128)(2,1)S(1)}, bf16[144,640]{1,0:T(8,128)(2,1)S(1)}, f32[144,640]{1,0:T(8,128)S(1)}, bf16[5,144,256]{2,1,0:T(8,128)(2,1)S(1)}) custom-call(s32[1]{0:T(128)} %bitcast.3.pair_ref, bf16[144,640]{1,0:T(8,128)(2,1)S(1)} %shard_map.87.a_ref, bf16[144,640]{1,0:T(8,128)(2,1)S(1)} %shard_map.88.b_ref, ...), custom_call_target="tpu_custom_call" | custom-call | tf_op jit(solution)/shard_map/pallas_call | solution.py:277
  45.8 4.4 %collective-permute-start.2 = (bf16[144,640]{1,0:T(8,128)(2,1)S(1)}, bf16[144,640]{1,0:T(8,128)(2,1)S(1)}, u32[]{:S(2)}, u32[]{:S(2)}) collective-permute-start(bf16[144,640]{1,0:T(8,128)(2,1)S(1)} %get-tuple-element.18), channel_id=1, source_target_pairs={{8,16},{16,8},{24,32},{32,24},{40,48},{48,40},{56,64},{64,56},{72,... | collective-permute-start | bytes 552968 | tf_op jit(solution)/shard_map/ppermute | solution.py:249
  50.3 1.9 %collective-permute-start.3 = (bf16[144,640]{1,0:T(8,128)(2,1)S(1)}, bf16[144,640]{1,0:T(8,128)(2,1)S(1)}, u32[]{:S(2)}, u32[]{:S(2)}) collective-permute-start(bf16[144,640]{1,0:T(8,128)(2,1)S(1)} %get-tuple-element.19), channel_id=1, source_target_pairs={{0,8},{8,0},{16,24},{24,16},{32,40},{40,32},{48,56},{56,48},{64,72... | collective-permute-start | bytes 552968 | tf_op jit(solution)/shard_map/ppermute | solution.py:249
  52.2 1.2 %shard_map.90 = (bf16[144,1280]{1,0:T(8,128)(2,1)S(1)}, f32[144,1280]{1,0:T(8,128)S(1)}) custom-call(s32[1]{0:T(128)} %bitcast.3.pair_ref, bf16[5,144,256]{2,1,0:T(8,128)(2,1)S(1)} %get-tuple-element.14.small_ref, bf16[144,640]{1,0:T(8,128)(2,1)S(1)} %shard_map.88.b_ref, bf16[144,640]{1,0:T(8,128)(2,1)S(1)} %collective-permute-done.even_ref, ...), custom_call_target="tpu_custom_call" | custom-call | tf_op jit(solution)/shard_map/pallas_call | solution.py:284
  53.4 3.5 %all-gather.2 = bf16[288,1280]{1,0:T(8,128)(2,1)S(1)} all-gather(bf16[144,1280]{1,0:T(8,128)(2,1)S(1)} %get-tuple-element.15), channel_id=4, replica_groups={{0,1},{2,3},{4,5},{6,7},{8,9},{10,11},{12,13},{14,15},{16,17},{18,19},{..., dimensions={0}, use_global_device_ids=true | all-gather | bytes 1105920 | tf_op jit(solution)/shard_map/all_gather | solution.py:291
  56.9 0.2 shard_map.91.out_ref
  57.1 5.0 %collective-permute-done.2.odd_ref = bf16[144,640]{1,0:T(8,128)(2,1)S(1)} collective-permute-done((bf16[144,640]{1,0:T(8,128)(2,1)S(1)}, bf16[144,640]{1,0:T(8,128)(2,1)S(1)}, u32[]{:S(2)}, u32[]{:S(2)}) %collective-permute-start.2) | collective-permute-done | bytes 184352 | tf_op jit(solution)/shard_map/ppermute | solution.py:249
  62.2 0.6 shard_map.92
  62.8 0.0 copy-start.5
  62.8 15.8 %all_to_all.11.parts_ref = bf16[8,54,640]{2,1,0:T(8,128)(2,1)S(1)} all-to-all(bf16[8,54,640]{2,1,0:T(8,128)(2,1)S(1)} %shard_map.92), channel_id=1, replica_groups=mesh['pair'=64,'half'=2,'space'=4] {'half','space'}, dimensions={0} | all-to-all | bytes 1105920 | tf_op jit(solution)/shard_map/all_to_all | solution.py:300
  78.6 1.0 %shard_map.93 = (bf16[36,1280]{1,0:T(8,128)(2,1)}, bf16[36,1280]{1,0:T(8,128)(2,1)}) custom-call(bf16[36,1280]{1,0:T(8,128)(2,1)S(1)} %bitcast.22, bf16[36,1280]{1,0:T(8,128)(2,1)S(1)} %bitcast.23, bf16[1280]{0:T(1024)(128)(2,1)S(1)} %copy-done.8, bf16[8,54,640]{2,1,0:T(8,128)(2,1)S(1)} %all_to_all.11.parts_ref), custom_call_target="tpu_custom_call" | custom-call | tf_op jit(solution)/shard_map/pallas_call | solution.py:301
  (18 shorter events, 0.1 us)
Async XLA Ops:
  0.6 1.0 %copy-start.6 = (bf16[1,1,36,1280]{3,2,1,0:T(8,128)(2,1)S(1)}, bf16[1,1,36,1280]{3,2,1,0:T(8,128)(2,1)}, u32[]{:S(2)}) copy-start(bf16[1,1,36,1280]{3,2,1,0:T(8,128)(2,1)} %param.8) | copy-start | bytes 276484
  1.7 6.9 %copy-start.8 = (bf16[1280]{0:T(1024)(128)(2,1)S(1)}, bf16[1280]{0:T(1024)(128)(2,1)}, u32[]{:S(2)}) copy-start(bf16[1280]{0:T(1024)(128)(2,1)} %gain_ref.3) | copy-start | bytes 7684
  8.6 8.5 %copy-start.2 = (bf16[1280,320]{0,1:T(8,128)(2,1)S(1)}, bf16[1280,320]{0,1:T(8,128)(2,1)}, u32[]{:S(2)}) copy-start(bf16[1280,320]{0,1:T(8,128)(2,1)} %param.11) | copy-start | bytes 2457604
  8.6 8.5 %copy-start.3 = (bf16[1280,320]{0,1:T(8,128)(2,1)S(1)}, bf16[1280,320]{0,1:T(8,128)(2,1)}, u32[]{:S(2)}) copy-start(bf16[1280,320]{0,1:T(8,128)(2,1)} %param.12) | copy-start | bytes 2457604
  8.8 8.3 %copy-start.7 = (bf16[72,640]{1,0:T(8,128)(2,1)}, bf16[72,640]{1,0:T(8,128)(2,1)S(1)}, u32[]{:S(2)}) copy-start(bf16[72,640]{1,0:T(8,128)(2,1)S(1)} %get-tuple-element.13) | copy-start | bytes 276484
  17.1 22.9 %copy-start = (bf16[1280,320]{0,1:T(8,128)(2,1)S(1)}, bf16[1280,320]{0,1:T(8,128)(2,1)}, u32[]{:S(2)}) copy-start(bf16[1280,320]{0,1:T(8,128)(2,1)} %param.10) | copy-start | bytes 2457604
  17.1 22.9 %copy-start.1 = (bf16[320,1280]{1,0:T(8,128)(2,1)S(1)}, bf16[320,1280]{1,0:T(8,128)(2,1)}, u32[]{:S(2)}) copy-start(bf16[320,1280]{1,0:T(8,128)(2,1)} %wo_ref.3) | copy-start | bytes 2457604
  17.9 23.0 %collective-permute-start.1 = (bf16[144,640]{1,0:T(8,128)(2,1)S(1)}, bf16[144,640]{1,0:T(8,128)(2,1)S(1)}, u32[]{:S(2)}, u32[]{:S(2)}) collective-permute-start(bf16[144,640]{1,0:T(8,128)(2,1)S(1)} %shard_map.88.b_ref), channel_id=1, source_target_pairs={{8,16},{16,8},{24,32},{32,24},{40,48},{48,40},{56,64},{64,56},{72,... | collective-permute-start | bytes 552968 | tf_op jit(solution)/shard_map/ppermute | solution.py:249
  31.4 12.8 %collective-permute-start = (bf16[144,640]{1,0:T(8,128)(2,1)S(1)}, bf16[144,640]{1,0:T(8,128)(2,1)S(1)}, u32[]{:S(2)}, u32[]{:S(2)}) collective-permute-start(bf16[144,640]{1,0:T(8,128)(2,1)S(1)} %shard_map.88.b_ref), channel_id=1, source_target_pairs={{0,8},{8,0},{16,24},{24,16},{32,40},{40,32},{48,56},{56,48},{64,72... | collective-permute-start | bytes 552968 | tf_op jit(solution)/shard_map/ppermute | solution.py:249
  45.8 16.3 %collective-permute-start.2 = (bf16[144,640]{1,0:T(8,128)(2,1)S(1)}, bf16[144,640]{1,0:T(8,128)(2,1)S(1)}, u32[]{:S(2)}, u32[]{:S(2)}) collective-permute-start(bf16[144,640]{1,0:T(8,128)(2,1)S(1)} %get-tuple-element.18), channel_id=1, source_target_pairs={{8,16},{16,8},{24,32},{32,24},{40,48},{48,40},{56,64},{64,56},{72,... | collective-permute-start | bytes 552968 | tf_op jit(solution)/shard_map/ppermute | solution.py:249
  50.3 11.9 %collective-permute-start.3 = (bf16[144,640]{1,0:T(8,128)(2,1)S(1)}, bf16[144,640]{1,0:T(8,128)(2,1)S(1)}, u32[]{:S(2)}, u32[]{:S(2)}) collective-permute-start(bf16[144,640]{1,0:T(8,128)(2,1)S(1)} %get-tuple-element.19), channel_id=1, source_target_pairs={{0,8},{8,0},{16,24},{24,16},{32,40},{40,32},{48,56},{56,48},{64,72... | collective-permute-start | bytes 552968 | tf_op jit(solution)/shard_map/ppermute | solution.py:249
  56.9 5.3 %copy-start.4 = (bf16[1280,320]{0,1:T(8,128)(2,1)S(1)}, bf16[1280,320]{0,1:T(8,128)(2,1)}, u32[]{:S(2)}) copy-start(bf16[1280,320]{0,1:T(8,128)(2,1)} %param.12) | copy-start | bytes 2457604
  62.8 15.8 %copy-start.5 = (bf16[1,1,36,1280]{3,2,1,0:T(8,128)(2,1)S(1)}, bf16[1,1,36,1280]{3,2,1,0:T(8,128)(2,1)}, u32[]{:S(2)}) copy-start(bf16[1,1,36,1280]{3,2,1,0:T(8,128)(2,1)} %param.7) | copy-start | bytes 276484
